TPU v7x, 256 devices: a whole 4x4x8 slice. The times are simulated.
256 devices in a mesh: space: 16 (over x, y), tm: 16 (over z, core).
Axes of the slice: x: 4, y: 4, z: 8, core: 2. Of those that a mesh axis runs over, the one named last changes fastest.
Arguments:
- start: float32 [1024, 65536], P('tm', 'space'), may hold values from -3 to 3
- right_side: float32 [1024, 65536], P('tm', 'space'), may hold values from -12 to 12
- noise: float32 [65536], P('space'), may hold values from 0.5 to 2
- tile_ids: int32 [512, 4], P('space'), may hold values from 0 to 511, as said below
- space_tiles: float32 [512, 4, 128, 128], P('space'), may hold values from -1 to 2
- time_kernel: float32 [1024, 1024], P('tm'), may hold values from -1 to 2
Outputs:
- next_iterate: float32 [1024, 65536], P('tm', 'space')
- next_residual: float32 [1024, 65536], P('tm', 'space')
Inputs may be any that keep to these rules, and one draw needn't show every extreme that they name: tile_ids[t, 0] = t; the other 3 entries of row t are distinct tiles other than t within the (5) consecutive tiles from max(0, min(t - 2, 507)); tiles are in space-filling-curve order.
All inputs are finite; a program needn't handle non-finite values.
Results may differ from a plain program's by a relative error of at most 0.0003.
Values sent between devices are 32-bit elements; how exact they have to be, the bound alone decides.
No kernel may reach another device: no remote copies, remote signals or barrier semaphores. Data moves between devices by JAX's collectives and lax.ppermute only.
A program may use at most 64 MiB of HBM per device.

v0:
```python
import jax
import jax.numpy as jnp
from jax import lax
from jax.sharding import PartitionSpec as P

REACH = 2


def padded(block, sides, width):
    for axis, dim in sides:
        count = lax.axis_size(axis)
        forward = [(i, i + 1) for i in range(count - 1)]
        backward = [(target, source) for source, target in forward]
        low = lax.ppermute(
            lax.slice_in_dim(block, block.shape[dim] - width, None, axis=dim), axis, forward
        )
        high = lax.ppermute(lax.slice_in_dim(block, 0, width, axis=dim), axis, backward)
        block = jnp.concatenate([low, block, high], axis=dim)
    return block


def local(start, right_side, noise, tile_ids, space_tiles, time_kernel):
    full_kernel = lax.all_gather(time_kernel, "tm", axis=0, tiled=True)
    tiles_dev = tile_ids.shape[0]
    tile_size = space_tiles.shape[2]
    hours_dev, sites_dev = start.shape
    groups = lax.axis_size("tm")
    width = sites_dev // groups
    first_tile = lax.axis_index("space") * tiles_dev - REACH
    local_ids = tile_ids - first_tile

    def spatial(field):
        widened = padded(field, (("space", 1),), REACH * tile_size)
        blocks = widened.reshape(widened.shape[0], tiles_dev + 2 * REACH, tile_size)
        gathered = jnp.take(blocks, local_ids, axis=1)
        product = jnp.einsum(
            "htnc,tnrc->htr", gathered, space_tiles, precision=lax.Precision.HIGHEST
        )
        return product.reshape(widened.shape[0], sites_dev)

    def kernel_items(piece):
        return jnp.einsum("gh,hok->gok", full_kernel, piece, precision=lax.Precision.HIGHEST)

    def temporal(field):
        grouped = field.reshape(hours_dev, groups, width)
        mixed_sites = kernel_items(
            lax.all_to_all(grouped, "tm", split_axis=1, concat_axis=0, tiled=True)
        )
        mixed_sites = mixed_sites.reshape(mixed_sites.shape[0], width)
        return lax.all_to_all(mixed_sites, "tm", split_axis=0, concat_axis=1, tiled=True)

    residual = right_side - temporal(spatial(start)) - noise[None, :] * start
    image = temporal(spatial(residual)) + noise[None, :] * residual
    norm_sum = lax.psum(jnp.sum(residual * residual), ("space", "tm"))
    curve_sum = lax.psum(jnp.sum(residual * image), ("space", "tm"))
    alpha = norm_sum / curve_sum
    return (start + alpha * residual, residual - alpha * image)


def solution(mesh):
    placed = (
        P("tm", "space"),
        P("tm", "space"),
        P("space"),
        P("space", None),
        P("space", None, None, None),
        P("tm", None),
    )
    return jax.shard_map(
        local,
        mesh=mesh,
        in_specs=placed,
        out_specs=(P("tm", "space"), P("tm", "space")),
        check_vma=False,
    )
```

profile of v0, /device:TPU:38, one launch (start us, length us, event | category | flops | bytes accessed | tf_op | source)
XLA Modules:
  0.0 303.8 jit_solution(16818436945088158878)
XLA Ops:
  7.2 0.0 all-gather.2.cloned.1.call-start
  7.2 0.7 all-gather.2.cloned.1.call-update
  7.9 0.9 fusion.19
  8.8 3.5 %collective-permute-start = (f32[64,256]{1,0:T(8,128)S(1)}, f32[64,256]{1,0:T(8,128)S(1)}, u32[]{:S(2)}, u32[]{:S(2)}) collective-permute-start(f32[64,256]{1,0:T(8,128)S(1)} %get-tuple-element.13), channel_id=1, source_target_pairs={{0,16},{16,32},{32,48},{48,64},{64,80},{80,96},{96,112},{112,128},... | collective-permute-start | bytes 196616 | tf_op jit(solution)/shard_map/ppermute | solution.py:14
  12.3 4.5 %collective-permute-start.1 = (f32[64,256]{1,0:T(8,128)S(1)}, f32[64,256]{1,0:T(8,128)S(1)}, u32[]{:S(2)}, u32[]{:S(2)}) collective-permute-start(f32[64,256]{1,0:T(8,128)S(1)} %get-tuple-element.14), channel_id=1, source_target_pairs={{16,0},{32,16},{48,32},{64,48},{80,64},{96,80},{112,96},{128,112},... | collective-permute-start | bytes 196616 | tf_op jit(solution)/shard_map/ppermute | solution.py:17
  16.8 0.7 compare_and_fusion
  17.5 0.1 copy.42
  17.6 0.1 copy.43
  17.6 0.1 reshape.60
  17.8 0.0 collective-permute-done
  17.8 0.9 collective-permute-done.1
  18.6 1.4 copy_bitcast_fusion.1
  20.0 2.8 gather_fusion
  22.8 12.2 %fusion.10 = f32[64,32,128]{2,0,1:T(8,128)S(1)} fusion(f32[32,4,128,128]{3,2,1,0:T(8,128)} %param.12, f32[32,4,64,128]{3,2,1,0:T(8,128)} %bitcast.61, pred[32,4]{1,0:T(8,128)(4,1)S(1)} %copy.42), kind=kOutput, calls=%fused_computation.12 | convolution fusion | flops 1611661312 | bytes 13631616 | tf_op jit(solution)/shard_map/htnc,tnrc->htr/dot_general | solution.py:36
  35.0 0.6 copy.45
  35.6 0.3 reshape_reshape.6
  35.9 0.6 copy.46
  36.6 35.8 %all_to_all.68 = f32[64,16,256]{2,0,1:T(8,128)S(1)} all-to-all(f32[64,16,256]{2,0,1:T(8,128)S(1)} %copy.46), channel_id=1, replica_groups=mesh['space'=16,'tm'=16] {'tm'}, dimensions={1} | all-to-all | bytes 2097152 | tf_op jit(solution)/shard_map/all_to_all | solution.py:47
  72.3 8.7 %convolution_bitcast_fusion.1 = f32[1024,256]{0,1:T(8,128)S(1)} fusion(f32[1024,256]{1,0:T(8,128)S(1)} %bitcast.68, f32[1024,1024]{1,0:T(8,128)} %all-gather.2.cloned.1.call-done), kind=kOutput, calls=%fused_computation.15 | convolution fusion | flops 3221225472 | bytes 6291456 | tf_op jit(solution)/shard_map/gh,hok->gok/dot_general | solution.py:42
  81.1 0.0 copy-start.1
  81.1 0.0 copy-start.3
  81.1 0.3 copy.47
  81.4 0.0 copy-start.2
  81.4 31.5 %all_to_all.69 = f32[16,64,256]{2,1,0:T(8,128)S(1)} all-to-all(f32[16,64,256]{2,1,0:T(8,128)S(1)} %bitcast.64), channel_id=1, replica_groups=mesh['space'=16,'tm'=16] {'tm'}, dimensions={0} | all-to-all | bytes 2097152 | tf_op jit(solution)/shard_map/all_to_all | solution.py:50
  112.9 0.1 copy.60
  113.0 0.0 copy-done.1
  113.0 0.0 copy-done.3
  113.0 0.0 copy-done.2
  113.1 0.2 multiply_subtract_fusion.1
  113.3 3.5 %collective-permute-start.2 = (f32[64,256]{1,0:T(8,128)S(1)}, f32[64,256]{1,0:T(8,128)S(1)}, u32[]{:S(2)}, u32[]{:S(2)}) collective-permute-start(f32[64,256]{1,0:T(8,128)S(1)} %get-tuple-element.11), channel_id=1, source_target_pairs={{0,16},{16,32},{32,48},{48,64},{64,80},{80,96},{96,112},{112,128},... | collective-permute-start | bytes 196616 | tf_op jit(solution)/shard_map/ppermute | solution.py:14
  116.8 4.6 %collective-permute-start.3 = (f32[64,256]{1,0:T(8,128)S(1)}, f32[64,256]{1,0:T(8,128)S(1)}, u32[]{:S(2)}, u32[]{:S(2)}) collective-permute-start(f32[64,256]{1,0:T(8,128)S(1)} %get-tuple-element.12), channel_id=1, source_target_pairs={{16,0},{32,16},{48,32},{64,48},{80,64},{96,80},{112,96},{128,112},... | collective-permute-start | bytes 196616 | tf_op jit(solution)/shard_map/ppermute | solution.py:17
  121.5 0.1 collective-permute-done.2
  121.6 1.6 collective-permute-done.3
  123.2 0.1 copy_bitcast_fusion
  123.3 2.8 gather_fusion.1
  126.1 12.0 %fusion.13 = f32[64,32,128]{2,0,1:T(8,128)S(1)} fusion(f32[32,4,128,128]{3,2,1,0:T(8,128)} %param.12, f32[32,4,64,128]{3,2,1,0:T(8,128)} %bitcast.60, pred[32,4]{1,0:T(8,128)(4,1)S(1)} %copy.42), kind=kOutput, calls=%fused_computation.13 | convolution fusion | flops 1611661312 | bytes 13631616 | tf_op jit(solution)/shard_map/htnc,tnrc->htr/dot_general | solution.py:36
  138.2 1.6 copy.52
  139.7 1.5 reshape_reshape.7
  141.3 0.0 copy-start
  141.3 0.6 copy.53
  141.9 31.4 %all_to_all.70 = f32[64,16,256]{2,0,1:T(8,128)S(1)} all-to-all(f32[64,16,256]{2,0,1:T(8,128)S(1)} %copy.53), channel_id=1, replica_groups=mesh['space'=16,'tm'=16] {'tm'}, dimensions={1} | all-to-all | bytes 2097152 | tf_op jit(solution)/shard_map/all_to_all | solution.py:47
  173.3 7.9 %convolution_bitcast_fusion = f32[1024,256]{0,1:T(8,128)} fusion(f32[1024,256]{1,0:T(8,128)S(1)} %bitcast.69, f32[1024,1024]{1,0:T(8,128)S(1)} %copy-done), kind=kOutput, calls=%fused_computation.14 | convolution fusion | flops 3221225472 | bytes 6291456 | tf_op jit(solution)/shard_map/gh,hok->gok/dot_general | solution.py:42
  181.2 1.6 copy.54
  182.7 31.3 %all_to_all.71 = f32[16,64,256]{2,1,0:T(8,128)S(1)} all-to-all(f32[16,64,256]{2,1,0:T(8,128)S(1)} %bitcast.66), channel_id=1, replica_groups=mesh['space'=16,'tm'=16] {'tm'}, dimensions={0} | all-to-all | bytes 2097152 | tf_op jit(solution)/shard_map/all_to_all | solution.py:50
  214.0 0.1 copy.61
  214.1 1.0 multiply_reduce_fusion
  215.1 78.9 %all-reduce = (f32[]{:T(128)}, f32[]{:T(128)}) all-reduce(f32[]{:T(128)} %get-tuple-element.4, f32[]{:T(128)} %get-tuple-element.3), channel_id=1, replica_groups=mesh['space'=16,'tm'=16] {'space','tm'}, use_global_device_ids=true, to_apply=%region_1.3 | all-reduce | flops 2 | bytes 16 | tf_op jit(solution)/shard_map/psum | solution.py:54
  295.3 1.6 multiply_subtract_fusion
  (4 shorter events, 0.0 us)
Async XLA Ops:
  7.2 65.2 %all-gather.2.cloned.1.call-start = ((), (), s32[]{:S(2)}) async-start(), calls=%async_computation.4 | async-start | bytes 4456448 | tf_op jit(solution)/shard_map/all_gather | solution.py:23
  8.8 9.0 %collective-permute-start = (f32[64,256]{1,0:T(8,128)S(1)}, f32[64,256]{1,0:T(8,128)S(1)}, u32[]{:S(2)}, u32[]{:S(2)}) collective-permute-start(f32[64,256]{1,0:T(8,128)S(1)} %get-tuple-element.13), channel_id=1, source_target_pairs={{0,16},{16,32},{32,48},{48,64},{64,80},{80,96},{96,112},{112,128},... | collective-permute-start | bytes 196616 | tf_op jit(solution)/shard_map/ppermute | solution.py:14
  12.3 6.4 %collective-permute-start.1 = (f32[64,256]{1,0:T(8,128)S(1)}, f32[64,256]{1,0:T(8,128)S(1)}, u32[]{:S(2)}, u32[]{:S(2)}) collective-permute-start(f32[64,256]{1,0:T(8,128)S(1)} %get-tuple-element.14), channel_id=1, source_target_pairs={{16,0},{32,16},{48,32},{64,48},{80,64},{96,80},{112,96},{128,112},... | collective-permute-start | bytes 196616 | tf_op jit(solution)/shard_map/ppermute | solution.py:17
  81.1 32.0 %copy-start.1 = (f32[64,4096]{1,0:T(8,128)S(1)}, f32[64,4096]{1,0:T(8,128)}, u32[]{:S(2)}) copy-start(f32[64,4096]{1,0:T(8,128)} %param.8) | copy-start | bytes 3145732
  81.1 32.0 %copy-start.3 = (f32[4096]{0:T(1024)S(1)}, f32[4096]{0:T(1024)}, u32[]{:S(2)}) copy-start(f32[4096]{0:T(1024)} %param.10) | copy-start | bytes 49156
  81.4 31.6 %copy-start.2 = (f32[64,4096]{1,0:T(8,128)S(1)}, f32[64,4096]{1,0:T(8,128)}, u32[]{:S(2)}) copy-start(f32[64,4096]{1,0:T(8,128)} %param.9) | copy-start | bytes 3145732
  113.3 8.3 %collective-permute-start.2 = (f32[64,256]{1,0:T(8,128)S(1)}, f32[64,256]{1,0:T(8,128)S(1)}, u32[]{:S(2)}, u32[]{:S(2)}) collective-permute-start(f32[64,256]{1,0:T(8,128)S(1)} %get-tuple-element.11), channel_id=1, source_target_pairs={{0,16},{16,32},{32,48},{48,64},{64,80},{80,96},{96,112},{112,128},... | collective-permute-start | bytes 196616 | tf_op jit(solution)/shard_map/ppermute | solution.py:14
  116.8 6.3 %collective-permute-start.3 = (f32[64,256]{1,0:T(8,128)S(1)}, f32[64,256]{1,0:T(8,128)S(1)}, u32[]{:S(2)}, u32[]{:S(2)}) collective-permute-start(f32[64,256]{1,0:T(8,128)S(1)} %get-tuple-element.12), channel_id=1, source_target_pairs={{16,0},{32,16},{48,32},{64,48},{80,64},{96,80},{112,96},{128,112},... | collective-permute-start | bytes 196616 | tf_op jit(solution)/shard_map/ppermute | solution.py:17
  141.3 32.0 %copy-start = (f32[1024,1024]{1,0:T(8,128)S(1)}, f32[1024,1024]{1,0:T(8,128)}, u32[]{:S(2)}) copy-start(f32[1024,1024]{1,0:T(8,128)} %all-gather.2.cloned.1.call-done) | copy-start | bytes 12582916
Sparse Core Ops, SparseCore 0:
  9.8 52.7 all-gather.1
where the time goes:
time: 306 us; the launch traced here: 304 us
  blocking collectives  209 us (68%)
  matrix products  40.8 us (13%)
  starting transfers between devices  16.1 us (5%)
  between operations  15.6 us (5%)
  local copies, waits for them, and re-layouts  14.1 us (5%)
  other arithmetic  4.98 us (2%)
  waiting for transfers between devices  3.25 us (1%)
    psum x1, blocking collectives, local(): norm_sum = lax.psum(jnp.sum(residual * residual), ('space', 'tm'))  78.9 us
    all_to_all x2, blocking collectives, temporal(): lax.all_to_all(grouped, 'tm', split_axis=1, concat_axis=0, tiled=True)  67.2 us
    all_to_all x2, blocking collectives, temporal(): lax.all_to_all(mixed_sites, 'tm', split_axis=0, concat_axis=1, tiled=True)  62.7 us
    dot_general x2, matrix products, spatial(): jnp.einsum('htnc,tnrc->htr', gathered, space_tiles, precision=lax.Precisi...  24.2 us
    dot_general x2, matrix products, kernel_items(): jnp.einsum('gh,hok->gok', full_kernel, piece, precision=lax.Precision.HIG...  16.6 us
    ppermute x2, starting transfers between devices, padded(): lax.ppermute(lax.slice_in_dim(block, 0, width, axis=dim), axis, backward)  9.08 us
    ppermute x2, starting transfers between devices, padded(): lax.ppermute(lax.slice_in_dim(block, block.shape[dim] - width, None, axis...  7 us
  transfers between devices with their start and end apart: 5, of which 3 were waited for; matrix products, arithmetic and copies ran while one was open for 7% of the time, Pallas kernels for 0%

commit v1 on v0

v1 whole, which is shorter than its diff:
```python
import jax
import jax.numpy as jnp
from jax import lax
from jax.experimental import pallas as pl
from jax.experimental.pallas import tpu as pltpu
from jax.sharding import PartitionSpec as P

REACH = 2
TILE = 128
CHIPS = 8
SAME_CORE = [[chip * 2 + core for chip in range(CHIPS)] for core in range(2)]
SIDE = 4
ORIGIN = (0, 4, 6, 2, 1, 5, 7, 3)
SWAP = [(i, i ^ 1) for i in range(2 * CHIPS)]
F32 = jnp.float32
BF16 = jnp.bfloat16
VMEM = pl.BlockSpec(memory_space=pltpu.VMEM)
SMEM = pl.BlockSpec(memory_space=pltpu.SMEM)
ANY = pl.BlockSpec(memory_space=pl.ANY)
HBM = pl.BlockSpec(memory_space=pltpu.HBM)


def along_z(shift):
    return [(z * 2 + c, (z + shift) % CHIPS * 2 + c) for z in range(CHIPS) for c in range(2)]


def halves(value):
    high = value.astype(BF16)
    return high, (value - high.astype(F32)).astype(BF16)


def params(megabytes):
    return pltpu.CompilerParams(vmem_limit_bytes=megabytes * 1024 * 1024)


def cost(flops, moved):
    return pl.CostEstimate(flops=flops, bytes_accessed=moved, transcendentals=0)


def dot_nt(a, b):
    return lax.dot_general(a, b, (((1,), (1,)), ((), ())), preferred_element_type=F32)


def dot_nn(a, b):
    return lax.dot_general(a, b, (((1,), (0,)), ((), ())), preferred_element_type=F32)


def stacked_halves(tiles):
    high, low = halves(tiles)
    return jnp.concatenate([high, low], axis=-2)


def weights_kernel(at_ref, tiles_ref, out_ref):
    out_ref[...] = stacked_halves(tiles_ref[...])


def weights_of(at, tiles):
    count, nb = tiles.shape[:2]
    rows = count // CHIPS
    return pl.pallas_call(
        weights_kernel,
        grid_spec=pltpu.PrefetchScalarGridSpec(
            num_scalar_prefetch=1,
            grid=(rows,),
            in_specs=[pl.BlockSpec((1, nb, TILE, TILE), lambda i, at: (at[0] * rows + i, 0, 0, 0))],
            out_specs=pl.BlockSpec((1, nb, 2 * TILE, TILE), lambda i, at: (i, 0, 0, 0)),
        ),
        out_shape=jax.ShapeDtypeStruct((rows, nb, 2 * TILE, TILE), BF16),
        compiler_params=params(56),
        cost_estimate=cost(0, 0),
        name="weights_of",
    )(at, tiles)


def space_wide_kernel(first, at_ref, ids_ref, edge_ref, noise_ref, x_ref, tiles_ref, right_ref, *refs):
    out_ref, win_ref, x_here, tile_ref, right_here, stage_ref, x_sems, tile_sems, right_sems, out_sems = refs[-10:]
    hours, sites = x_ref.shape
    groups = stage_ref.shape[0]
    rows, nb = tile_ref.shape[0] // groups, tile_ref.shape[1]
    width = rows * TILE
    count = sites // TILE
    needed = range(first * rows, (first + groups) * rows + 2 * REACH)
    inside = [i - REACH for i in needed if 0 <= i - REACH < count]
    pieces = range(inside[0] // rows, inside[-1] // rows + 1)
    place = lambda g: slice(g * width, (g + 1) * width)
    fetch = [pltpu.make_async_copy(x_ref.at[:, place(g)], x_here.at[:, place(g)], x_sems.at[g]) for g in pieces]
    tiles = [
        pltpu.make_async_copy(tiles_ref.at[first * rows + k], tile_ref.at[k], tile_sems.at[k])
        for k in range(rows * groups)
    ]
    right = [
        pltpu.make_async_copy(right_ref.at[:, place(first + k)], right_here.at[k], right_sems.at[k]) for k in range(groups)
    ]
    for copy in fetch + tiles + right:
        copy.start()
    for copy in fetch:
        copy.wait()
    for k, i in enumerate(needed):
        if i < REACH:
            piece = edge_ref[:, i * TILE : (i + 1) * TILE]
        elif i < count + REACH:
            piece = x_here[:, (i - REACH) * TILE : (i - REACH + 1) * TILE]
        else:
            j = i - count - REACH
            piece = edge_ref[:, j * TILE : (j + 1) * TILE]
        high, low = halves(piece)
        win_ref[k, :hours, :] = high
        win_ref[k, hours:, :] = low
    sent = []
    for k in range(groups):
        for i in range(rows):
            tiles[k * rows + i].wait()
        for i in range(rows):
            row = (first + k) * rows + i
            field = [win_ref[ids_ref[n, row] - at_ref[3] - first * rows] for n in range(nb)]
            mine = jnp.concatenate([tile_ref[k * rows + i, n] for n in range(nb)], axis=1)
            product = dot_nt(jnp.concatenate(field, axis=1), stacked_halves(mine))
            columns = slice(i * TILE, (i + 1) * TILE)
            stage_ref[k, :hours, columns] = product[:hours, :TILE] + (product[:hours, TILE:] + product[hours:, :TILE])
        right[k].wait()
        stage_ref[k, hours:, :] = right_here[k] - noise_ref[:, place(first + k)] * x_here[:, place(first + k)]
        sent.append(pltpu.make_async_copy(stage_ref.at[k], out_ref.at[first + k], out_sems.at[k]))
        sent[-1].start()
    for copy in sent:
        copy.wait()


def space_wide(first, at, ids, edge, x, tiles, right_side, noise, begun, after):
    hours, sites = x.shape
    nb, count = ids.shape
    rows, groups = count // CHIPS, CHIPS // 2
    more = ([] if begun is None else [begun]) + after
    return pl.pallas_call(
        lambda *refs: space_wide_kernel(first, *refs),
        in_specs=[SMEM] * 2 + [VMEM] * 2 + [HBM] * 3 + [ANY] * len(more),
        out_specs=ANY,
        out_shape=jax.ShapeDtypeStruct((CHIPS, 2 * hours, rows * TILE), F32),
        input_output_aliases={} if begun is None else {7: 0},
        scratch_shapes=[
            pltpu.VMEM((count // 2 + 2 * REACH, 2 * hours, TILE), BF16),
            pltpu.VMEM((hours, sites), F32),
            pltpu.VMEM((rows * groups, nb, TILE, TILE), F32),
            pltpu.VMEM((groups, hours, rows * TILE), F32),
            pltpu.VMEM((groups, 2 * hours, rows * TILE), F32),
            pltpu.SemaphoreType.DMA((CHIPS,)),
            pltpu.SemaphoreType.DMA((rows * groups,)),
            pltpu.SemaphoreType.DMA((groups,)),
            pltpu.SemaphoreType.DMA((groups,)),
        ],
        compiler_params=params(56),
        cost_estimate=cost(0, 0),
        name="space_wide",
    )(at, ids, edge, noise[None, :], x, tiles, right_side, *more)


def space_mixed_kernel(at_ref, ids_ref, left_ref, own_ref, right_ref, weights_ref, *refs):
    out_ref, hi_ref, lo_ref = refs[-3:]
    rows, nb = weights_ref.shape[:2]
    for i in range(rows + 2 * REACH):
        if i < REACH:
            piece = left_ref[:, :, i * TILE : (i + 1) * TILE]
        elif i < rows + REACH:
            piece = own_ref[:, :, (i - REACH) * TILE : (i - REACH + 1) * TILE]
        else:
            k = i - rows - REACH
            piece = right_ref[:, :, k * TILE : (k + 1) * TILE]
        high, low = halves(piece.reshape(-1, TILE))
        hi_ref[i] = high
        lo_ref[i] = low
    for row in range(rows):
        total = None
        for n in range(nb):
            i = ids_ref[n, at_ref[0] * rows + row] - at_ref[2]
            both = dot_nt(hi_ref[i], weights_ref[row, n])
            part = both[:, :TILE] + (both[:, TILE:] + dot_nt(lo_ref[i], weights_ref[row, n, :TILE]))
            total = part if total is None else total + part
        out_ref[:, :, row * TILE : (row + 1) * TILE] = total.reshape(out_ref.shape[:2] + (TILE,))


def space_mixed(at, ids, left, own, right, weights, after):
    nb, count = ids.shape
    rows, hours = count // CHIPS, own.shape[0] * own.shape[1]
    whole = lambda i, at, ids: (0, 0, 0)
    return pl.pallas_call(
        space_mixed_kernel,
        grid_spec=pltpu.PrefetchScalarGridSpec(
            num_scalar_prefetch=2,
            grid=(1,),
            in_specs=[
                pl.BlockSpec(left.shape, whole),
                pl.BlockSpec(own.shape, whole),
                pl.BlockSpec(right.shape, whole),
                pl.BlockSpec((rows, nb, 2 * TILE, TILE), lambda i, at, ids: (0, 0, 0, 0)),
            ]
            + [ANY] * len(after),
            out_specs=pl.BlockSpec(own.shape, whole),
            scratch_shapes=[pltpu.VMEM((rows + 2 * REACH, hours, TILE), BF16)] * 2,
        ),
        out_shape=jax.ShapeDtypeStruct(own.shape, F32),
        compiler_params=params(24),
        cost_estimate=cost(0, 0),
        name="space_mixed",
    )(at, ids, left, own, right, weights, *after)


def time_rows_kernel(at_ref, *refs):
    strips, (hi_ref, lo_ref) = refs[:SIDE], refs[SIDE:]
    chips, rows, _ = strips[0].shape
    for k in range(SIDE):
        row = pl.multiple_of((at_ref[4] + k) % SIDE * rows, rows)
        for j in range(chips):
            chip = (at_ref[0] + ORIGIN[j]) % chips
            high, low = halves(strips[k][j])
            hi_ref[chip, pl.ds(row, rows), :] = high
            lo_ref[chip, pl.ds(row, rows), :] = low


def time_rows(at, strips):
    chips, rows, depth = strips[0].shape
    shape = jax.ShapeDtypeStruct((chips, rows * SIDE, depth), BF16)
    return pl.pallas_call(
        time_rows_kernel,
        in_specs=[SMEM] + [VMEM] * SIDE,
        out_specs=(VMEM, VMEM),
        out_shape=(shape, shape),
        compiler_params=params(16),
        cost_estimate=cost(0, 0),
        name="time_rows",
    )(at, *strips)


def split_hours(at_ref, own_ref, other_ref, uhi_ref, ulo_ref):
    hours = other_ref.shape[1]
    for chip in range(CHIPS):
        for ref, core in ((own_ref, at_ref[1]), (other_ref, 1 - at_ref[1])):
            row = pl.multiple_of((2 * chip + core) * hours, hours)
            high, low = halves(ref[chip, :hours, :])
            uhi_ref[pl.ds(row, hours), :] = high
            ulo_ref[pl.ds(row, hours), :] = low


def time_product(khi_ref, klo_ref, uhi_ref, ulo_ref, columns):
    chips, hours, depth = khi_ref.shape
    khi = khi_ref[...].reshape(chips * hours, depth)
    klo = klo_ref[...].reshape(chips * hours, depth)
    uhi, ulo = uhi_ref[:, columns], ulo_ref[:, columns]
    mixed = dot_nn(khi, uhi) + (dot_nn(khi, ulo) + dot_nn(klo, uhi))
    return mixed.reshape(chips, hours, -1)


def residual_kernel(at_ref, khi_ref, klo_ref, got_ref, other_ref, out_ref, uhi_ref, ulo_ref):
    chips, hours, sites = out_ref.shape
    split_hours(at_ref, got_ref, other_ref, uhi_ref, ulo_ref)
    width = sites // 2
    for part in range(2):
        columns = slice(part * width, (part + 1) * width)
        mixed = time_product(khi_ref, klo_ref, uhi_ref, ulo_ref, columns)
        out_ref[:, :, columns] = got_ref[:, hours:, columns] - mixed


def residual_of(at, khi, klo, got, other):
    chips, hours, sites = other.shape
    return pl.pallas_call(
        residual_kernel,
        in_specs=[SMEM] + [VMEM] * 4,
        out_specs=VMEM,
        out_shape=jax.ShapeDtypeStruct(other.shape, F32),
        scratch_shapes=[pltpu.VMEM((2 * chips * hours, sites), BF16)] * 2,
        compiler_params=params(24),
        cost_estimate=cost(0, 0),
        name="residual_of",
    )(at, khi, klo, got, other)


def image_kernel(at_ref, khi_ref, klo_ref, own_ref, other_ref, r_ref, noise_ref, out_ref, sums_ref, uhi_ref, ulo_ref, image_ref, sems):
    chips, hours, sites = own_ref.shape
    width = sites // 2
    places = [slice(part * width, (part + 1) * width) for part in range(2)]
    copies = [
        pltpu.make_async_copy(image_ref.at[:, :, place], out_ref.at[:, pl.ds(0, hours), place], sems.at[part])
        for part, place in enumerate(places)
    ]
    kept = pltpu.make_async_copy(r_ref, out_ref.at[:, pl.ds(hours, hours)], sems.at[2])
    kept.start()
    split_hours(at_ref, own_ref, other_ref, uhi_ref, ulo_ref)
    squares = jnp.zeros((8, TILE), F32)
    curves = jnp.zeros((8, TILE), F32)
    for copy, columns in zip(copies, places):
        mixed = time_product(khi_ref, klo_ref, uhi_ref, ulo_ref, columns)
        r = r_ref[:, :, columns]
        image = mixed + noise_ref[:, columns][None] * r
        image_ref[:, :, columns] = image
        copy.start()
        for t in range(width // TILE):
            piece = slice(t * TILE, (t + 1) * TILE)
            a, b = r[:, :, piece].reshape(-1, 8, TILE), image[:, :, piece].reshape(-1, 8, TILE)
            squares += jnp.sum(a * a, axis=0)
            curves += jnp.sum(a * b, axis=0)
    sums_ref[:8, :] = squares
    sums_ref[8:, :] = curves
    for copy in copies + [kept]:
        copy.wait()


def image_of(at, khi, klo, own, other, residual, noise):
    chips, hours, sites = own.shape
    return pl.pallas_call(
        image_kernel,
        in_specs=[SMEM] + [VMEM] * 6,
        out_specs=[ANY, VMEM],
        out_shape=[jax.ShapeDtypeStruct((chips, 2 * hours, sites), F32), jax.ShapeDtypeStruct((16, TILE), F32)],
        scratch_shapes=[pltpu.VMEM((2 * chips * hours, sites), BF16)] * 2
        + [pltpu.VMEM(own.shape, F32), pltpu.SemaphoreType.DMA((3,))],
        compiler_params=params(24),
        cost_estimate=cost(0, 0),
        name="image_of",
    )(at, khi, klo, own, other, residual, noise)


def update_kernel(start_ref, got_ref, *refs):
    sums, (iterate_ref, next_ref) = refs[:-2], refs[-2:]
    chips, _, width = got_ref.shape
    hours = start_ref.shape[0]
    total = sums[0][...]
    for part in sums[1:]:
        total += part[...]
    alpha = jnp.sum(total[:8, :]) / jnp.sum(total[8:, :])
    for g in range(chips):
        columns = slice(g * width, (g + 1) * width)
        r = got_ref[g, hours:, :]
        iterate_ref[:, columns] = start_ref[:, columns] + alpha * r
        next_ref[:, columns] = r - alpha * got_ref[g, :hours, :]


def update(start, got, sums):
    shape = jax.ShapeDtypeStruct(start.shape, F32)
    return pl.pallas_call(
        update_kernel,
        in_specs=[VMEM] * (2 + len(sums)),
        out_specs=(VMEM, VMEM),
        out_shape=(shape, shape),
        compiler_params=params(24),
        cost_estimate=cost(0, 0),
        name="update",
    )(start, got, *sums)


def first_rows_kernel(value_ref, *refs):
    refs[-1][...] = value_ref[:, : refs[-1].shape[1], :]


def first_rows(value, rows, after):
    return pl.pallas_call(
        first_rows_kernel,
        in_specs=[VMEM] + [ANY] * len(after),
        out_specs=VMEM,
        out_shape=jax.ShapeDtypeStruct((value.shape[0], rows, value.shape[2]), F32),
        compiler_params=params(16),
        cost_estimate=cost(0, 0),
        name="first_rows",
    )(value, *after)


def ordered(value, *after):
    return pl.pallas_call(
        lambda *refs: None,
        in_specs=[ANY] * (1 + len(after)),
        out_specs=ANY,
        out_shape=jax.ShapeDtypeStruct(value.shape, value.dtype),
        input_output_aliases={0: 0},
        cost_estimate=cost(0, 0),
        name="ordered",
    )(value, *after)


def joined_kernel(a_ref, b_ref, *refs):
    refs[-1][: a_ref.shape[0]] = a_ref[...]
    refs[-1][a_ref.shape[0] :] = b_ref[...]


def joined(a, b, after):
    return pl.pallas_call(
        joined_kernel,
        in_specs=[VMEM] * 2 + [ANY] * len(after),
        out_specs=VMEM,
        out_shape=jax.ShapeDtypeStruct((a.shape[0] + b.shape[0],) + a.shape[1:], F32),
        compiler_params=params(8),
        cost_estimate=cost(0, 0),
        name="joined",
    )(a, b, *after)


def token(value):
    return value.reshape((-1,) + value.shape[-2:])[0, :16, :TILE]


def exchange(blocks):
    return lax.all_to_all(blocks, "tm", 0, 0, axis_index_groups=SAME_CORE, tiled=True)


def along_side(shift, axis):
    place = lambda a, b: a * SIDE + b
    if axis == "y":
        return [(place(a, b), place(a, (b + shift) % SIDE)) for a in range(SIDE) for b in range(SIDE)]
    return [(place(a, b), place((a + shift) % SIDE, b)) for a in range(SIDE) for b in range(SIDE)]


def local(start, right_side, noise, tile_ids, space_tiles, time_kernel):
    hours_dev, sites_dev = start.shape
    count = tile_ids.shape[0]
    width = sites_dev // CHIPS
    edge = REACH * TILE
    spaces = lax.axis_size("space")
    space, tm = lax.axis_index("space"), lax.axis_index("tm")
    chip, core = tm // 2, tm % 2
    base = space * count - REACH
    at = jnp.stack([chip, core, base + chip * (count // CHIPS), base, space % SIDE]).astype(jnp.int32)

    forward = [(i, i + 1) for i in range(spaces - 1)]
    backward = [(target, source) for source, target in forward]
    low = lax.ppermute(start[:, sites_dev - edge :], "space", forward)
    high = lax.ppermute(start[:, :edge], "space", backward)
    rows = time_kernel.shape[0] // SIDE
    ids = tile_ids.T
    strip = lax.dynamic_slice(time_kernel, (space % SIDE * rows, 0), (rows, time_kernel.shape[1]))[None]
    far = lax.ppermute(strip, "tm", along_z(4))
    strip = joined(strip, far, [token(low), token(high)])
    far = lax.ppermute(strip, "tm", along_z(2))
    sent = space_wide(0, at, ids, low, start, space_tiles, right_side, noise, None, [])
    strip = joined(strip, far, [token(sent)])
    far = lax.ppermute(strip, "tm", along_z(-1))
    sent = space_wide(CHIPS // 2, at, ids, high, start, space_tiles, right_side, noise, sent, [token(strip)])
    strip = joined(strip, far, [])
    strips = [strip] + [lax.ppermute(strip, "space", along_side(-k, "y")) for k in range(1, SIDE)]
    khi, klo = time_rows(at, strips)
    weights = weights_of(at, space_tiles)

    got = exchange(ordered(sent, token(far)))
    other = lax.ppermute(first_rows(got, hours_dev, [token(khi), token(weights)]), "tm", SWAP)
    residual = residual_of(at, khi, klo, got, other)

    up, down = [], []
    for s in range(spaces):
        for z in range(CHIPS):
            for c in range(2):
                source, target = (s * CHIPS + z), (s * CHIPS + z + 1)
                if target < spaces * CHIPS:
                    up.append((source * 2 + c, target * 2 + c))
                    down.append((target * 2 + c, source * 2 + c))
    left = lax.ppermute(residual[:, :, width - edge :], ("space", "tm"), up)
    right = lax.ppermute(residual[:, :, :edge], ("space", "tm"), down)
    mixed = space_mixed(at, ids, left, residual, right, weights, [])
    other = lax.ppermute(mixed, "tm", SWAP)
    noise_here = lax.dynamic_slice(noise, (chip * width,), (width,))[None, :]
    image, sums = image_of(at, khi, klo, mixed, other, residual, noise_here)
    back = exchange(image)
    sums = sums + lax.ppermute(sums, "tm", SWAP)
    for axis in ("y", "x"):
        for shift in (2, 1):
            sums = sums + lax.ppermute(sums, "space", along_side(shift, axis))
    sums = [sums] + [lax.ppermute(sums, "tm", along_z(shift)) for shift in range(1, CHIPS)]
    return update(start, back, sums)


def solution(mesh):
    placed = (
        P("tm", "space"),
        P("tm", "space"),
        P("space"),
        P("space", None),
        P("space", None, None, None),
        P("tm", None),
    )
    return jax.shard_map(
        local,
        mesh=mesh,
        in_specs=placed,
        out_specs=(P("tm", "space"), P("tm", "space")),
        check_vma=False,
    )
```

time: 306 us -> 197 us (0.64)
  blocking collectives: 209 us -> 0 us
  waiting for transfers between devices: 3.25 us -> 95.7 us
  starting transfers between devices: 16.1 us -> 58.4 us
  matrix products: 40.8 us -> 0 us
  Pallas kernels: 0 us -> 31.3 us
  between operations: 15.6 us -> 0.93 us
  other arithmetic: 4.98 us -> 0.02 us
  local copies, waits for them, and re-layouts: 14.1 us -> 9.55 us
    all_to_all x4 -> x0, blocking collectives: 130 us -> none  [the longest x2 67.2 us: temporal(): lax.all_to_all(grouped, 'tm', split_axis=1, concat_axis=0, tiled=True)]
    psum x1 -> x0, blocking collectives: 78.9 us -> none  [local(): norm_sum = lax.psum(jnp.sum(residual * residual), ('space', 'tm'))]
    ppermute x4 -> x24, waiting for transfers between devices: 2.57 us -> 75.7 us  [the longest x4 17.7 us: local(): sums = sums + lax.ppermute(sums, 'space', along_side(shift, axis))]
    dot_general x4 -> x0, matrix products: 40.8 us -> none  [the longest x2 24.2 us: spatial(): jnp.einsum('htnc,tnrc->htr', gathered, space_tiles, precision=lax.Precisi...]
    pallas_call x0 -> x13, Pallas kernels: none -> 31.3 us  [the longest x2 12.6 us: space_wide(): pl.pallas_call(lambda *refs: space_wide_kernel(first, *refs), in_specs=[S...]
    ppermute x4 -> x24, starting transfers between devices: 16.1 us -> 44.5 us  [the longest x7 17.6 us: local(): lax.ppermute(sums, 'tm', along_z(shift))]
    all_to_all x0 -> x2, waiting for transfers between devices: none -> 20 us  [exchange(): lax.all_to_all(blocks, 'tm', 0, 0, axis_index_groups=SAME_CORE, tiled=True)]
    all_to_all x0 -> x2, starting transfers between devices: none -> 13.9 us  [exchange(): lax.all_to_all(blocks, 'tm', 0, 0, axis_index_groups=SAME_CORE, tiled=True)]
  transfers between devices with their start and end apart: 5 -> 26, of which waited for: 3 -> 15; matrix products, arithmetic and copies ran while one was open for 7% -> 2% of each run, Pallas kernels for 0% -> 9%
where the time goes in v1:
time: 197 us; the launch traced here: 196 us
  waiting for transfers between devices  95.7 us (49%)
  starting transfers between devices  58.4 us (30%)
  Pallas kernels  31.3 us (16%)
  local copies, waits for them, and re-layouts  9.55 us (5%)
    all_to_all x2, waiting for transfers between devices, exchange(): lax.all_to_all(blocks, 'tm', 0, 0, axis_index_groups=SAME_CORE, tiled=True)  20 us
    ppermute x4, waiting for transfers between devices, local(): sums = sums + lax.ppermute(sums, 'space', along_side(shift, axis))  17.7 us
    ppermute x7, starting transfers between devices, local(): lax.ppermute(sums, 'tm', along_z(shift))  17.6 us
    ppermute x3, waiting for transfers between devices, local(): lax.ppermute(strip, 'space', along_side(-k, 'y'))  16.9 us
    ppermute x7, waiting for transfers between devices, local(): lax.ppermute(sums, 'tm', along_z(shift))  16.5 us
    all_to_all x2, starting transfers between devices, exchange(): lax.all_to_all(blocks, 'tm', 0, 0, axis_index_groups=SAME_CORE, tiled=True)  13.9 us
    pallas_call x2, Pallas kernels, space_wide(): pl.pallas_call(lambda *refs: space_wide_kernel(first, *refs), in_specs=[S...  12.6 us
    ppermute x1, waiting for transfers between devices, local(): right = lax.ppermute(residual[:, :, :edge], ('space', 'tm'), down)  9.67 us
  transfers between devices with their start and end apart: 26, of which 15 were waited for; matrix products, arithmetic and copies ran while one was open for 2% of the time, Pallas kernels for 9%

profile of v1, /device:TPU:38, one launch (start us, length us, event | category | flops | bytes accessed | tf_op | source)
XLA Modules:
  0.0 195.9 jit_solution(14090180607021298617)
XLA Ops:
  0.6 0.9 fusion.1
  1.6 5.2 %collective-permute-start.2 = (f32[64,256]{1,0:T(8,128)S(1)}, f32[64,256]{1,0:T(8,128)S(1)}, u32[]{:S(2)}, u32[]{:S(2)}) collective-permute-start(f32[64,256]{1,0:T(8,128)S(1)} %get-tuple-element.12), channel_id=1, source_target_pairs={{16,0},{32,16},{48,32},{64,48},{80,64},{96,80},{112,96},{128,112},... | collective-permute-start | bytes 196616 | tf_op jit(solution)/shard_map/ppermute | solution.py:422
  6.8 6.4 %collective-permute-start = (f32[1,16,1024]{2,1,0:T(8,128)S(1)}, f32[1,16,1024]{2,1,0:T(8,128)S(1)}, u32[]{:S(2)}, u32[]{:S(2)}) collective-permute-start(f32[1,16,1024]{2,1,0:T(8,128)S(1)} %dynamic-slice_bitcast_fusion.a_ref), channel_id=1, source_target_pairs={{0,8},{1,9},{2,10},{3,11},{4,12},{5,13},{6,14},{7,15},{8,0},{9,1},... | collective-permute-start | bytes 196616 | tf_op jit(solution)/shard_map/ppermute | solution.py:426
  13.2 1.9 collective-permute-start.1
  15.8 5.7 %collective-permute-done.1.refs_2_ = f32[64,256]{1,0:T(8,128)S(1)} collective-permute-done((f32[64,256]{1,0:T(8,128)S(1)}, f32[64,256]{1,0:T(8,128)S(1)}, u32[]{:S(2)}, u32[]{:S(2)}) %collective-permute-start.1) | collective-permute-done | bytes 65568 | tf_op jit(solution)/shard_map/ppermute | solution.py:421
  21.5 1.5 collective-permute-start.3
  23.0 6.3 %space_wide.2.refs_7_ = f32[8,128,512]{2,1,0:T(8,128)} custom-call(s32[5]{0:T(128)} %stack.23.refs_0_.at_ref, s32[4,32]{1,0:T(4,128)} %bitcast.28, f32[64,256]{1,0:T(8,128)} %copy-done.13, f32[1,4096]{1,0:T(1,128)} %bitcast.34, f32[64,4096]{1,0:T(8,128)} %start_ref.1, f32[32,4,128,128]{3,2,1,0:T(8,128)} %tiles_ref.1, f32[64,4096]{1,0:T(8,128)} %refs_6_.3), custom_call_target="tpu_custom_call" | custom-call | tf_op jit(solution)/shard_map/space_wide/pallas_call | solution.py:133
  29.3 0.7 slice_bitcast_fusion.2.refs_0_
  30.1 1.1 collective-permute-start.4
  31.8 6.3 %space_wide.3.refs_0_ = f32[8,128,512]{2,1,0:T(8,128)} custom-call(s32[5]{0:T(128)} %stack.23.refs_0_.at_ref, s32[4,32]{1,0:T(4,128)} %bitcast.29, f32[64,256]{1,0:T(8,128)} %copy-done.12, f32[1,4096]{1,0:T(1,128)} %bitcast.35, f32[64,4096]{1,0:T(8,128)} %start_ref.1, f32[32,4,128,128]{3,2,1,0:T(8,128)} %tiles_ref.1, ...), custom_call_target="tpu_custom_call", output_to_operand_aliasing={{}: (7, {})} | custom-call | tf_op jit(solution)/shard_map/space_wide/pallas_call | solution.py:133
  38.7 5.7 %all-to-all-start = ((f32[8,128,512]{2,1,0:T(8,128)}), f32[8,128,512]{2,1,0:T(8,128)S(1)}, u32[]{:S(2)}, u32[]{:S(2)}) async-start(f32[8,128,512]{2,1,0:T(8,128)} %ordered.1), calls=%async_computation | async-start | bytes 4194304 | tf_op jit(solution)/shard_map/all_to_all | solution.py:398
  44.5 1.0 collective-permute-start.6
  45.5 2.3 %collective-permute-start.5 = (f32[8,16,1024]{2,1,0:T(8,128)S(1)}, f32[8,16,1024]{2,1,0:T(8,128)S(1)}, u32[]{:S(2)}, u32[]{:S(2)}) collective-permute-start(f32[8,16,1024]{2,1,0:T(8,128)S(1)} %joined.5.refs_0_), channel_id=1, source_target_pairs={{0,48},{16,0},{32,16},{48,32},{64,112},{80,64},{96,80},{112,96},{1... | collective-permute-start | bytes 1572872 | tf_op jit(solution)/shard_map/ppermute | solution.py:434
  47.8 4.1 %weights_of.1.weights_ref = bf16[4,4,256,128]{3,2,1,0:T(8,128)(2,1)} custom-call(s32[5]{0:T(128)} %stack.23.refs_0_.at_ref, f32[32,4,128,128]{3,2,1,0:T(8,128)} %tiles_ref.1), custom_call_target="tpu_custom_call" | custom-call | tf_op jit(solution)/shard_map/weights_of/pallas_call | solution.py:60
  51.8 16.3 %collective-permute-done.7.refs_3_ = f32[8,16,1024]{2,1,0:T(8,128)S(1)} collective-permute-done((f32[8,16,1024]{2,1,0:T(8,128)S(1)}, f32[8,16,1024]{2,1,0:T(8,128)S(1)}, u32[]{:S(2)}, u32[]{:S(2)}) %collective-permute-start.7) | collective-permute-done | bytes 524320 | tf_op jit(solution)/shard_map/ppermute | solution.py:434
  68.7 0.8 time_rows.1
  69.5 1.0 copy-done.6
  70.5 0.7 slice_bitcast_fusion.5
  71.2 1.0 copy-done.2
  72.1 20.0 %all-to-all-done.value_ref.got_ref = f32[8,128,512]{2,1,0:T(8,128)S(1)} async-done(((f32[8,128,512]{2,1,0:T(8,128)}), f32[8,128,512]{2,1,0:T(8,128)S(1)}, u32[]{:S(2)}, u32[]{:S(2)}) %all-to-all-start) | async-done | bytes 2097184 | tf_op jit(solution)/shard_map/all_to_all | solution.py:398
  92.3 2.6 %collective-permute-done.8.other_ref = f32[8,64,512]{2,1,0:T(8,128)S(1)} collective-permute-done((f32[8,64,512]{2,1,0:T(8,128)S(1)}, f32[8,64,512]{2,1,0:T(8,128)S(1)}, u32[]{:S(2)}, u32[]{:S(2)}) %collective-permute-start.8) | collective-permute-done | bytes 1048608 | tf_op jit(solution)/shard_map/ppermute | solution.py:439
  95.0 2.7 %residual_of.1.own_ref.r_ref = f32[8,64,512]{2,1,0:T(8,128)S(1)} custom-call(s32[5]{0:T(128)S(1)} %copy-done.10, bf16[8,64,1024]{2,1,0:T(8,128)(2,1)S(1)} %copy-done.3, bf16[8,64,1024]{2,1,0:T(8,128)(2,1)S(1)} %copy-done.7, f32[8,128,512]{2,1,0:T(8,128)S(1)} %all-to-all-done.value_ref.got_ref, f32[8,64,512]{2,1,0:T(8,128)S(1)} %collective-permute-done.8.other_ref), custom_call_target="tpu_custom_call" | custom-call | tf_op jit(solution)/shard_map/residual_of/pallas_call | solution.py:263
  97.8 3.5 %collective-permute-start.10 = (f32[8,64,256]{2,1,0:T(8,128)S(1)}, f32[8,64,256]{2,1,0:T(8,128)S(1)}, u32[]{:S(2)}, u32[]{:S(2)}) collective-permute-start(f32[8,64,256]{2,1,0:T(8,128)S(1)} %get-tuple-element.10), channel_id=1, source_target_pairs={{2,0},{3,1},{4,2},{5,3},{6,4},{7,5},{8,6},{9,7},{10,8},{11,9},{12,... | collective-permute-start | bytes 1572872 | tf_op jit(solution)/shard_map/ppermute | solution.py:451
  101.3 2.8 %collective-permute-start.9 = (f32[8,64,256]{2,1,0:T(8,128)S(1)}, f32[8,64,256]{2,1,0:T(8,128)S(1)}, u32[]{:S(2)}, u32[]{:S(2)}) collective-permute-start(f32[8,64,256]{2,1,0:T(8,128)S(1)} %get-tuple-element.11), channel_id=1, source_target_pairs={{0,2},{1,3},{2,4},{3,5},{4,6},{5,7},{6,8},{7,9},{8,10},{9,11},{10,... | collective-permute-start | bytes 1572872 | tf_op jit(solution)/shard_map/ppermute | solution.py:450
  104.1 9.7 %collective-permute-done.10.right_ref = f32[8,64,256]{2,1,0:T(8,128)S(1)} collective-permute-done((f32[8,64,256]{2,1,0:T(8,128)S(1)}, f32[8,64,256]{2,1,0:T(8,128)S(1)}, u32[]{:S(2)}, u32[]{:S(2)}) %collective-permute-start.10) | collective-permute-done | bytes 524320 | tf_op jit(solution)/shard_map/ppermute | solution.py:451
  113.8 3.2 %collective-permute-done.9.left_ref = f32[8,64,256]{2,1,0:T(8,128)S(1)} collective-permute-done((f32[8,64,256]{2,1,0:T(8,128)S(1)}, f32[8,64,256]{2,1,0:T(8,128)S(1)}, u32[]{:S(2)}, u32[]{:S(2)}) %collective-permute-start.9) | collective-permute-done | bytes 524320 | tf_op jit(solution)/shard_map/ppermute | solution.py:450
  117.0 3.9 %space_mixed.1.own_ref = f32[8,64,512]{2,1,0:T(8,128)} custom-call(s32[5]{0:T(128)S(1)} %copy-done.10, s32[4,32]{1,0:T(4,128)S(1)} %bitcast.30, f32[8,64,256]{2,1,0:T(8,128)S(1)} %collective-permute-done.9.left_ref, f32[8,64,512]{2,1,0:T(8,128)S(1)} %residual_of.1.own_ref.r_ref, f32[8,64,256]{2,1,0:T(8,128)S(1)} %collective-permute-done.10.right_ref, ...), custom_call_target="tpu_custom_call" | custom-call | tf_op jit(solution)/shard_map/space_mixed/pallas_call | solution.py:184
  120.9 0.8 dynamic_slice.7
  121.7 2.1 %collective-permute-done.11.other_ref = f32[8,64,512]{2,1,0:T(8,128)S(1)} collective-permute-done((f32[8,64,512]{2,1,0:T(8,128)}, f32[8,64,512]{2,1,0:T(8,128)S(1)}, u32[]{:S(2)}, u32[]{:S(2)}) %collective-permute-start.11) | collective-permute-done | bytes 1048608 | tf_op jit(solution)/shard_map/ppermute | solution.py:453
  123.8 1.2 copy-done.8
  125.0 5.4 %image_of.1 = (f32[8,128,512]{2,1,0:T(8,128)S(1)}, f32[16,128]{1,0:T(8,128)S(1)}) custom-call(s32[5]{0:T(128)S(1)} %copy-done.10, bf16[8,64,1024]{2,1,0:T(8,128)(2,1)S(1)} %copy-done.4, bf16[8,64,1024]{2,1,0:T(8,128)(2,1)S(1)} %copy-done.8, f32[8,64,512]{2,1,0:T(8,128)} %space_mixed.1.own_ref, f32[8,64,512]{2,1,0:T(8,128)S(1)} %collective-permute-done.11.other_ref, ...), custom_call_target="tpu_custom_call" | custom-call | tf_op jit(solution)/shard_map/image_of/pallas_call | solution.py:307
  130.5 1.3 copy-done.9
  131.8 8.1 %all-to-all-start.1 = ((f32[8,128,512]{2,1,0:T(8,128)}), f32[8,128,512]{2,1,0:T(8,128)S(1)}, u32[]{:S(2)}, u32[]{:S(2)}) async-start(f32[8,128,512]{2,1,0:T(8,128)} %copy-done.9), calls=%async_computation.1 | async-start | bytes 4194304 | tf_op jit(solution)/shard_map/all_to_all | solution.py:398
  140.0 1.2 collective-permute-done.12
  141.2 5.2 %collective-permute-done.13 = f32[16,128]{1,0:T(8,128)S(1)} collective-permute-done((f32[16,128]{1,0:T(8,128)S(1)}, f32[16,128]{1,0:T(8,128)S(1)}, u32[]{:S(2)}, u32[]{:S(2)}) %collective-permute-start.13) | collective-permute-done | bytes 8224 | tf_op jit(solution)/shard_map/ppermute | solution.py:460
  146.3 4.9 %collective-permute-done.14 = f32[16,128]{1,0:T(8,128)S(1)} collective-permute-done((f32[16,128]{1,0:T(8,128)S(1)}, f32[16,128]{1,0:T(8,128)S(1)}, u32[]{:S(2)}, u32[]{:S(2)}) %collective-permute-start.14) | collective-permute-done | bytes 8224 | tf_op jit(solution)/shard_map/ppermute | solution.py:460
  151.2 1.1 collective-permute-start.15
  152.3 4.0 %collective-permute-done.15 = f32[16,128]{1,0:T(8,128)S(1)} collective-permute-done((f32[16,128]{1,0:T(8,128)S(1)}, f32[16,128]{1,0:T(8,128)S(1)}, u32[]{:S(2)}, u32[]{:S(2)}) %collective-permute-start.15) | collective-permute-done | bytes 8224 | tf_op jit(solution)/shard_map/ppermute | solution.py:460
  156.4 3.6 %collective-permute-done.16 = f32[16,128]{1,0:T(8,128)S(1)} collective-permute-done((f32[16,128]{1,0:T(8,128)S(1)}, f32[16,128]{1,0:T(8,128)S(1)}, u32[]{:S(2)}, u32[]{:S(2)}) %collective-permute-start.16) | collective-permute-done | bytes 8224 | tf_op jit(solution)/shard_map/ppermute | solution.py:460
  160.2 4.0 %collective-permute-start.22 = (f32[16,128]{1,0:T(8,128)S(1)}, f32[16,128]{1,0:T(8,128)S(1)}, u32[]{:S(2)}, u32[]{:S(2)}) collective-permute-start(f32[16,128]{1,0:T(8,128)S(1)} %add.43.refs_0_), channel_id=1, source_target_pairs={{0,12},{1,13},{2,14},{3,15},{4,0},{5,1},{6,2},{7,3},{8,4},{9,5},{1... | collective-permute-start | bytes 24584 | tf_op jit(solution)/shard_map/ppermute | solution.py:461
  164.2 2.3 %collective-permute-start.21 = (f32[16,128]{1,0:T(8,128)S(1)}, f32[16,128]{1,0:T(8,128)S(1)}, u32[]{:S(2)}, u32[]{:S(2)}) collective-permute-start(f32[16,128]{1,0:T(8,128)S(1)} %add.43.refs_0_), channel_id=1, source_target_pairs={{0,10},{1,11},{2,12},{3,13},{4,14},{5,15},{6,0},{7,1},{8,2},{9,3},... | collective-permute-start | bytes 24584 | tf_op jit(solution)/shard_map/ppermute | solution.py:461
  166.5 2.7 %collective-permute-start.20 = (f32[16,128]{1,0:T(8,128)S(1)}, f32[16,128]{1,0:T(8,128)S(1)}, u32[]{:S(2)}, u32[]{:S(2)}) collective-permute-start(f32[16,128]{1,0:T(8,128)S(1)} %add.43.refs_0_), channel_id=1, source_target_pairs={{0,8},{1,9},{2,10},{3,11},{4,12},{5,13},{6,14},{7,15},{8,0},{9,1},... | collective-permute-start | bytes 24584 | tf_op jit(solution)/shard_map/ppermute | solution.py:461
  169.2 2.3 %collective-permute-start.19 = (f32[16,128]{1,0:T(8,128)S(1)}, f32[16,128]{1,0:T(8,128)S(1)}, u32[]{:S(2)}, u32[]{:S(2)}) collective-permute-start(f32[16,128]{1,0:T(8,128)S(1)} %add.43.refs_0_), channel_id=1, source_target_pairs={{0,6},{1,7},{2,8},{3,9},{4,10},{5,11},{6,12},{7,13},{8,14},{9,15},... | collective-permute-start | bytes 24584 | tf_op jit(solution)/shard_map/ppermute | solution.py:461
  171.5 15.0 %collective-permute-done.23.refs_7_ = f32[16,128]{1,0:T(8,128)S(1)} collective-permute-done((f32[16,128]{1,0:T(8,128)S(1)}, f32[16,128]{1,0:T(8,128)S(1)}, u32[]{:S(2)}, u32[]{:S(2)}) %collective-permute-start.23) | collective-permute-done | bytes 8224 | tf_op jit(solution)/shard_map/ppermute | solution.py:461
  186.5 4.0 %collective-permute-start.18 = (f32[16,128]{1,0:T(8,128)S(1)}, f32[16,128]{1,0:T(8,128)S(1)}, u32[]{:S(2)}, u32[]{:S(2)}) collective-permute-start(f32[16,128]{1,0:T(8,128)S(1)} %add.43.refs_0_), channel_id=1, source_target_pairs={{0,4},{1,5},{2,6},{3,7},{4,8},{5,9},{6,10},{7,11},{8,12},{9,13},{1... | collective-permute-start | bytes 24584 | tf_op jit(solution)/shard_map/ppermute | solution.py:461
  190.5 2.1 %collective-permute-start.17 = (f32[16,128]{1,0:T(8,128)S(1)}, f32[16,128]{1,0:T(8,128)S(1)}, u32[]{:S(2)}, u32[]{:S(2)}) collective-permute-start(f32[16,128]{1,0:T(8,128)S(1)} %add.43.refs_0_), channel_id=1, source_target_pairs={{0,2},{1,3},{2,4},{3,5},{4,6},{5,7},{6,8},{7,9},{8,10},{9,11},{10,... | collective-permute-start | bytes 24584 | tf_op jit(solution)/shard_map/ppermute | solution.py:461
  192.6 1.5 collective-permute-done.17.refs_1_
  194.2 1.7 update.1
  (61 shorter events, 3.2 us)
Async XLA Ops:
  0.6 6.2 %copy-start = (f32[64,1024]{1,0:T(8,128)S(1)}, f32[64,1024]{1,0:T(8,128)}, u32[]{:S(2)}) copy-start(f32[64,1024]{1,0:T(8,128)} %param.11) | copy-start | bytes 786436
  1.6 14.2 %collective-permute-start.2 = (f32[64,256]{1,0:T(8,128)S(1)}, f32[64,256]{1,0:T(8,128)S(1)}, u32[]{:S(2)}, u32[]{:S(2)}) collective-permute-start(f32[64,256]{1,0:T(8,128)S(1)} %get-tuple-element.12), channel_id=1, source_target_pairs={{16,0},{32,16},{48,32},{64,48},{80,64},{96,80},{112,96},{128,112},... | collective-permute-start | bytes 196616 | tf_op jit(solution)/shard_map/ppermute | solution.py:422
  6.8 14.6 %collective-permute-start = (f32[1,16,1024]{2,1,0:T(8,128)S(1)}, f32[1,16,1024]{2,1,0:T(8,128)S(1)}, u32[]{:S(2)}, u32[]{:S(2)}) collective-permute-start(f32[1,16,1024]{2,1,0:T(8,128)S(1)} %dynamic-slice_bitcast_fusion.a_ref), channel_id=1, source_target_pairs={{0,8},{1,9},{2,10},{3,11},{4,12},{5,13},{6,14},{7,15},{8,0},{9,1},... | collective-permute-start | bytes 196616 | tf_op jit(solution)/shard_map/ppermute | solution.py:426
  13.2 8.3 %collective-permute-start.1 = (f32[64,256]{1,0:T(8,128)S(1)}, f32[64,256]{1,0:T(8,128)S(1)}, u32[]{:S(2)}, u32[]{:S(2)}) collective-permute-start(f32[64,256]{1,0:T(8,128)S(1)} %get-tuple-element.13), channel_id=1, source_target_pairs={{0,16},{16,32},{32,48},{48,64},{64,80},{80,96},{96,112},{112,128},... | collective-permute-start | bytes 196616 | tf_op jit(solution)/shard_map/ppermute | solution.py:421
  15.8 13.6 %copy-start.12 = (f32[64,256]{1,0:T(8,128)}, f32[64,256]{1,0:T(8,128)S(1)}, u32[]{:S(2)}) copy-start(f32[64,256]{1,0:T(8,128)S(1)} %collective-permute-done.2.refs_2_) | copy-start | bytes 196612
  21.5 1.6 copy-start.13
  21.5 8.6 %collective-permute-start.3 = (f32[2,16,1024]{2,1,0:T(8,128)S(1)}, f32[2,16,1024]{2,1,0:T(8,128)S(1)}, u32[]{:S(2)}, u32[]{:S(2)}) collective-permute-start(f32[2,16,1024]{2,1,0:T(8,128)S(1)} %joined.3.a_ref), channel_id=1, source_target_pairs={{0,4},{1,5},{2,6},{3,7},{4,8},{5,9},{6,10},{7,11},{8,12},{9,13},{1... | collective-permute-start | bytes 393224 | tf_op jit(solution)/shard_map/ppermute | solution.py:428
  30.1 8.0 %collective-permute-start.4 = (f32[4,16,1024]{2,1,0:T(8,128)S(1)}, f32[4,16,1024]{2,1,0:T(8,128)S(1)}, u32[]{:S(2)}, u32[]{:S(2)}) collective-permute-start(f32[4,16,1024]{2,1,0:T(8,128)S(1)} %joined.4.a_ref), channel_id=1, source_target_pairs={{0,14},{1,15},{2,0},{3,1},{4,2},{5,3},{6,4},{7,5},{8,6},{9,7},{10,... | collective-permute-start | bytes 786440 | tf_op jit(solution)/shard_map/ppermute | solution.py:431
  38.7 53.5 %all-to-all-start = ((f32[8,128,512]{2,1,0:T(8,128)}), f32[8,128,512]{2,1,0:T(8,128)S(1)}, u32[]{:S(2)}, u32[]{:S(2)}) async-start(f32[8,128,512]{2,1,0:T(8,128)} %ordered.1), calls=%async_computation | async-start | bytes 4194304 | tf_op jit(solution)/shard_map/all_to_all | solution.py:398
  44.4 24.3 %copy-start.10 = (s32[5]{0:T(128)S(1)}, s32[5]{0:T(128)}, u32[]{:S(2)}) copy-start(s32[5]{0:T(128)} %stack.23.refs_0_.at_ref) | copy-start | bytes 64
  44.4 23.6 %collective-permute-start.7 = (f32[8,16,1024]{2,1,0:T(8,128)S(1)}, f32[8,16,1024]{2,1,0:T(8,128)S(1)}, u32[]{:S(2)}, u32[]{:S(2)}) collective-permute-start(f32[8,16,1024]{2,1,0:T(8,128)S(1)} %joined.5.refs_0_), channel_id=1, source_target_pairs={{0,16},{16,32},{32,48},{48,0},{64,80},{80,96},{96,112},{112,64},{1... | collective-permute-start | bytes 1572872 | tf_op jit(solution)/shard_map/ppermute | solution.py:434
  44.5 23.5 %collective-permute-start.6 = (f32[8,16,1024]{2,1,0:T(8,128)S(1)}, f32[8,16,1024]{2,1,0:T(8,128)S(1)}, u32[]{:S(2)}, u32[]{:S(2)}) collective-permute-start(f32[8,16,1024]{2,1,0:T(8,128)S(1)} %joined.5.refs_0_), channel_id=1, source_target_pairs={{0,32},{16,48},{32,0},{48,16},{64,96},{80,112},{96,64},{112,80},{1... | collective-permute-start | bytes 1572872 | tf_op jit(solution)/shard_map/ppermute | solution.py:434
  45.5 23.2 %collective-permute-start.5 = (f32[8,16,1024]{2,1,0:T(8,128)S(1)}, f32[8,16,1024]{2,1,0:T(8,128)S(1)}, u32[]{:S(2)}, u32[]{:S(2)}) collective-permute-start(f32[8,16,1024]{2,1,0:T(8,128)S(1)} %joined.5.refs_0_), channel_id=1, source_target_pairs={{0,48},{16,0},{32,16},{48,32},{64,112},{80,64},{96,80},{112,96},{1... | collective-permute-start | bytes 1572872 | tf_op jit(solution)/shard_map/ppermute | solution.py:434
  69.5 1.0 copy-start.6
  71.2 1.0 copy-start.2
  92.2 2.8 %copy-start.3 = (bf16[8,64,1024]{2,1,0:T(8,128)(2,1)S(1)}, bf16[8,64,1024]{2,1,0:T(8,128)(2,1)}, u32[]{:S(2)}) copy-start(bf16[8,64,1024]{2,1,0:T(8,128)(2,1)} %copy-done.2) | copy-start | bytes 3145732
  92.2 2.8 %copy-start.7 = (bf16[8,64,1024]{2,1,0:T(8,128)(2,1)S(1)}, bf16[8,64,1024]{2,1,0:T(8,128)(2,1)}, u32[]{:S(2)}) copy-start(bf16[8,64,1024]{2,1,0:T(8,128)(2,1)} %copy-done.6) | copy-start | bytes 3145732
  92.2 2.7 %collective-permute-start.8 = (f32[8,64,512]{2,1,0:T(8,128)S(1)}, f32[8,64,512]{2,1,0:T(8,128)S(1)}, u32[]{:S(2)}, u32[]{:S(2)}) collective-permute-start(f32[8,64,512]{2,1,0:T(8,128)S(1)} %first_rows.1), channel_id=1, source_target_pairs={{0,1},{1,0},{2,3},{3,2},{4,5},{5,4},{6,7},{7,6},{8,9},{9,8},{10,11... | collective-permute-start | bytes 3145736 | tf_op jit(solution)/shard_map/ppermute | solution.py:439
  97.7 19.4 %copy-start.5 = (bf16[4,4,256,128]{3,2,1,0:T(8,128)(2,1)S(1)}, bf16[4,4,256,128]{3,2,1,0:T(8,128)(2,1)}, u32[]{:S(2)}) copy-start(bf16[4,4,256,128]{3,2,1,0:T(8,128)(2,1)} %weights_of.1.weights_ref) | copy-start | bytes 3145732
  97.7 19.3 %copy-start.11 = (s32[32,4]{0,1:T(4,128)S(1)}, s32[32,4]{0,1:T(4,128)}, u32[]{:S(2)}) copy-start(s32[32,4]{0,1:T(4,128)} %param.9) | copy-start | bytes 1540
  97.8 16.0 %collective-permute-start.10 = (f32[8,64,256]{2,1,0:T(8,128)S(1)}, f32[8,64,256]{2,1,0:T(8,128)S(1)}, u32[]{:S(2)}, u32[]{:S(2)}) collective-permute-start(f32[8,64,256]{2,1,0:T(8,128)S(1)} %get-tuple-element.10), channel_id=1, source_target_pairs={{2,0},{3,1},{4,2},{5,3},{6,4},{7,5},{8,6},{9,7},{10,8},{11,9},{12,... | collective-permute-start | bytes 1572872 | tf_op jit(solution)/shard_map/ppermute | solution.py:451
  101.3 22.5 %copy-start.4 = (bf16[8,64,1024]{2,1,0:T(8,128)(2,1)S(1)}, bf16[8,64,1024]{2,1,0:T(8,128)(2,1)}, u32[]{:S(2)}) copy-start(bf16[8,64,1024]{2,1,0:T(8,128)(2,1)} %copy-done.2) | copy-start | bytes 3145732
  101.3 15.7 %collective-permute-start.9 = (f32[8,64,256]{2,1,0:T(8,128)S(1)}, f32[8,64,256]{2,1,0:T(8,128)S(1)}, u32[]{:S(2)}, u32[]{:S(2)}) collective-permute-start(f32[8,64,256]{2,1,0:T(8,128)S(1)} %get-tuple-element.11), channel_id=1, source_target_pairs={{0,2},{1,3},{2,4},{3,5},{4,6},{5,7},{6,8},{7,9},{8,10},{9,11},{10,... | collective-permute-start | bytes 1572872 | tf_op jit(solution)/shard_map/ppermute | solution.py:450
  120.9 2.9 %collective-permute-start.11 = (f32[8,64,512]{2,1,0:T(8,128)}, f32[8,64,512]{2,1,0:T(8,128)S(1)}, u32[]{:S(2)}, u32[]{:S(2)}) collective-permute-start(f32[8,64,512]{2,1,0:T(8,128)} %space_mixed.1.own_ref), channel_id=1, source_target_pairs={{0,1},{1,0},{2,3},{3,2},{4,5},{5,4},{6,7},{7,6},{8,9},{9,8},{10,11... | collective-permute-start | bytes 3145736 | tf_op jit(solution)/shard_map/ppermute | solution.py:453
  123.8 1.2 copy-start.8
  130.5 1.3 copy-start.9
  131.8 62.3 %copy-start.1 = (f32[64,4096]{1,0:T(8,128)S(1)}, f32[64,4096]{1,0:T(8,128)}, u32[]{:S(2)}) copy-start(f32[64,4096]{1,0:T(8,128)} %start_ref.1) | copy-start | bytes 3145732
  131.8 62.3 %all-to-all-start.1 = ((f32[8,128,512]{2,1,0:T(8,128)}), f32[8,128,512]{2,1,0:T(8,128)S(1)}, u32[]{:S(2)}, u32[]{:S(2)}) async-start(f32[8,128,512]{2,1,0:T(8,128)} %copy-done.9), calls=%async_computation.1 | async-start | bytes 4194304 | tf_op jit(solution)/shard_map/all_to_all | solution.py:398
  140.0 1.2 collective-permute-start.12
  141.2 5.2 %collective-permute-start.13 = (f32[16,128]{1,0:T(8,128)S(1)}, f32[16,128]{1,0:T(8,128)S(1)}, u32[]{:S(2)}, u32[]{:S(2)}) collective-permute-start(f32[16,128]{1,0:T(8,128)S(1)} %add.39), channel_id=1, source_target_pairs={{0,32},{16,48},{32,0},{48,16},{64,96},{80,112},{96,64},{112,80},{1... | collective-permute-start | bytes 24584 | tf_op jit(solution)/shard_map/ppermute | solution.py:460
  146.3 4.9 %collective-permute-start.14 = (f32[16,128]{1,0:T(8,128)S(1)}, f32[16,128]{1,0:T(8,128)S(1)}, u32[]{:S(2)}, u32[]{:S(2)}) collective-permute-start(f32[16,128]{1,0:T(8,128)S(1)} %add.40), channel_id=1, source_target_pairs={{0,16},{16,32},{32,48},{48,0},{64,80},{80,96},{96,112},{112,64},{1... | collective-permute-start | bytes 24584 | tf_op jit(solution)/shard_map/ppermute | solution.py:460
  151.2 5.2 %collective-permute-start.15 = (f32[16,128]{1,0:T(8,128)S(1)}, f32[16,128]{1,0:T(8,128)S(1)}, u32[]{:S(2)}, u32[]{:S(2)}) collective-permute-start(f32[16,128]{1,0:T(8,128)S(1)} %add.41), channel_id=1, source_target_pairs={{0,128},{16,144},{32,160},{48,176},{64,192},{80,208},{96,224},{112... | collective-permute-start | bytes 24584 | tf_op jit(solution)/shard_map/ppermute | solution.py:460
  156.4 3.7 %collective-permute-start.16 = (f32[16,128]{1,0:T(8,128)S(1)}, f32[16,128]{1,0:T(8,128)S(1)}, u32[]{:S(2)}, u32[]{:S(2)}) collective-permute-start(f32[16,128]{1,0:T(8,128)S(1)} %add.42), channel_id=1, source_target_pairs={{0,64},{16,80},{32,96},{48,112},{64,128},{80,144},{96,160},{112,17... | collective-permute-start | bytes 24584 | tf_op jit(solution)/shard_map/ppermute | solution.py:460
  160.0 26.5 %collective-permute-start.23 = (f32[16,128]{1,0:T(8,128)S(1)}, f32[16,128]{1,0:T(8,128)S(1)}, u32[]{:S(2)}, u32[]{:S(2)}) collective-permute-start(f32[16,128]{1,0:T(8,128)S(1)} %add.43.refs_0_), channel_id=1, source_target_pairs={{0,14},{1,15},{2,0},{3,1},{4,2},{5,3},{6,4},{7,5},{8,6},{9,7},{10,... | collective-permute-start | bytes 24584 | tf_op jit(solution)/shard_map/ppermute | solution.py:461
  160.2 30.3 %collective-permute-start.22 = (f32[16,128]{1,0:T(8,128)S(1)}, f32[16,128]{1,0:T(8,128)S(1)}, u32[]{:S(2)}, u32[]{:S(2)}) collective-permute-start(f32[16,128]{1,0:T(8,128)S(1)} %add.43.refs_0_), channel_id=1, source_target_pairs={{0,12},{1,13},{2,14},{3,15},{4,0},{5,1},{6,2},{7,3},{8,4},{9,5},{1... | collective-permute-start | bytes 24584 | tf_op jit(solution)/shard_map/ppermute | solution.py:461
  164.2 28.4 %collective-permute-start.21 = (f32[16,128]{1,0:T(8,128)S(1)}, f32[16,128]{1,0:T(8,128)S(1)}, u32[]{:S(2)}, u32[]{:S(2)}) collective-permute-start(f32[16,128]{1,0:T(8,128)S(1)} %add.43.refs_0_), channel_id=1, source_target_pairs={{0,10},{1,11},{2,12},{3,13},{4,14},{5,15},{6,0},{7,1},{8,2},{9,3},... | collective-permute-start | bytes 24584 | tf_op jit(solution)/shard_map/ppermute | solution.py:461
  166.5 26.1 %collective-permute-start.20 = (f32[16,128]{1,0:T(8,128)S(1)}, f32[16,128]{1,0:T(8,128)S(1)}, u32[]{:S(2)}, u32[]{:S(2)}) collective-permute-start(f32[16,128]{1,0:T(8,128)S(1)} %add.43.refs_0_), channel_id=1, source_target_pairs={{0,8},{1,9},{2,10},{3,11},{4,12},{5,13},{6,14},{7,15},{8,0},{9,1},... | collective-permute-start | bytes 24584 | tf_op jit(solution)/shard_map/ppermute | solution.py:461
  169.2 23.4 %collective-permute-start.19 = (f32[16,128]{1,0:T(8,128)S(1)}, f32[16,128]{1,0:T(8,128)S(1)}, u32[]{:S(2)}, u32[]{:S(2)}) collective-permute-start(f32[16,128]{1,0:T(8,128)S(1)} %add.43.refs_0_), channel_id=1, source_target_pairs={{0,6},{1,7},{2,8},{3,9},{4,10},{5,11},{6,12},{7,13},{8,14},{9,15},... | collective-permute-start | bytes 24584 | tf_op jit(solution)/shard_map/ppermute | solution.py:461
  186.5 6.1 %collective-permute-start.18 = (f32[16,128]{1,0:T(8,128)S(1)}, f32[16,128]{1,0:T(8,128)S(1)}, u32[]{:S(2)}, u32[]{:S(2)}) collective-permute-start(f32[16,128]{1,0:T(8,128)S(1)} %add.43.refs_0_), channel_id=1, source_target_pairs={{0,4},{1,5},{2,6},{3,7},{4,8},{5,9},{6,10},{7,11},{8,12},{9,13},{1... | collective-permute-start | bytes 24584 | tf_op jit(solution)/shard_map/ppermute | solution.py:461
  190.5 3.7 %collective-permute-start.17 = (f32[16,128]{1,0:T(8,128)S(1)}, f32[16,128]{1,0:T(8,128)S(1)}, u32[]{:S(2)}, u32[]{:S(2)}) collective-permute-start(f32[16,128]{1,0:T(8,128)S(1)} %add.43.refs_0_), channel_id=1, source_target_pairs={{0,2},{1,3},{2,4},{3,5},{4,6},{5,7},{6,8},{7,9},{8,10},{9,11},{10,... | collective-permute-start | bytes 24584 | tf_op jit(solution)/shard_map/ppermute | solution.py:461

commit v2 on v1

--- a/solution.py
+++ b/solution.py
@@ -29,6 +29,10 @@
     return high, (value - high.astype(F32)).astype(BF16)
 
 
+def turned(at, index):
+    return jnp.where(at[6] == 1, CHIPS - 1 - index, index)
+
+
 def params(megabytes):
     return pltpu.CompilerParams(vmem_limit_bytes=megabytes * 1024 * 1024)
 
@@ -62,7 +66,7 @@
         grid_spec=pltpu.PrefetchScalarGridSpec(
             num_scalar_prefetch=1,
             grid=(rows,),
-            in_specs=[pl.BlockSpec((1, nb, TILE, TILE), lambda i, at: (at[0] * rows + i, 0, 0, 0))],
+            in_specs=[pl.BlockSpec((1, nb, TILE, TILE), lambda i, at: (at[5] * rows + i, 0, 0, 0))],
             out_specs=pl.BlockSpec((1, nb, 2 * TILE, TILE), lambda i, at: (i, 0, 0, 0)),
         ),
         out_shape=jax.ShapeDtypeStruct((rows, nb, 2 * TILE, TILE), BF16),
@@ -119,7 +123,7 @@
             stage_ref[k, :hours, columns] = product[:hours, :TILE] + (product[:hours, TILE:] + product[hours:, :TILE])
         right[k].wait()
         stage_ref[k, hours:, :] = right_here[k] - noise_ref[:, place(first + k)] * x_here[:, place(first + k)]
-        sent.append(pltpu.make_async_copy(stage_ref.at[k], out_ref.at[first + k], out_sems.at[k]))
+        sent.append(pltpu.make_async_copy(stage_ref.at[k], out_ref.at[turned(at_ref, first + k)], out_sems.at[k]))
         sent[-1].start()
     for copy in sent:
         copy.wait()
@@ -170,7 +174,7 @@
     for row in range(rows):
         total = None
         for n in range(nb):
-            i = ids_ref[n, at_ref[0] * rows + row] - at_ref[2]
+            i = ids_ref[n, at_ref[5] * rows + row] - at_ref[2]
             both = dot_nt(hi_ref[i], weights_ref[row, n])
             part = both[:, :TILE] + (both[:, TILE:] + dot_nt(lo_ref[i], weights_ref[row, n, :TILE]))
             total = part if total is None else total + part
@@ -198,7 +202,7 @@
         ),
         out_shape=jax.ShapeDtypeStruct(own.shape, F32),
         compiler_params=params(24),
-        cost_estimate=cost(0, 0),
+        cost_estimate=cost(4000000000, 0),
         name="space_mixed",
     )(at, ids, left, own, right, weights, *after)
 
@@ -272,25 +276,18 @@
     )(at, khi, klo, got, other)
 
 
-def image_kernel(at_ref, khi_ref, klo_ref, own_ref, other_ref, r_ref, noise_ref, out_ref, sums_ref, uhi_ref, ulo_ref, image_ref, sems):
+def image_kernel(at_ref, khi_ref, klo_ref, own_ref, other_ref, r_ref, noise_ref, out_ref, sums_ref, uhi_ref, ulo_ref):
     chips, hours, sites = own_ref.shape
+    split_hours(at_ref, own_ref, other_ref, uhi_ref, ulo_ref)
     width = sites // 2
-    places = [slice(part * width, (part + 1) * width) for part in range(2)]
-    copies = [
-        pltpu.make_async_copy(image_ref.at[:, :, place], out_ref.at[:, pl.ds(0, hours), place], sems.at[part])
-        for part, place in enumerate(places)
-    ]
-    kept = pltpu.make_async_copy(r_ref, out_ref.at[:, pl.ds(hours, hours)], sems.at[2])
-    kept.start()
-    split_hours(at_ref, own_ref, other_ref, uhi_ref, ulo_ref)
     squares = jnp.zeros((8, TILE), F32)
     curves = jnp.zeros((8, TILE), F32)
-    for copy, columns in zip(copies, places):
+    for part in range(2):
+        columns = slice(part * width, (part + 1) * width)
         mixed = time_product(khi_ref, klo_ref, uhi_ref, ulo_ref, columns)
         r = r_ref[:, :, columns]
         image = mixed + noise_ref[:, columns][None] * r
-        image_ref[:, :, columns] = image
-        copy.start()
+        out_ref[:, :, columns] = image
         for t in range(width // TILE):
             piece = slice(t * TILE, (t + 1) * TILE)
             a, b = r[:, :, piece].reshape(-1, 8, TILE), image[:, :, piece].reshape(-1, 8, TILE)
@@ -298,8 +295,6 @@
             curves += jnp.sum(a * b, axis=0)
     sums_ref[:8, :] = squares
     sums_ref[8:, :] = curves
-    for copy in copies + [kept]:
-        copy.wait()
 
 
 def image_of(at, khi, klo, own, other, residual, noise):
@@ -307,42 +302,41 @@
     return pl.pallas_call(
         image_kernel,
         in_specs=[SMEM] + [VMEM] * 6,
-        out_specs=[ANY, VMEM],
-        out_shape=[jax.ShapeDtypeStruct((chips, 2 * hours, sites), F32), jax.ShapeDtypeStruct((16, TILE), F32)],
-        scratch_shapes=[pltpu.VMEM((2 * chips * hours, sites), BF16)] * 2
-        + [pltpu.VMEM(own.shape, F32), pltpu.SemaphoreType.DMA((3,))],
+        out_specs=[VMEM] * 2,
+        out_shape=[jax.ShapeDtypeStruct(own.shape, F32), jax.ShapeDtypeStruct((16, TILE), F32)],
+        scratch_shapes=[pltpu.VMEM((2 * chips * hours, sites), BF16)] * 2,
         compiler_params=params(24),
         cost_estimate=cost(0, 0),
         name="image_of",
     )(at, khi, klo, own, other, residual, noise)
 
 
-def update_kernel(start_ref, got_ref, *refs):
+def update_kernel(at_ref, start_ref, residual_ref, image_ref, *refs):
     sums, (iterate_ref, next_ref) = refs[:-2], refs[-2:]
-    chips, _, width = got_ref.shape
-    hours = start_ref.shape[0]
+    chips, _, width = residual_ref.shape
     total = sums[0][...]
     for part in sums[1:]:
         total += part[...]
     alpha = jnp.sum(total[:8, :]) / jnp.sum(total[8:, :])
     for g in range(chips):
         columns = slice(g * width, (g + 1) * width)
-        r = got_ref[g, hours:, :]
+        chip = turned(at_ref, g)
+        r = residual_ref[chip]
         iterate_ref[:, columns] = start_ref[:, columns] + alpha * r
-        next_ref[:, columns] = r - alpha * got_ref[g, :hours, :]
-
-
-def update(start, got, sums):
+        next_ref[:, columns] = r - alpha * image_ref[chip]
+
+
+def update(at, start, residual, image, sums):
     shape = jax.ShapeDtypeStruct(start.shape, F32)
     return pl.pallas_call(
         update_kernel,
-        in_specs=[VMEM] * (2 + len(sums)),
+        in_specs=[SMEM] + [VMEM] * (3 + len(sums)),
         out_specs=(VMEM, VMEM),
         out_shape=(shape, shape),
         compiler_params=params(24),
         cost_estimate=cost(0, 0),
         name="update",
-    )(start, got, *sums)
+    )(at, start, residual, image, *sums)
 
 
 def first_rows_kernel(value_ref, *refs):
@@ -388,6 +382,25 @@
         cost_estimate=cost(0, 0),
         name="joined",
     )(a, b, *after)
+
+
+def copied_kernel(value_ref, out_ref, sem):
+    copy = pltpu.make_async_copy(value_ref, out_ref, sem)
+    copy.start()
+    copy.wait()
+
+
+def copied(value):
+    return pl.pallas_call(
+        copied_kernel,
+        in_specs=[VMEM],
+        out_specs=ANY,
+        out_shape=jax.ShapeDtypeStruct(value.shape, value.dtype),
+        scratch_shapes=[pltpu.SemaphoreType.DMA],
+        compiler_params=params(16),
+        cost_estimate=cost(0, 0),
+        name="copied",
+    )(value)
 
 
 def token(value):
@@ -414,7 +427,9 @@
     space, tm = lax.axis_index("space"), lax.axis_index("tm")
     chip, core = tm // 2, tm % 2
     base = space * count - REACH
-    at = jnp.stack([chip, core, base + chip * (count // CHIPS), base, space % SIDE]).astype(jnp.int32)
+    flip = space % 2
+    group = jnp.where(flip == 1, CHIPS - 1 - chip, chip)
+    at = jnp.stack([chip, core, base + group * (count // CHIPS), base, space % SIDE, group, flip]).astype(jnp.int32)
 
     forward = [(i, i + 1) for i in range(spaces - 1)]
     backward = [(target, source) for source, target in forward]
@@ -440,26 +455,25 @@
     residual = residual_of(at, khi, klo, got, other)
 
     up, down = [], []
-    for s in range(spaces):
-        for z in range(CHIPS):
-            for c in range(2):
-                source, target = (s * CHIPS + z), (s * CHIPS + z + 1)
-                if target < spaces * CHIPS:
-                    up.append((source * 2 + c, target * 2 + c))
-                    down.append((target * 2 + c, source * 2 + c))
+    line = [s * CHIPS + (CHIPS - 1 - g if s % 2 else g) for s in range(spaces) for g in range(CHIPS)]
+    for source, target in zip(line, line[1:]):
+        for c in range(2):
+            up.append((source * 2 + c, target * 2 + c))
+            down.append((target * 2 + c, source * 2 + c))
     left = lax.ppermute(residual[:, :, width - edge :], ("space", "tm"), up)
     right = lax.ppermute(residual[:, :, :edge], ("space", "tm"), down)
+    back_r = exchange(copied(residual))
     mixed = space_mixed(at, ids, left, residual, right, weights, [])
     other = lax.ppermute(mixed, "tm", SWAP)
-    noise_here = lax.dynamic_slice(noise, (chip * width,), (width,))[None, :]
+    noise_here = lax.dynamic_slice(noise, (group * width,), (width,))[None, :]
     image, sums = image_of(at, khi, klo, mixed, other, residual, noise_here)
-    back = exchange(image)
     sums = sums + lax.ppermute(sums, "tm", SWAP)
+    sums = sums + lax.ppermute(sums, "tm", along_z(CHIPS // 2))
+    back_p = exchange(ordered(image, sums))
     for axis in ("y", "x"):
-        for shift in (2, 1):
-            sums = sums + lax.ppermute(sums, "space", along_side(shift, axis))
-    sums = [sums] + [lax.ppermute(sums, "tm", along_z(shift)) for shift in range(1, CHIPS)]
-    return update(start, back, sums)
+        sums = sum([lax.ppermute(sums, "space", along_side(shift, axis)) for shift in range(1, SIDE)], sums)
+    sums = [sums] + [lax.ppermute(sums, "tm", along_z(shift)) for shift in range(1, CHIPS // 2)]
+    return update(at, start, back_r, back_p, sums)
 
 
 def solution(mesh):

time: 197 us -> 185 us (0.939)
  waiting for transfers between devices: 95.7 us -> 81.7 us
    ppermute x7 -> x3, starting transfers between devices: 17.6 us -> 5.3 us  [local(): lax.ppermute(sums, 'tm', along_z(shift))]
    ppermute x7 -> x3, waiting for transfers between devices: 16.5 us -> 7.13 us  [local(): lax.ppermute(sums, 'tm', along_z(shift))]
    ppermute x1, waiting for transfers between devices: 3.24 us -> 11.5 us  [local(): left = lax.ppermute(residual[:, :, width - edge:], ('space', 'tm'), up)]
    ppermute x1, waiting for transfers between devices: 5.68 us -> 0.01 us  [local(): low = lax.ppermute(start[:, sites_dev - edge:], 'space', forward)]
    ppermute x4 -> x7, starting transfers between devices: 1.12 us -> 6.7 us  [the longest x6 6.7 us: local(): lax.ppermute(sums, 'space', along_side(shift, axis))]
    ppermute x1, waiting for transfers between devices: 9.67 us -> 4.48 us  [local(): right = lax.ppermute(residual[:, :, :edge], ('space', 'tm'), down)]
    all_to_all x2 -> x3, starting transfers between devices: 13.9 us -> 18.4 us  [exchange(): lax.all_to_all(blocks, 'tm', 0, 0, axis_index_groups=SAME_CORE, tiled=True)]
    ppermute x4 -> x7, waiting for transfers between devices: 17.7 us -> 14.5 us  [the longest x1 7.56 us: local(): sums = sums + lax.ppermute(sums, 'tm', along_z(CHIPS // 2))]
  transfers between devices with their start and end apart: 26 -> 26, of which waited for: 15 -> 21; matrix products, arithmetic and copies ran while one was open for 2% -> 2% of each run, Pallas kernels for 9% -> 15%
where the time goes in v2:
time: 185 us; the launch traced here: 184 us
  waiting for transfers between devices  81.7 us (44%)
  starting transfers between devices  57.1 us (31%)
  Pallas kernels  33 us (18%)
  local copies, waits for them, and re-layouts  10.2 us (6%)
    all_to_all x3, waiting for transfers between devices, exchange(): lax.all_to_all(blocks, 'tm', 0, 0, axis_index_groups=SAME_CORE, tiled=True)  19.8 us
    all_to_all x3, starting transfers between devices, exchange(): lax.all_to_all(blocks, 'tm', 0, 0, axis_index_groups=SAME_CORE, tiled=True)  18.4 us
    ppermute x3, waiting for transfers between devices, local(): lax.ppermute(strip, 'space', along_side(-k, 'y'))  16.5 us
    pallas_call x2, Pallas kernels, space_wide(): pl.pallas_call(lambda *refs: space_wide_kernel(first, *refs), in_specs=[S...  12.6 us
    ppermute x1, waiting for transfers between devices, local(): left = lax.ppermute(residual[:, :, width - edge:], ('space', 'tm'), up)  11.5 us
    ppermute x1, waiting for transfers between devices, local(): sums = sums + lax.ppermute(sums, 'tm', along_z(CHIPS // 2))  7.56 us
    ppermute x3, waiting for transfers between devices, local(): lax.ppermute(sums, 'tm', along_z(shift))  7.13 us
    ppermute x6, waiting for transfers between devices, local(): lax.ppermute(sums, 'space', along_side(shift, axis))  6.95 us
  transfers between devices with their start and end apart: 26, of which 21 were waited for; matrix products, arithmetic and copies ran while one was open for 2% of the time, Pallas kernels for 15%

profile of v2, /device:TPU:38, one launch (start us, length us, event | category | flops | bytes accessed | tf_op | source)
XLA Modules:
  0.0 183.6 jit_solution(12627838254862631605)
XLA Ops:
  0.6 0.9 fusion.1
  1.6 3.5 %collective-permute-start.1 = (f32[64,256]{1,0:T(8,128)S(1)}, f32[64,256]{1,0:T(8,128)S(1)}, u32[]{:S(2)}, u32[]{:S(2)}) collective-permute-start(f32[64,256]{1,0:T(8,128)S(1)} %get-tuple-element.13), channel_id=1, source_target_pairs={{0,16},{16,32},{32,48},{48,64},{64,80},{80,96},{96,112},{112,128},... | collective-permute-start | bytes 196616 | tf_op jit(solution)/shard_map/ppermute | solution.py:436
  5.1 4.5 %collective-permute-start.2 = (f32[64,256]{1,0:T(8,128)S(1)}, f32[64,256]{1,0:T(8,128)S(1)}, u32[]{:S(2)}, u32[]{:S(2)}) collective-permute-start(f32[64,256]{1,0:T(8,128)S(1)} %get-tuple-element.12), channel_id=1, source_target_pairs={{16,0},{32,16},{48,32},{64,48},{80,64},{96,80},{112,96},{128,112},... | collective-permute-start | bytes 196616 | tf_op jit(solution)/shard_map/ppermute | solution.py:437
  9.6 6.4 %collective-permute-start = (f32[1,16,1024]{2,1,0:T(8,128)S(1)}, f32[1,16,1024]{2,1,0:T(8,128)S(1)}, u32[]{:S(2)}, u32[]{:S(2)}) collective-permute-start(f32[1,16,1024]{2,1,0:T(8,128)S(1)} %dynamic-slice_bitcast_fusion.a_ref), channel_id=1, source_target_pairs={{0,8},{1,9},{2,10},{3,11},{4,12},{5,13},{6,14},{7,15},{8,0},{9,1},... | collective-permute-start | bytes 196616 | tf_op jit(solution)/shard_map/ppermute | solution.py:441
  16.6 1.7 collective-permute-done.b_ref
  18.3 2.9 %collective-permute-start.3 = (f32[2,16,1024]{2,1,0:T(8,128)S(1)}, f32[2,16,1024]{2,1,0:T(8,128)S(1)}, u32[]{:S(2)}, u32[]{:S(2)}) collective-permute-start(f32[2,16,1024]{2,1,0:T(8,128)S(1)} %joined.3.a_ref), channel_id=1, source_target_pairs={{0,4},{1,5},{2,6},{3,7},{4,8},{5,9},{6,10},{7,11},{8,12},{9,13},{1... | collective-permute-start | bytes 393224 | tf_op jit(solution)/shard_map/ppermute | solution.py:443
  21.2 6.3 %space_wide.2.refs_7_ = f32[8,128,512]{2,1,0:T(8,128)} custom-call(s32[7]{0:T(128)} %stack.31.refs_0_.at_ref, s32[4,32]{1,0:T(4,128)} %bitcast.31, f32[64,256]{1,0:T(8,128)} %copy-done.13, f32[1,4096]{1,0:T(1,128)} %bitcast.36, f32[64,4096]{1,0:T(8,128)} %start_ref.1, f32[32,4,128,128]{3,2,1,0:T(8,128)} %tiles_ref.1, f32[64,4096]{1,0:T(8,128)} %refs_6_.3), custom_call_target="tpu_custom_call" | custom-call | tf_op jit(solution)/shard_map/space_wide/pallas_call | solution.py:137
  28.4 0.9 collective-permute-start.4
  29.8 6.3 %space_wide.3.refs_0_ = f32[8,128,512]{2,1,0:T(8,128)} custom-call(s32[7]{0:T(128)} %stack.31.refs_0_.at_ref, s32[4,32]{1,0:T(4,128)} %bitcast.32, f32[64,256]{1,0:T(8,128)} %copy-done.12, f32[1,4096]{1,0:T(1,128)} %bitcast.37, f32[64,4096]{1,0:T(8,128)} %start_ref.1, f32[32,4,128,128]{3,2,1,0:T(8,128)} %tiles_ref.1, ...), custom_call_target="tpu_custom_call", output_to_operand_aliasing={{}: (7, {})} | custom-call | tf_op jit(solution)/shard_map/space_wide/pallas_call | solution.py:137
  36.8 9.1 %all-to-all-start = ((f32[8,128,512]{2,1,0:T(8,128)}), f32[8,128,512]{2,1,0:T(8,128)S(1)}, u32[]{:S(2)}, u32[]{:S(2)}) async-start(f32[8,128,512]{2,1,0:T(8,128)} %ordered.2), calls=%async_computation | async-start | bytes 4194304 | tf_op jit(solution)/shard_map/all_to_all | solution.py:411
  46.0 1.0 collective-permute-start.5
  47.6 1.0 collective-permute-start.7
  48.5 4.1 %weights_of.1.weights_ref = bf16[4,4,256,128]{3,2,1,0:T(8,128)(2,1)} custom-call(s32[7]{0:T(128)} %stack.31.refs_0_.at_ref, f32[32,4,128,128]{3,2,1,0:T(8,128)} %tiles_ref.1), custom_call_target="tpu_custom_call" | custom-call | tf_op jit(solution)/shard_map/weights_of/pallas_call | solution.py:64
  52.6 8.3 %collective-permute-done.5.refs_1_ = f32[8,16,1024]{2,1,0:T(8,128)S(1)} collective-permute-done((f32[8,16,1024]{2,1,0:T(8,128)S(1)}, f32[8,16,1024]{2,1,0:T(8,128)S(1)}, u32[]{:S(2)}, u32[]{:S(2)}) %collective-permute-start.5) | collective-permute-done | bytes 524320 | tf_op jit(solution)/shard_map/ppermute | solution.py:449
  60.9 2.4 %collective-permute-done.6.refs_2_ = f32[8,16,1024]{2,1,0:T(8,128)S(1)} collective-permute-done((f32[8,16,1024]{2,1,0:T(8,128)S(1)}, f32[8,16,1024]{2,1,0:T(8,128)S(1)}, u32[]{:S(2)}, u32[]{:S(2)}) %collective-permute-start.6) | collective-permute-done | bytes 524320 | tf_op jit(solution)/shard_map/ppermute | solution.py:449
  63.3 5.9 %collective-permute-done.7.refs_3_ = f32[8,16,1024]{2,1,0:T(8,128)S(1)} collective-permute-done((f32[8,16,1024]{2,1,0:T(8,128)S(1)}, f32[8,16,1024]{2,1,0:T(8,128)S(1)}, u32[]{:S(2)}, u32[]{:S(2)}) %collective-permute-start.7) | collective-permute-done | bytes 524320 | tf_op jit(solution)/shard_map/ppermute | solution.py:449
  69.2 0.8 time_rows.1
  70.0 1.0 copy-done.5
  71.6 1.0 copy-done.2
  72.6 19.7 %all-to-all-done.value_ref.got_ref = f32[8,128,512]{2,1,0:T(8,128)S(1)} async-done(((f32[8,128,512]{2,1,0:T(8,128)}), f32[8,128,512]{2,1,0:T(8,128)S(1)}, u32[]{:S(2)}, u32[]{:S(2)}) %all-to-all-start) | async-done | bytes 2097184 | tf_op jit(solution)/shard_map/all_to_all | solution.py:411
  92.5 2.6 %collective-permute-done.8.other_ref = f32[8,64,512]{2,1,0:T(8,128)S(1)} collective-permute-done((f32[8,64,512]{2,1,0:T(8,128)S(1)}, f32[8,64,512]{2,1,0:T(8,128)S(1)}, u32[]{:S(2)}, u32[]{:S(2)}) %collective-permute-start.8) | collective-permute-done | bytes 1048608 | tf_op jit(solution)/shard_map/ppermute | solution.py:454
  95.1 2.7 %residual_of.1.value_ref.own_ref.r_ref = f32[8,64,512]{2,1,0:T(8,128)S(1)} custom-call(s32[7]{0:T(128)S(1)} %copy-done.10, bf16[8,64,1024]{2,1,0:T(8,128)(2,1)S(1)} %copy-done.3, bf16[8,64,1024]{2,1,0:T(8,128)(2,1)S(1)} %copy-done.6, f32[8,128,512]{2,1,0:T(8,128)S(1)} %all-to-all-done.value_ref.got_ref, f32[8,64,512]{2,1,0:T(8,128)S(1)} %collective-permute-done.8.other_ref), custom_call_target="tpu_custom_call" | custom-call | tf_op jit(solution)/shard_map/residual_of/pallas_call | solution.py:267
  97.8 1.1 fusion
  98.9 3.4 %collective-permute-start.10 = (f32[8,64,256]{2,1,0:T(8,128)}, f32[8,64,256]{2,1,0:T(8,128)}, u32[]{:S(2)}, u32[]{:S(2)}) collective-permute-start(f32[8,64,256]{2,1,0:T(8,128)} %get-tuple-element.10), channel_id=1, source_target_pairs={{2,0},{3,1},{4,2},{5,3},{6,4},{7,5},{8,6},{9,7},{10,8},{11,9},{12,... | collective-permute-start | bytes 1572872 | tf_op jit(solution)/shard_map/ppermute | solution.py:464
  102.3 2.5 %collective-permute-start.9 = (f32[8,64,256]{2,1,0:T(8,128)}, f32[8,64,256]{2,1,0:T(8,128)}, u32[]{:S(2)}, u32[]{:S(2)}) collective-permute-start(f32[8,64,256]{2,1,0:T(8,128)} %get-tuple-element.11), channel_id=1, source_target_pairs={{0,2},{1,3},{2,4},{3,5},{4,6},{5,7},{6,8},{7,9},{8,10},{9,11},{10,... | collective-permute-start | bytes 1572872 | tf_op jit(solution)/shard_map/ppermute | solution.py:463
  104.8 1.0 copied.1
  105.8 5.6 %all-to-all-start.1 = ((f32[8,64,512]{2,1,0:T(8,128)}), f32[8,64,512]{2,1,0:T(8,128)}, u32[]{:S(2)}, u32[]{:S(2)}) async-start(f32[8,64,512]{2,1,0:T(8,128)} %copied.1), calls=%async_computation.1 | async-start | bytes 2097152 | tf_op jit(solution)/shard_map/all_to_all | solution.py:411
  111.4 4.5 %collective-permute-done.10.right_ref = f32[8,64,256]{2,1,0:T(8,128)} collective-permute-done((f32[8,64,256]{2,1,0:T(8,128)}, f32[8,64,256]{2,1,0:T(8,128)}, u32[]{:S(2)}, u32[]{:S(2)}) %collective-permute-start.10) | collective-permute-done | bytes 524320 | tf_op jit(solution)/shard_map/ppermute | solution.py:464
  115.9 11.5 %collective-permute-done.9.left_ref = f32[8,64,256]{2,1,0:T(8,128)} collective-permute-done((f32[8,64,256]{2,1,0:T(8,128)}, f32[8,64,256]{2,1,0:T(8,128)}, u32[]{:S(2)}, u32[]{:S(2)}) %collective-permute-start.9) | collective-permute-done | bytes 524320 | tf_op jit(solution)/shard_map/ppermute | solution.py:463
  127.4 1.2 copy-done.9
  128.6 5.1 %space_mixed.1.own_ref = f32[8,64,512]{2,1,0:T(8,128)} custom-call(s32[7]{0:T(128)S(1)} %copy-done.10, s32[4,32]{1,0:T(4,128)S(1)} %bitcast.33, f32[8,64,256]{2,1,0:T(8,128)} %collective-permute-done.9.left_ref, f32[8,64,512]{2,1,0:T(8,128)S(1)} %residual_of.1.value_ref.own_ref.r_ref, f32[8,64,256]{2,1,0:T(8,128)} %collective-permute-done.10.right_ref, ...), custom_call_target="tpu_custom_call" | custom-call | flops 4000000000 | tf_op jit(solution)/shard_map/space_mixed/pallas_call | solution.py:188
  134.4 2.2 %collective-permute-done.11.other_ref = f32[8,64,512]{2,1,0:T(8,128)} collective-permute-done((f32[8,64,512]{2,1,0:T(8,128)}, f32[8,64,512]{2,1,0:T(8,128)}, u32[]{:S(2)}, u32[]{:S(2)}) %collective-permute-start.11) | collective-permute-done | bytes 1048608 | tf_op jit(solution)/shard_map/ppermute | solution.py:467
  136.7 3.7 %image_of.1 = (f32[8,64,512]{2,1,0:T(8,128)S(1)}, f32[16,128]{1,0:T(8,128)S(1)}) custom-call(s32[7]{0:T(128)S(1)} %copy-done.10, bf16[8,64,1024]{2,1,0:T(8,128)(2,1)S(1)} %copy-done.4, bf16[8,64,1024]{2,1,0:T(8,128)(2,1)S(1)} %copy-done.7, f32[8,64,512]{2,1,0:T(8,128)} %space_mixed.1.own_ref, f32[8,64,512]{2,1,0:T(8,128)} %collective-permute-done.11.other_ref, ...), custom_call_target="tpu_custom_call" | custom-call | tf_op jit(solution)/shard_map/image_of/pallas_call | solution.py:302
  140.4 1.0 copy-done.8
  141.5 1.0 collective-permute-done.12
  142.6 7.6 %collective-permute-done.13 = f32[16,128]{1,0:T(8,128)S(1)} collective-permute-done((f32[16,128]{1,0:T(8,128)S(1)}, f32[16,128]{1,0:T(8,128)S(1)}, u32[]{:S(2)}, u32[]{:S(2)}) %collective-permute-start.13) | collective-permute-done | bytes 8224 | tf_op jit(solution)/shard_map/ppermute | solution.py:471
  150.8 3.7 %all-to-all-start.2 = ((f32[8,64,512]{2,1,0:T(8,128)}), f32[8,64,512]{2,1,0:T(8,128)S(1)}, u32[]{:S(2)}, u32[]{:S(2)}) async-start(f32[8,64,512]{2,1,0:T(8,128)} %ordered.3), calls=%async_computation.2 | async-start | bytes 2097152 | tf_op jit(solution)/shard_map/all_to_all | solution.py:411
  154.5 1.2 collective-permute-start.15
  155.7 2.5 %collective-permute-start.16 = (f32[16,128]{1,0:T(8,128)S(1)}, f32[16,128]{1,0:T(8,128)S(1)}, u32[]{:S(2)}, u32[]{:S(2)}) collective-permute-start(f32[16,128]{1,0:T(8,128)S(1)} %copy-done.14), channel_id=1, source_target_pairs={{0,48},{16,0},{32,16},{48,32},{64,112},{80,64},{96,80},{112,96},{1... | collective-permute-start | bytes 24584 | tf_op jit(solution)/shard_map/ppermute | solution.py:474
  158.2 1.1 collective-permute-done.14
  160.3 2.9 %collective-permute-start.18 = (f32[16,128]{1,0:T(8,128)S(1)}, f32[16,128]{1,0:T(8,128)S(1)}, u32[]{:S(2)}, u32[]{:S(2)}) collective-permute-start(f32[16,128]{1,0:T(8,128)S(1)} %add_add_fusion.1), channel_id=1, source_target_pairs={{0,128},{16,144},{32,160},{48,176},{64,192},{80,208},{96,224},{112... | collective-permute-start | bytes 24584 | tf_op jit(solution)/shard_map/ppermute | solution.py:474
  164.0 1.6 collective-permute-done.18
  165.6 2.5 %collective-permute-done.19 = f32[16,128]{1,0:T(8,128)S(1)} collective-permute-done((f32[16,128]{1,0:T(8,128)S(1)}, f32[16,128]{1,0:T(8,128)S(1)}, u32[]{:S(2)}, u32[]{:S(2)}) %collective-permute-start.19) | collective-permute-done | bytes 8224 | tf_op jit(solution)/shard_map/ppermute | solution.py:474
  168.1 1.2 collective-permute-start.20
  169.3 3.6 %collective-permute-start.21 = (f32[16,128]{1,0:T(8,128)S(1)}, f32[16,128]{1,0:T(8,128)S(1)}, u32[]{:S(2)}, u32[]{:S(2)}) collective-permute-start(f32[16,128]{1,0:T(8,128)S(1)} %add_add_fusion.refs_0_), channel_id=1, source_target_pairs={{0,4},{1,5},{2,6},{3,7},{4,8},{5,9},{6,10},{7,11},{8,12},{9,13},{1... | collective-permute-start | bytes 24584 | tf_op jit(solution)/shard_map/ppermute | solution.py:475
  173.4 2.1 %collective-permute-done.20.refs_1_ = f32[16,128]{1,0:T(8,128)S(1)} collective-permute-done((f32[16,128]{1,0:T(8,128)S(1)}, f32[16,128]{1,0:T(8,128)S(1)}, u32[]{:S(2)}, u32[]{:S(2)}) %collective-permute-start.20) | collective-permute-done | bytes 8224 | tf_op jit(solution)/shard_map/ppermute | solution.py:475
  175.5 5.1 %collective-permute-done.22.refs_3_ = f32[16,128]{1,0:T(8,128)S(1)} collective-permute-done((f32[16,128]{1,0:T(8,128)S(1)}, f32[16,128]{1,0:T(8,128)S(1)}, u32[]{:S(2)}, u32[]{:S(2)}) %collective-permute-start.22) | collective-permute-done | bytes 8224 | tf_op jit(solution)/shard_map/ppermute | solution.py:475
  180.7 2.9 %update.1 = (f32[64,4096]{1,0:T(8,128)}, f32[64,4096]{1,0:T(8,128)}) custom-call(s32[7]{0:T(128)S(1)} %copy-done.10, f32[64,4096]{1,0:T(8,128)S(1)} %copy-done.1, f32[8,64,512]{2,1,0:T(8,128)} %all-to-all-done.1.residual_ref, f32[8,64,512]{2,1,0:T(8,128)S(1)} %all-to-all-done.2.image_ref, f32[16,128]{1,0:T(8,128)S(1)} %add_add_fusion.refs_0_, ...), custom_call_target="tpu_custom_call" | custom-call | tf_op jit(solution)/shard_map/update/pallas_call | solution.py:331
  (64 shorter events, 8.3 us)
Async XLA Ops:
  0.6 8.9 %copy-start = (f32[64,1024]{1,0:T(8,128)S(1)}, f32[64,1024]{1,0:T(8,128)}, u32[]{:S(2)}) copy-start(f32[64,1024]{1,0:T(8,128)} %param.11) | copy-start | bytes 786436
  1.6 15.0 %collective-permute-start.1 = (f32[64,256]{1,0:T(8,128)S(1)}, f32[64,256]{1,0:T(8,128)S(1)}, u32[]{:S(2)}, u32[]{:S(2)}) collective-permute-start(f32[64,256]{1,0:T(8,128)S(1)} %get-tuple-element.13), channel_id=1, source_target_pairs={{0,16},{16,32},{32,48},{48,64},{64,80},{80,96},{96,112},{112,128},... | collective-permute-start | bytes 196616 | tf_op jit(solution)/shard_map/ppermute | solution.py:436
  5.1 11.5 %collective-permute-start.2 = (f32[64,256]{1,0:T(8,128)S(1)}, f32[64,256]{1,0:T(8,128)S(1)}, u32[]{:S(2)}, u32[]{:S(2)}) collective-permute-start(f32[64,256]{1,0:T(8,128)S(1)} %get-tuple-element.12), channel_id=1, source_target_pairs={{16,0},{32,16},{48,32},{64,48},{80,64},{96,80},{112,96},{128,112},... | collective-permute-start | bytes 196616 | tf_op jit(solution)/shard_map/ppermute | solution.py:437
  9.6 8.7 %collective-permute-start = (f32[1,16,1024]{2,1,0:T(8,128)S(1)}, f32[1,16,1024]{2,1,0:T(8,128)S(1)}, u32[]{:S(2)}, u32[]{:S(2)}) collective-permute-start(f32[1,16,1024]{2,1,0:T(8,128)S(1)} %dynamic-slice_bitcast_fusion.a_ref), channel_id=1, source_target_pairs={{0,8},{1,9},{2,10},{3,11},{4,12},{5,13},{6,14},{7,15},{8,0},{9,1},... | collective-permute-start | bytes 196616 | tf_op jit(solution)/shard_map/ppermute | solution.py:441
  16.6 10.9 %copy-start.12 = (f32[64,256]{1,0:T(8,128)}, f32[64,256]{1,0:T(8,128)S(1)}, u32[]{:S(2)}) copy-start(f32[64,256]{1,0:T(8,128)S(1)} %collective-permute-done.2.refs_2_) | copy-start | bytes 196612
  16.6 4.6 %copy-start.13 = (f32[64,256]{1,0:T(8,128)}, f32[64,256]{1,0:T(8,128)S(1)}, u32[]{:S(2)}) copy-start(f32[64,256]{1,0:T(8,128)S(1)} %collective-permute-done.1.refs_2_) | copy-start | bytes 196612
  18.3 10.0 %collective-permute-start.3 = (f32[2,16,1024]{2,1,0:T(8,128)S(1)}, f32[2,16,1024]{2,1,0:T(8,128)S(1)}, u32[]{:S(2)}, u32[]{:S(2)}) collective-permute-start(f32[2,16,1024]{2,1,0:T(8,128)S(1)} %joined.3.a_ref), channel_id=1, source_target_pairs={{0,4},{1,5},{2,6},{3,7},{4,8},{5,9},{6,10},{7,11},{8,12},{9,13},{1... | collective-permute-start | bytes 393224 | tf_op jit(solution)/shard_map/ppermute | solution.py:443
  28.4 7.8 %collective-permute-start.4 = (f32[4,16,1024]{2,1,0:T(8,128)S(1)}, f32[4,16,1024]{2,1,0:T(8,128)S(1)}, u32[]{:S(2)}, u32[]{:S(2)}) collective-permute-start(f32[4,16,1024]{2,1,0:T(8,128)S(1)} %joined.4.a_ref), channel_id=1, source_target_pairs={{0,14},{1,15},{2,0},{3,1},{4,2},{5,3},{6,4},{7,5},{8,6},{9,7},{10,... | collective-permute-start | bytes 786440 | tf_op jit(solution)/shard_map/ppermute | solution.py:446
  36.8 55.5 %all-to-all-start = ((f32[8,128,512]{2,1,0:T(8,128)}), f32[8,128,512]{2,1,0:T(8,128)S(1)}, u32[]{:S(2)}, u32[]{:S(2)}) async-start(f32[8,128,512]{2,1,0:T(8,128)} %ordered.2), calls=%async_computation | async-start | bytes 4194304 | tf_op jit(solution)/shard_map/all_to_all | solution.py:411
  45.9 23.2 %copy-start.10 = (s32[7]{0:T(128)S(1)}, s32[7]{0:T(128)}, u32[]{:S(2)}) copy-start(s32[7]{0:T(128)} %stack.31.refs_0_.at_ref) | copy-start | bytes 88
  46.0 14.9 %collective-permute-start.5 = (f32[8,16,1024]{2,1,0:T(8,128)S(1)}, f32[8,16,1024]{2,1,0:T(8,128)S(1)}, u32[]{:S(2)}, u32[]{:S(2)}) collective-permute-start(f32[8,16,1024]{2,1,0:T(8,128)S(1)} %joined.5.refs_0_), channel_id=1, source_target_pairs={{0,48},{16,0},{32,16},{48,32},{64,112},{80,64},{96,80},{112,96},{1... | collective-permute-start | bytes 1572872 | tf_op jit(solution)/shard_map/ppermute | solution.py:449
  46.9 16.4 %collective-permute-start.6 = (f32[8,16,1024]{2,1,0:T(8,128)S(1)}, f32[8,16,1024]{2,1,0:T(8,128)S(1)}, u32[]{:S(2)}, u32[]{:S(2)}) collective-permute-start(f32[8,16,1024]{2,1,0:T(8,128)S(1)} %joined.5.refs_0_), channel_id=1, source_target_pairs={{0,32},{16,48},{32,0},{48,16},{64,96},{80,112},{96,64},{112,80},{1... | collective-permute-start | bytes 1572872 | tf_op jit(solution)/shard_map/ppermute | solution.py:449
  47.6 21.6 %collective-permute-start.7 = (f32[8,16,1024]{2,1,0:T(8,128)S(1)}, f32[8,16,1024]{2,1,0:T(8,128)S(1)}, u32[]{:S(2)}, u32[]{:S(2)}) collective-permute-start(f32[8,16,1024]{2,1,0:T(8,128)S(1)} %joined.5.refs_0_), channel_id=1, source_target_pairs={{0,16},{16,32},{32,48},{48,0},{64,80},{80,96},{96,112},{112,64},{1... | collective-permute-start | bytes 1572872 | tf_op jit(solution)/shard_map/ppermute | solution.py:449
  70.0 1.0 copy-start.5
  71.6 1.0 copy-start.2
  92.3 2.8 %copy-start.3 = (bf16[8,64,1024]{2,1,0:T(8,128)(2,1)S(1)}, bf16[8,64,1024]{2,1,0:T(8,128)(2,1)}, u32[]{:S(2)}) copy-start(bf16[8,64,1024]{2,1,0:T(8,128)(2,1)} %copy-done.2) | copy-start | bytes 3145732
  92.3 2.8 %copy-start.6 = (bf16[8,64,1024]{2,1,0:T(8,128)(2,1)S(1)}, bf16[8,64,1024]{2,1,0:T(8,128)(2,1)}, u32[]{:S(2)}) copy-start(bf16[8,64,1024]{2,1,0:T(8,128)(2,1)} %copy-done.5) | copy-start | bytes 3145732
  92.4 2.7 %collective-permute-start.8 = (f32[8,64,512]{2,1,0:T(8,128)S(1)}, f32[8,64,512]{2,1,0:T(8,128)S(1)}, u32[]{:S(2)}, u32[]{:S(2)}) collective-permute-start(f32[8,64,512]{2,1,0:T(8,128)S(1)} %first_rows.1), channel_id=1, source_target_pairs={{0,1},{1,0},{2,3},{3,2},{4,5},{5,4},{6,7},{7,6},{8,9},{9,8},{10,11... | collective-permute-start | bytes 3145736 | tf_op jit(solution)/shard_map/ppermute | solution.py:454
  98.9 17.0 %collective-permute-start.10 = (f32[8,64,256]{2,1,0:T(8,128)}, f32[8,64,256]{2,1,0:T(8,128)}, u32[]{:S(2)}, u32[]{:S(2)}) collective-permute-start(f32[8,64,256]{2,1,0:T(8,128)} %get-tuple-element.10), channel_id=1, source_target_pairs={{2,0},{3,1},{4,2},{5,3},{6,4},{7,5},{8,6},{9,7},{10,8},{11,9},{12,... | collective-permute-start | bytes 1572872 | tf_op jit(solution)/shard_map/ppermute | solution.py:464
  102.3 25.1 %copy-start.11 = (s32[32,4]{0,1:T(4,128)S(1)}, s32[32,4]{0,1:T(4,128)}, u32[]{:S(2)}) copy-start(s32[32,4]{0,1:T(4,128)} %param.9) | copy-start | bytes 1540
  102.3 25.1 %collective-permute-start.9 = (f32[8,64,256]{2,1,0:T(8,128)}, f32[8,64,256]{2,1,0:T(8,128)}, u32[]{:S(2)}, u32[]{:S(2)}) collective-permute-start(f32[8,64,256]{2,1,0:T(8,128)} %get-tuple-element.11), channel_id=1, source_target_pairs={{0,2},{1,3},{2,4},{3,5},{4,6},{5,7},{6,8},{7,9},{8,10},{9,11},{10,... | collective-permute-start | bytes 1572872 | tf_op jit(solution)/shard_map/ppermute | solution.py:463
  105.8 45.0 %all-to-all-start.1 = ((f32[8,64,512]{2,1,0:T(8,128)}), f32[8,64,512]{2,1,0:T(8,128)}, u32[]{:S(2)}, u32[]{:S(2)}) async-start(f32[8,64,512]{2,1,0:T(8,128)} %copied.1), calls=%async_computation.1 | async-start | bytes 2097152 | tf_op jit(solution)/shard_map/all_to_all | solution.py:411
  111.4 25.3 %copy-start.4 = (bf16[8,64,1024]{2,1,0:T(8,128)(2,1)S(1)}, bf16[8,64,1024]{2,1,0:T(8,128)(2,1)}, u32[]{:S(2)}) copy-start(bf16[8,64,1024]{2,1,0:T(8,128)(2,1)} %copy-done.2) | copy-start | bytes 3145732
  111.4 25.3 %copy-start.7 = (bf16[8,64,1024]{2,1,0:T(8,128)(2,1)S(1)}, bf16[8,64,1024]{2,1,0:T(8,128)(2,1)}, u32[]{:S(2)}) copy-start(bf16[8,64,1024]{2,1,0:T(8,128)(2,1)} %copy-done.5) | copy-start | bytes 3145732
  127.4 1.2 copy-start.9
  133.7 3.0 %collective-permute-start.11 = (f32[8,64,512]{2,1,0:T(8,128)}, f32[8,64,512]{2,1,0:T(8,128)}, u32[]{:S(2)}, u32[]{:S(2)}) collective-permute-start(f32[8,64,512]{2,1,0:T(8,128)} %space_mixed.1.own_ref), channel_id=1, source_target_pairs={{0,1},{1,0},{2,3},{3,2},{4,5},{5,4},{6,7},{7,6},{8,9},{9,8},{10,11... | collective-permute-start | bytes 3145736 | tf_op jit(solution)/shard_map/ppermute | solution.py:467
  140.4 1.0 copy-start.8
  141.4 1.2 collective-permute-start.12
  142.6 7.6 %collective-permute-start.13 = (f32[16,128]{1,0:T(8,128)S(1)}, f32[16,128]{1,0:T(8,128)S(1)}, u32[]{:S(2)}, u32[]{:S(2)}) collective-permute-start(f32[16,128]{1,0:T(8,128)S(1)} %add.52), channel_id=1, source_target_pairs={{0,8},{1,9},{2,10},{3,11},{4,12},{5,13},{6,14},{7,15},{8,0},{9,1},... | collective-permute-start | bytes 24584 | tf_op jit(solution)/shard_map/ppermute | solution.py:471
  150.7 3.7 %copy-start.14 = (f32[16,128]{1,0:T(8,128)S(1)}, f32[16,128]{1,0:T(8,128)}, u32[]{:S(2)}) copy-start(f32[16,128]{1,0:T(8,128)} %add.53.refs_1_) | copy-start | bytes 24580
  150.7 29.9 %copy-start.1 = (f32[64,4096]{1,0:T(8,128)S(1)}, f32[64,4096]{1,0:T(8,128)}, u32[]{:S(2)}) copy-start(f32[64,4096]{1,0:T(8,128)} %start_ref.1) | copy-start | bytes 3145732
  150.8 29.9 %all-to-all-start.2 = ((f32[8,64,512]{2,1,0:T(8,128)}), f32[8,64,512]{2,1,0:T(8,128)S(1)}, u32[]{:S(2)}, u32[]{:S(2)}) async-start(f32[8,64,512]{2,1,0:T(8,128)} %ordered.3), calls=%async_computation.2 | async-start | bytes 2097152 | tf_op jit(solution)/shard_map/all_to_all | solution.py:411
  154.4 4.9 %collective-permute-start.14 = (f32[16,128]{1,0:T(8,128)S(1)}, f32[16,128]{1,0:T(8,128)S(1)}, u32[]{:S(2)}, u32[]{:S(2)}) collective-permute-start(f32[16,128]{1,0:T(8,128)S(1)} %copy-done.14), channel_id=1, source_target_pairs={{0,16},{16,32},{32,48},{48,0},{64,80},{80,96},{96,112},{112,64},{1... | collective-permute-start | bytes 24584 | tf_op jit(solution)/shard_map/ppermute | solution.py:474
  154.5 5.2 %collective-permute-start.15 = (f32[16,128]{1,0:T(8,128)S(1)}, f32[16,128]{1,0:T(8,128)S(1)}, u32[]{:S(2)}, u32[]{:S(2)}) collective-permute-start(f32[16,128]{1,0:T(8,128)S(1)} %copy-done.14), channel_id=1, source_target_pairs={{0,32},{16,48},{32,0},{48,16},{64,96},{80,112},{96,64},{112,80},{1... | collective-permute-start | bytes 24584 | tf_op jit(solution)/shard_map/ppermute | solution.py:474
  155.7 4.6 %collective-permute-start.16 = (f32[16,128]{1,0:T(8,128)S(1)}, f32[16,128]{1,0:T(8,128)S(1)}, u32[]{:S(2)}, u32[]{:S(2)}) collective-permute-start(f32[16,128]{1,0:T(8,128)S(1)} %copy-done.14), channel_id=1, source_target_pairs={{0,48},{16,0},{32,16},{48,32},{64,112},{80,64},{96,80},{112,96},{1... | collective-permute-start | bytes 24584 | tf_op jit(solution)/shard_map/ppermute | solution.py:474
  160.3 3.7 %collective-permute-start.17 = (f32[16,128]{1,0:T(8,128)S(1)}, f32[16,128]{1,0:T(8,128)S(1)}, u32[]{:S(2)}, u32[]{:S(2)}) collective-permute-start(f32[16,128]{1,0:T(8,128)S(1)} %add_add_fusion.1), channel_id=1, source_target_pairs={{0,64},{16,80},{32,96},{48,112},{64,128},{80,144},{96,160},{112,17... | collective-permute-start | bytes 24584 | tf_op jit(solution)/shard_map/ppermute | solution.py:474
  160.3 5.2 %collective-permute-start.18 = (f32[16,128]{1,0:T(8,128)S(1)}, f32[16,128]{1,0:T(8,128)S(1)}, u32[]{:S(2)}, u32[]{:S(2)}) collective-permute-start(f32[16,128]{1,0:T(8,128)S(1)} %add_add_fusion.1), channel_id=1, source_target_pairs={{0,128},{16,144},{32,160},{48,176},{64,192},{80,208},{96,224},{112... | collective-permute-start | bytes 24584 | tf_op jit(solution)/shard_map/ppermute | solution.py:474
  163.2 4.9 %collective-permute-start.19 = (f32[16,128]{1,0:T(8,128)S(1)}, f32[16,128]{1,0:T(8,128)S(1)}, u32[]{:S(2)}, u32[]{:S(2)}) collective-permute-start(f32[16,128]{1,0:T(8,128)S(1)} %add_add_fusion.1), channel_id=1, source_target_pairs={{0,192},{16,208},{32,224},{48,240},{64,0},{80,16},{96,32},{112,48}... | collective-permute-start | bytes 24584 | tf_op jit(solution)/shard_map/ppermute | solution.py:474
  168.1 7.4 %collective-permute-start.20 = (f32[16,128]{1,0:T(8,128)S(1)}, f32[16,128]{1,0:T(8,128)S(1)}, u32[]{:S(2)}, u32[]{:S(2)}) collective-permute-start(f32[16,128]{1,0:T(8,128)S(1)} %add_add_fusion.refs_0_), channel_id=1, source_target_pairs={{0,2},{1,3},{2,4},{3,5},{4,6},{5,7},{6,8},{7,9},{8,10},{9,11},{10,... | collective-permute-start | bytes 24584 | tf_op jit(solution)/shard_map/ppermute | solution.py:475
  169.3 6.2 %collective-permute-start.21 = (f32[16,128]{1,0:T(8,128)S(1)}, f32[16,128]{1,0:T(8,128)S(1)}, u32[]{:S(2)}, u32[]{:S(2)}) collective-permute-start(f32[16,128]{1,0:T(8,128)S(1)} %add_add_fusion.refs_0_), channel_id=1, source_target_pairs={{0,4},{1,5},{2,6},{3,7},{4,8},{5,9},{6,10},{7,11},{8,12},{9,13},{1... | collective-permute-start | bytes 24584 | tf_op jit(solution)/shard_map/ppermute | solution.py:475
  172.8 7.7 %collective-permute-start.22 = (f32[16,128]{1,0:T(8,128)S(1)}, f32[16,128]{1,0:T(8,128)S(1)}, u32[]{:S(2)}, u32[]{:S(2)}) collective-permute-start(f32[16,128]{1,0:T(8,128)S(1)} %add_add_fusion.refs_0_), channel_id=1, source_target_pairs={{0,6},{1,7},{2,8},{3,9},{4,10},{5,11},{6,12},{7,13},{8,14},{9,15},... | collective-permute-start | bytes 24584 | tf_op jit(solution)/shard_map/ppermute | solution.py:475

commit v3 on v2

--- a/solution.py
+++ b/solution.py
@@ -10,7 +10,7 @@
 CHIPS = 8
 SAME_CORE = [[chip * 2 + core for chip in range(CHIPS)] for core in range(2)]
 SIDE = 4
-ORIGIN = (0, 4, 6, 2, 1, 5, 7, 3)
+ORIGIN = (0, 4, 1, 5, 7, 3, 6, 2)
 SWAP = [(i, i ^ 1) for i in range(2 * CHIPS)]
 F32 = jnp.float32
 BF16 = jnp.bfloat16
@@ -29,8 +29,8 @@
     return high, (value - high.astype(F32)).astype(BF16)
 
 
-def turned(at, index):
-    return jnp.where(at[6] == 1, CHIPS - 1 - index, index)
+def turned(space, index):
+    return jnp.where(space % 2 == 1, CHIPS - 1 - index, index)
 
 
 def params(megabytes):
@@ -76,85 +76,80 @@
     )(at, tiles)
 
 
-def space_wide_kernel(first, at_ref, ids_ref, edge_ref, noise_ref, x_ref, tiles_ref, right_ref, *refs):
-    out_ref, win_ref, x_here, tile_ref, right_here, stage_ref, x_sems, tile_sems, right_sems, out_sems = refs[-10:]
+def space_wide_kernel(ids_ref, low_ref, high_ref, noise_ref, x_ref, tiles_ref, right_ref, *refs):
+    out_ref, win_ref, x_here, tile_ref, right_here, stage_ref, sems, out_sems = refs
     hours, sites = x_ref.shape
+    space = lax.axis_index("space")
     groups = stage_ref.shape[0]
     rows, nb = tile_ref.shape[0] // groups, tile_ref.shape[1]
     width = rows * TILE
     count = sites // TILE
-    needed = range(first * rows, (first + groups) * rows + 2 * REACH)
-    inside = [i - REACH for i in needed if 0 <= i - REACH < count]
-    pieces = range(inside[0] // rows, inside[-1] // rows + 1)
+    base = space * count - REACH
     place = lambda g: slice(g * width, (g + 1) * width)
-    fetch = [pltpu.make_async_copy(x_ref.at[:, place(g)], x_here.at[:, place(g)], x_sems.at[g]) for g in pieces]
+    x_copy = pltpu.make_async_copy(x_ref, x_here, sems.at[groups])
+    right_copy = pltpu.make_async_copy(right_ref, right_here, sems.at[groups + 1])
     tiles = [
-        pltpu.make_async_copy(tiles_ref.at[first * rows + k], tile_ref.at[k], tile_sems.at[k])
-        for k in range(rows * groups)
+        pltpu.make_async_copy(tiles_ref.at[pl.ds(g * rows, rows)], tile_ref.at[pl.ds(g * rows, rows)], sems.at[g])
+        for g in range(groups)
     ]
-    right = [
-        pltpu.make_async_copy(right_ref.at[:, place(first + k)], right_here.at[k], right_sems.at[k]) for k in range(groups)
-    ]
-    for copy in fetch + tiles + right:
+    x_copy.start()
+    tiles[0].start()
+    right_copy.start()
+    for copy in tiles[1:]:
         copy.start()
-    for copy in fetch:
-        copy.wait()
-    for k, i in enumerate(needed):
-        if i < REACH:
-            piece = edge_ref[:, i * TILE : (i + 1) * TILE]
-        elif i < count + REACH:
-            piece = x_here[:, (i - REACH) * TILE : (i - REACH + 1) * TILE]
-        else:
-            j = i - count - REACH
-            piece = edge_ref[:, j * TILE : (j + 1) * TILE]
+
+    def keep(i, piece):
         high, low = halves(piece)
-        win_ref[k, :hours, :] = high
-        win_ref[k, hours:, :] = low
+        win_ref[i, :hours, :] = high
+        win_ref[i, hours:, :] = low
+
+    for i in range(REACH):
+        keep(i, low_ref[:, i * TILE : (i + 1) * TILE])
+        keep(i + count + REACH, high_ref[:, i * TILE : (i + 1) * TILE])
+    x_copy.wait()
+    for i in range(count):
+        keep(i + REACH, x_here[:, i * TILE : (i + 1) * TILE])
     sent = []
-    for k in range(groups):
+    for g in range(groups):
+        tiles[g].wait()
         for i in range(rows):
-            tiles[k * rows + i].wait()
-        for i in range(rows):
-            row = (first + k) * rows + i
-            field = [win_ref[ids_ref[n, row] - at_ref[3] - first * rows] for n in range(nb)]
-            mine = jnp.concatenate([tile_ref[k * rows + i, n] for n in range(nb)], axis=1)
+            row = g * rows + i
+            field = [win_ref[ids_ref[n, row] - base] for n in range(nb)]
+            mine = jnp.concatenate([tile_ref[row, n] for n in range(nb)], axis=1)
             product = dot_nt(jnp.concatenate(field, axis=1), stacked_halves(mine))
             columns = slice(i * TILE, (i + 1) * TILE)
-            stage_ref[k, :hours, columns] = product[:hours, :TILE] + (product[:hours, TILE:] + product[hours:, :TILE])
-        right[k].wait()
-        stage_ref[k, hours:, :] = right_here[k] - noise_ref[:, place(first + k)] * x_here[:, place(first + k)]
-        sent.append(pltpu.make_async_copy(stage_ref.at[k], out_ref.at[turned(at_ref, first + k)], out_sems.at[k]))
+            stage_ref[g, :hours, columns] = product[:hours, :TILE] + (product[:hours, TILE:] + product[hours:, :TILE])
+        if g == 0:
+            right_copy.wait()
+        stage_ref[g, hours:, :] = right_here[:, place(g)] - noise_ref[:, place(g)] * x_here[:, place(g)]
+        sent.append(pltpu.make_async_copy(stage_ref.at[g], out_ref.at[turned(space, g)], out_sems.at[g]))
         sent[-1].start()
     for copy in sent:
         copy.wait()
 
 
-def space_wide(first, at, ids, edge, x, tiles, right_side, noise, begun, after):
+def space_wide(ids, low, high, x, tiles, right_side, noise):
     hours, sites = x.shape
     nb, count = ids.shape
-    rows, groups = count // CHIPS, CHIPS // 2
-    more = ([] if begun is None else [begun]) + after
-    return pl.pallas_call(
-        lambda *refs: space_wide_kernel(first, *refs),
-        in_specs=[SMEM] * 2 + [VMEM] * 2 + [HBM] * 3 + [ANY] * len(more),
+    rows = count // CHIPS
+    return pl.pallas_call(
+        space_wide_kernel,
+        in_specs=[SMEM] + [VMEM] * 3 + [HBM] * 3,
         out_specs=ANY,
         out_shape=jax.ShapeDtypeStruct((CHIPS, 2 * hours, rows * TILE), F32),
-        input_output_aliases={} if begun is None else {7: 0},
         scratch_shapes=[
-            pltpu.VMEM((count // 2 + 2 * REACH, 2 * hours, TILE), BF16),
+            pltpu.VMEM((count + 2 * REACH, 2 * hours, TILE), BF16),
             pltpu.VMEM((hours, sites), F32),
-            pltpu.VMEM((rows * groups, nb, TILE, TILE), F32),
-            pltpu.VMEM((groups, hours, rows * TILE), F32),
-            pltpu.VMEM((groups, 2 * hours, rows * TILE), F32),
+            pltpu.VMEM((count, nb, TILE, TILE), F32),
+            pltpu.VMEM((hours, sites), F32),
+            pltpu.VMEM((CHIPS, 2 * hours, rows * TILE), F32),
+            pltpu.SemaphoreType.DMA((CHIPS + 2,)),
             pltpu.SemaphoreType.DMA((CHIPS,)),
-            pltpu.SemaphoreType.DMA((rows * groups,)),
-            pltpu.SemaphoreType.DMA((groups,)),
-            pltpu.SemaphoreType.DMA((groups,)),
         ],
         compiler_params=params(56),
-        cost_estimate=cost(0, 0),
+        cost_estimate=cost(2 * 10**9, 0),
         name="space_wide",
-    )(at, ids, edge, noise[None, :], x, tiles, right_side, *more)
+    )(ids, low, high, noise[None, :], x, tiles, right_side)
 
 
 def space_mixed_kernel(at_ref, ids_ref, left_ref, own_ref, right_ref, weights_ref, *refs):
@@ -320,7 +315,7 @@
     alpha = jnp.sum(total[:8, :]) / jnp.sum(total[8:, :])
     for g in range(chips):
         columns = slice(g * width, (g + 1) * width)
-        chip = turned(at_ref, g)
+        chip = turned(at_ref[6], g)
         r = residual_ref[chip]
         iterate_ref[:, columns] = start_ref[:, columns] + alpha * r
         next_ref[:, columns] = r - alpha * image_ref[chip]
@@ -358,7 +353,7 @@
 def ordered(value, *after):
     return pl.pallas_call(
         lambda *refs: None,
-        in_specs=[ANY] * (1 + len(after)),
+        in_specs=[ANY] + [VMEM] * len(after),
         out_specs=ANY,
         out_shape=jax.ShapeDtypeStruct(value.shape, value.dtype),
         input_output_aliases={0: 0},
@@ -367,21 +362,22 @@
     )(value, *after)
 
 
-def joined_kernel(a_ref, b_ref, *refs):
-    refs[-1][: a_ref.shape[0]] = a_ref[...]
-    refs[-1][a_ref.shape[0] :] = b_ref[...]
-
-
-def joined(a, b, after):
-    return pl.pallas_call(
-        joined_kernel,
-        in_specs=[VMEM] * 2 + [ANY] * len(after),
+def joined(arrays, after):
+    def kernel(*refs):
+        first = 0
+        for ref in refs[: len(arrays)]:
+            refs[-1][first : first + ref.shape[0]] = ref[...]
+            first += ref.shape[0]
+
+    return pl.pallas_call(
+        kernel,
+        in_specs=[VMEM] * (len(arrays) + len(after)),
         out_specs=VMEM,
-        out_shape=jax.ShapeDtypeStruct((a.shape[0] + b.shape[0],) + a.shape[1:], F32),
+        out_shape=jax.ShapeDtypeStruct((sum(a.shape[0] for a in arrays),) + arrays[0].shape[1:], F32),
         compiler_params=params(8),
         cost_estimate=cost(0, 0),
         name="joined",
-    )(a, b, *after)
+    )(*arrays, *after)
 
 
 def copied_kernel(value_ref, out_ref, sem):
@@ -427,9 +423,8 @@
     space, tm = lax.axis_index("space"), lax.axis_index("tm")
     chip, core = tm // 2, tm % 2
     base = space * count - REACH
-    flip = space % 2
-    group = jnp.where(flip == 1, CHIPS - 1 - chip, chip)
-    at = jnp.stack([chip, core, base + group * (count // CHIPS), base, space % SIDE, group, flip]).astype(jnp.int32)
+    group = turned(space, chip)
+    at = jnp.stack([chip, core, base + group * (count // CHIPS), base, space % SIDE, group, space]).astype(jnp.int32)
 
     forward = [(i, i + 1) for i in range(spaces - 1)]
     backward = [(target, source) for source, target in forward]
@@ -438,19 +433,15 @@
     rows = time_kernel.shape[0] // SIDE
     ids = tile_ids.T
     strip = lax.dynamic_slice(time_kernel, (space % SIDE * rows, 0), (rows, time_kernel.shape[1]))[None]
-    far = lax.ppermute(strip, "tm", along_z(4))
-    strip = joined(strip, far, [token(low), token(high)])
-    far = lax.ppermute(strip, "tm", along_z(2))
-    sent = space_wide(0, at, ids, low, start, space_tiles, right_side, noise, None, [])
-    strip = joined(strip, far, [token(sent)])
-    far = lax.ppermute(strip, "tm", along_z(-1))
-    sent = space_wide(CHIPS // 2, at, ids, high, start, space_tiles, right_side, noise, sent, [token(strip)])
-    strip = joined(strip, far, [])
+    strip = joined([strip, lax.ppermute(strip, "tm", along_z(CHIPS // 2))], [])
+    beside = [lax.ppermute(strip, "tm", along_z(shift)) for shift in (-1, 1, 2)]
+    sent = space_wide(ids, low, high, start, space_tiles, right_side, noise)
+    strip = joined([strip] + beside, [])
     strips = [strip] + [lax.ppermute(strip, "space", along_side(-k, "y")) for k in range(1, SIDE)]
     khi, klo = time_rows(at, strips)
     weights = weights_of(at, space_tiles)
 
-    got = exchange(ordered(sent, token(far)))
+    got = exchange(ordered(sent, sum(token(b) for b in beside)))
     other = lax.ppermute(first_rows(got, hours_dev, [token(khi), token(weights)]), "tm", SWAP)
     residual = residual_of(at, khi, klo, got, other)
 

time: 185 us -> 178 us (0.962); the launches traced: 184 us -> 175 us
  waiting for transfers between devices: 81.7 us -> 66.5 us
  starting transfers between devices: 57.1 us -> 66.4 us
  Pallas kernels: 33 us -> 30 us
    ppermute x1, waiting for transfers between devices: 11.5 us -> 2.02 us  [local(): left = lax.ppermute(residual[:, :, width - edge:], ('space', 'tm'), up)]
    ppermute x6, starting transfers between devices: 6.7 us -> 12.8 us  [local(): lax.ppermute(sums, 'space', along_side(shift, axis))]
    pallas_call x7 -> x5, Pallas kernels: 12.7 us -> 8.81 us  [the longest x1 7.28 us: space_wide(): pl.pallas_call(space_wide_kernel, in_specs=[SMEM] + [VMEM] * 3 + [HBM] *...]
    squeeze x6 -> x1, local copies, waits for them, and re-layouts: 2.59 us -> 0.69 us  [token(): return value.reshape((-1,) + value.shape[-2:])[0, :16, :TILE]]
    ppermute x3 -> x4, starting transfers between devices: 10.1 us -> 11.1 us  [the longest x1 6.29 us: local(): strip = joined([strip, lax.ppermute(strip, 'tm', along_z(CHIPS // 2))], [])]
  transfers between devices with their start and end apart: 26 -> 27, of which waited for: 21 -> 16; matrix products, arithmetic and copies ran while one was open for 2% -> 2% of each run, Pallas kernels for 15% -> 13%
where the time goes in v3:
time: 178 us; the launch traced here: 175 us
  waiting for transfers between devices  66.5 us (37%)
  starting transfers between devices  66.4 us (37%)
  Pallas kernels  30 us (17%)
  local copies, waits for them, and re-layouts  9.75 us (5%)
    all_to_all x3, starting transfers between devices, exchange(): lax.all_to_all(blocks, 'tm', 0, 0, axis_index_groups=SAME_CORE, tiled=True)  19 us
    all_to_all x3, waiting for transfers between devices, exchange(): lax.all_to_all(blocks, 'tm', 0, 0, axis_index_groups=SAME_CORE, tiled=True)  18.9 us
    ppermute x3, waiting for transfers between devices, local(): lax.ppermute(strip, 'space', along_side(-k, 'y'))  18.2 us
    ppermute x6, starting transfers between devices, local(): lax.ppermute(sums, 'space', along_side(shift, axis))  12.8 us
    pallas_call x1, Pallas kernels, space_wide(): pl.pallas_call(space_wide_kernel, in_specs=[SMEM] + [VMEM] * 3 + [HBM] *...  7.28 us
    ppermute x6, waiting for transfers between devices, local(): lax.ppermute(sums, 'space', along_side(shift, axis))  6.5 us
    ppermute x1, starting transfers between devices, local(): strip = joined([strip, lax.ppermute(strip, 'tm', along_z(CHIPS // 2))], [])  6.29 us
    ppermute x3, waiting for transfers between devices, local(): lax.ppermute(sums, 'tm', along_z(shift))  6.1 us
  transfers between devices with their start and end apart: 27, of which 16 were waited for; matrix products, arithmetic and copies ran while one was open for 2% of the time, Pallas kernels for 13%

profile of v3, /device:TPU:38, one launch (start us, length us, event | category | flops | bytes accessed | tf_op | source)
XLA Modules:
  0.0 174.7 jit_solution(3068741298773902171)
XLA Ops:
  1.6 6.3 %collective-permute-start = (f32[1,16,1024]{2,1,0:T(8,128)S(1)}, f32[1,16,1024]{2,1,0:T(8,128)S(1)}, u32[]{:S(2)}, u32[]{:S(2)}) collective-permute-start(f32[1,16,1024]{2,1,0:T(8,128)S(1)} %dynamic-slice_bitcast_fusion.refs_0_), channel_id=1, source_target_pairs={{0,8},{1,9},{2,10},{3,11},{4,12},{5,13},{6,14},{7,15},{8,0},{9,1},... | collective-permute-start | bytes 196616 | tf_op jit(solution)/shard_map/ppermute | solution.py:436
  8.8 3.5 %collective-permute-start.7 = (f32[64,256]{1,0:T(8,128)S(1)}, f32[64,256]{1,0:T(8,128)S(1)}, u32[]{:S(2)}, u32[]{:S(2)}) collective-permute-start(f32[64,256]{1,0:T(8,128)S(1)} %get-tuple-element.13), channel_id=1, source_target_pairs={{0,16},{16,32},{32,48},{48,64},{64,80},{80,96},{96,112},{112,128},... | collective-permute-start | bytes 196616 | tf_op jit(solution)/shard_map/ppermute | solution.py:431
  12.3 4.5 %collective-permute-start.8 = (f32[64,256]{1,0:T(8,128)S(1)}, f32[64,256]{1,0:T(8,128)S(1)}, u32[]{:S(2)}, u32[]{:S(2)}) collective-permute-start(f32[64,256]{1,0:T(8,128)S(1)} %get-tuple-element.12), channel_id=1, source_target_pairs={{16,0},{32,16},{48,32},{64,48},{80,64},{96,80},{112,96},{128,112},... | collective-permute-start | bytes 196616 | tf_op jit(solution)/shard_map/ppermute | solution.py:432
  16.8 1.1 collective-permute-start.1
  17.8 1.0 collective-permute-start.2
  18.9 2.7 %collective-permute-start.3 = (f32[2,16,1024]{2,1,0:T(8,128)S(1)}, f32[2,16,1024]{2,1,0:T(8,128)S(1)}, u32[]{:S(2)}, u32[]{:S(2)}) collective-permute-start(f32[2,16,1024]{2,1,0:T(8,128)S(1)} %joined.2.refs_0_), channel_id=1, source_target_pairs={{0,4},{1,5},{2,6},{3,7},{4,8},{5,9},{6,10},{7,11},{8,12},{9,13},{1... | collective-permute-start | bytes 393224 | tf_op jit(solution)/shard_map/ppermute | solution.py:437
  22.2 7.3 %space_wide.1.refs_0_ = f32[8,128,512]{2,1,0:T(8,128)} custom-call(s32[4,32]{1,0:T(4,128)} %bitcast.21, f32[64,256]{1,0:T(8,128)} %copy-done.13, f32[64,256]{1,0:T(8,128)} %copy-done.14, f32[1,4096]{1,0:T(1,128)} %bitcast.23, f32[64,4096]{1,0:T(8,128)} %start_ref.1, f32[32,4,128,128]{3,2,1,0:T(8,128)} %tiles_ref.3, f32[64,4096]{1,0:T(8,128)} %right_ref.1), custom_call_target="tpu_custom_call" | custom-call | flops 2000000000 | tf_op jit(solution)/shard_map/space_wide/pallas_call | solution.py:135
  30.8 5.1 %all-to-all-start = ((f32[8,128,512]{2,1,0:T(8,128)}), f32[8,128,512]{2,1,0:T(8,128)S(1)}, u32[]{:S(2)}, u32[]{:S(2)}) async-start(f32[8,128,512]{2,1,0:T(8,128)} %ordered.2), calls=%async_computation | async-start | bytes 4194304 | tf_op jit(solution)/shard_map/all_to_all | solution.py:407
  36.0 1.0 collective-permute-start.4
  37.6 1.0 collective-permute-start.6
  39.2 4.2 %weights_of.1.weights_ref = bf16[4,4,256,128]{3,2,1,0:T(8,128)(2,1)} custom-call(s32[7]{0:T(128)} %stack.31.at_ref, f32[32,4,128,128]{3,2,1,0:T(8,128)} %tiles_ref.3), custom_call_target="tpu_custom_call" | custom-call | tf_op jit(solution)/shard_map/weights_of/pallas_call | solution.py:64
  43.4 7.6 %collective-permute-done.4.refs_1_ = f32[8,16,1024]{2,1,0:T(8,128)S(1)} collective-permute-done((f32[8,16,1024]{2,1,0:T(8,128)S(1)}, f32[8,16,1024]{2,1,0:T(8,128)S(1)}, u32[]{:S(2)}, u32[]{:S(2)}) %collective-permute-start.4) | collective-permute-done | bytes 524320 | tf_op jit(solution)/shard_map/ppermute | solution.py:440
  50.9 2.5 %collective-permute-done.5.refs_2_ = f32[8,16,1024]{2,1,0:T(8,128)} collective-permute-done((f32[8,16,1024]{2,1,0:T(8,128)S(1)}, f32[8,16,1024]{2,1,0:T(8,128)}, u32[]{:S(2)}, u32[]{:S(2)}) %collective-permute-start.5) | collective-permute-done | bytes 524320 | tf_op jit(solution)/shard_map/ppermute | solution.py:440
  53.5 8.1 %collective-permute-done.6.refs_3_ = f32[8,16,1024]{2,1,0:T(8,128)} collective-permute-done((f32[8,16,1024]{2,1,0:T(8,128)S(1)}, f32[8,16,1024]{2,1,0:T(8,128)}, u32[]{:S(2)}, u32[]{:S(2)}) %collective-permute-start.6) | collective-permute-done | bytes 524320 | tf_op jit(solution)/shard_map/ppermute | solution.py:440
  61.6 1.5 time_rows.1
  63.0 1.0 copy-done.5
  64.7 1.0 copy-done.2
  65.7 18.9 %all-to-all-done.value_ref.got_ref = f32[8,128,512]{2,1,0:T(8,128)S(1)} async-done(((f32[8,128,512]{2,1,0:T(8,128)}), f32[8,128,512]{2,1,0:T(8,128)S(1)}, u32[]{:S(2)}, u32[]{:S(2)}) %all-to-all-start) | async-done | bytes 2097184 | tf_op jit(solution)/shard_map/all_to_all | solution.py:407
  84.8 2.6 %collective-permute-done.9.other_ref = f32[8,64,512]{2,1,0:T(8,128)S(1)} collective-permute-done((f32[8,64,512]{2,1,0:T(8,128)S(1)}, f32[8,64,512]{2,1,0:T(8,128)S(1)}, u32[]{:S(2)}, u32[]{:S(2)}) %collective-permute-start.9) | collective-permute-done | bytes 1048608 | tf_op jit(solution)/shard_map/ppermute | solution.py:445
  87.4 2.7 %residual_of.1.value_ref.own_ref.r_ref = f32[8,64,512]{2,1,0:T(8,128)S(1)} custom-call(s32[7]{0:T(128)S(1)} %copy-done.10, bf16[8,64,1024]{2,1,0:T(8,128)(2,1)S(1)} %copy-done.3, bf16[8,64,1024]{2,1,0:T(8,128)(2,1)S(1)} %copy-done.6, f32[8,128,512]{2,1,0:T(8,128)S(1)} %all-to-all-done.value_ref.got_ref, f32[8,64,512]{2,1,0:T(8,128)S(1)} %collective-permute-done.9.other_ref), custom_call_target="tpu_custom_call" | custom-call | tf_op jit(solution)/shard_map/residual_of/pallas_call | solution.py:262
  90.1 1.1 fusion.1
  91.2 2.4 %collective-permute-start.10 = (f32[8,64,256]{2,1,0:T(8,128)}, f32[8,64,256]{2,1,0:T(8,128)}, u32[]{:S(2)}, u32[]{:S(2)}) collective-permute-start(f32[8,64,256]{2,1,0:T(8,128)} %get-tuple-element.11), channel_id=1, source_target_pairs={{0,2},{1,3},{2,4},{3,5},{4,6},{5,7},{6,8},{7,9},{8,10},{9,11},{10,... | collective-permute-start | bytes 1572872 | tf_op jit(solution)/shard_map/ppermute | solution.py:454
  93.6 3.5 %collective-permute-start.11 = (f32[8,64,256]{2,1,0:T(8,128)}, f32[8,64,256]{2,1,0:T(8,128)}, u32[]{:S(2)}, u32[]{:S(2)}) collective-permute-start(f32[8,64,256]{2,1,0:T(8,128)} %get-tuple-element.10), channel_id=1, source_target_pairs={{2,0},{3,1},{4,2},{5,3},{6,4},{7,5},{8,6},{9,7},{10,8},{11,9},{12,... | collective-permute-start | bytes 1572872 | tf_op jit(solution)/shard_map/ppermute | solution.py:455
  97.1 1.0 copied.1
  98.1 7.8 %all-to-all-start.1 = ((f32[8,64,512]{2,1,0:T(8,128)}), f32[8,64,512]{2,1,0:T(8,128)}, u32[]{:S(2)}, u32[]{:S(2)}) async-start(f32[8,64,512]{2,1,0:T(8,128)} %copied.1), calls=%async_computation.1 | async-start | bytes 2097152 | tf_op jit(solution)/shard_map/all_to_all | solution.py:407
  105.9 2.0 %collective-permute-done.10.left_ref = f32[8,64,256]{2,1,0:T(8,128)} collective-permute-done((f32[8,64,256]{2,1,0:T(8,128)}, f32[8,64,256]{2,1,0:T(8,128)}, u32[]{:S(2)}, u32[]{:S(2)}) %collective-permute-start.10) | collective-permute-done | bytes 524320 | tf_op jit(solution)/shard_map/ppermute | solution.py:454
  107.9 2.8 %collective-permute-done.11.right_ref = f32[8,64,256]{2,1,0:T(8,128)} collective-permute-done((f32[8,64,256]{2,1,0:T(8,128)}, f32[8,64,256]{2,1,0:T(8,128)}, u32[]{:S(2)}, u32[]{:S(2)}) %collective-permute-start.11) | collective-permute-done | bytes 524320 | tf_op jit(solution)/shard_map/ppermute | solution.py:455
  110.6 1.2 copy-done.9
  111.9 5.0 %space_mixed.1.own_ref = f32[8,64,512]{2,1,0:T(8,128)} custom-call(s32[7]{0:T(128)S(1)} %copy-done.10, s32[4,32]{1,0:T(4,128)S(1)} %bitcast.22, f32[8,64,256]{2,1,0:T(8,128)} %collective-permute-done.10.left_ref, f32[8,64,512]{2,1,0:T(8,128)S(1)} %residual_of.1.value_ref.own_ref.r_ref, f32[8,64,256]{2,1,0:T(8,128)} %collective-permute-done.11.right_ref, ...), custom_call_target="tpu_custom_call" | custom-call | flops 4000000000 | tf_op jit(solution)/shard_map/space_mixed/pallas_call | solution.py:183
  117.7 2.2 %collective-permute-done.12.other_ref = f32[8,64,512]{2,1,0:T(8,128)} collective-permute-done((f32[8,64,512]{2,1,0:T(8,128)}, f32[8,64,512]{2,1,0:T(8,128)}, u32[]{:S(2)}, u32[]{:S(2)}) %collective-permute-start.12) | collective-permute-done | bytes 1048608 | tf_op jit(solution)/shard_map/ppermute | solution.py:458
  119.9 3.7 %image_of.1 = (f32[8,64,512]{2,1,0:T(8,128)S(1)}, f32[16,128]{1,0:T(8,128)S(1)}) custom-call(s32[7]{0:T(128)S(1)} %copy-done.10, bf16[8,64,1024]{2,1,0:T(8,128)(2,1)S(1)} %copy-done.4, bf16[8,64,1024]{2,1,0:T(8,128)(2,1)S(1)} %copy-done.7, f32[8,64,512]{2,1,0:T(8,128)} %space_mixed.1.own_ref, f32[8,64,512]{2,1,0:T(8,128)} %collective-permute-done.12.other_ref, ...), custom_call_target="tpu_custom_call" | custom-call | tf_op jit(solution)/shard_map/image_of/pallas_call | solution.py:297
  124.8 1.0 collective-permute-done.13
  125.8 1.6 collective-permute-start.14
  127.4 6.1 %collective-permute-done.14 = f32[16,128]{1,0:T(8,128)S(1)} collective-permute-done((f32[16,128]{1,0:T(8,128)S(1)}, f32[16,128]{1,0:T(8,128)S(1)}, u32[]{:S(2)}, u32[]{:S(2)}) %collective-permute-start.14) | collective-permute-done | bytes 8224 | tf_op jit(solution)/shard_map/ppermute | solution.py:462
  134.8 6.1 %all-to-all-start.2 = ((f32[8,64,512]{2,1,0:T(8,128)}), f32[8,64,512]{2,1,0:T(8,128)S(1)}, u32[]{:S(2)}, u32[]{:S(2)}) async-start(f32[8,64,512]{2,1,0:T(8,128)} %ordered.3), calls=%async_computation.2 | async-start | bytes 2097152 | tf_op jit(solution)/shard_map/all_to_all | solution.py:407
  140.9 6.9 %collective-permute-start.17 = (f32[16,128]{1,0:T(8,128)S(1)}, f32[16,128]{1,0:T(8,128)S(1)}, u32[]{:S(2)}, u32[]{:S(2)}) collective-permute-start(f32[16,128]{1,0:T(8,128)S(1)} %copy-done.12), channel_id=1, source_target_pairs={{0,48},{16,0},{32,16},{48,32},{64,112},{80,64},{96,80},{112,96},{1... | collective-permute-start | bytes 24584 | tf_op jit(solution)/shard_map/ppermute | solution.py:465
  147.8 1.4 collective-permute-start.16
  149.2 3.7 %collective-permute-done.16 = f32[16,128]{1,0:T(8,128)S(1)} collective-permute-done((f32[16,128]{1,0:T(8,128)S(1)}, f32[16,128]{1,0:T(8,128)S(1)}, u32[]{:S(2)}, u32[]{:S(2)}) %collective-permute-start.16) | collective-permute-done | bytes 8224 | tf_op jit(solution)/shard_map/ppermute | solution.py:465
  153.0 1.1 collective-permute-done.15
  154.1 1.0 collective-permute-start.20
  155.1 1.4 collective-permute-start.19
  156.5 2.1 %collective-permute-start.18 = (f32[16,128]{1,0:T(8,128)S(1)}, f32[16,128]{1,0:T(8,128)S(1)}, u32[]{:S(2)}, u32[]{:S(2)}) collective-permute-start(f32[16,128]{1,0:T(8,128)S(1)} %add_add_fusion.1), channel_id=1, source_target_pairs={{0,64},{16,80},{32,96},{48,112},{64,128},{80,144},{96,160},{112,17... | collective-permute-start | bytes 24584 | tf_op jit(solution)/shard_map/ppermute | solution.py:465
  159.0 1.3 collective-permute-done.19
  160.3 1.2 collective-permute-start.21
  161.5 3.6 %collective-permute-start.22 = (f32[16,128]{1,0:T(8,128)S(1)}, f32[16,128]{1,0:T(8,128)S(1)}, u32[]{:S(2)}, u32[]{:S(2)}) collective-permute-start(f32[16,128]{1,0:T(8,128)S(1)} %add_add_fusion.refs_0_), channel_id=1, source_target_pairs={{0,4},{1,5},{2,6},{3,7},{4,8},{5,9},{6,10},{7,11},{8,12},{9,13},{1... | collective-permute-start | bytes 24584 | tf_op jit(solution)/shard_map/ppermute | solution.py:466
  165.6 2.0 %collective-permute-done.22.refs_2_ = f32[16,128]{1,0:T(8,128)S(1)} collective-permute-done((f32[16,128]{1,0:T(8,128)S(1)}, f32[16,128]{1,0:T(8,128)S(1)}, u32[]{:S(2)}, u32[]{:S(2)}) %collective-permute-start.22) | collective-permute-done | bytes 8224 | tf_op jit(solution)/shard_map/ppermute | solution.py:466
  167.6 4.1 %collective-permute-done.23.refs_3_ = f32[16,128]{1,0:T(8,128)S(1)} collective-permute-done((f32[16,128]{1,0:T(8,128)S(1)}, f32[16,128]{1,0:T(8,128)S(1)}, u32[]{:S(2)}, u32[]{:S(2)}) %collective-permute-start.23) | collective-permute-done | bytes 8224 | tf_op jit(solution)/shard_map/ppermute | solution.py:466
  171.7 2.9 %update.1 = (f32[64,4096]{1,0:T(8,128)}, f32[64,4096]{1,0:T(8,128)}) custom-call(s32[7]{0:T(128)S(1)} %copy-done.10, f32[64,4096]{1,0:T(8,128)S(1)} %copy-done.1, f32[8,64,512]{2,1,0:T(8,128)} %all-to-all-done.1.residual_ref, f32[8,64,512]{2,1,0:T(8,128)S(1)} %all-to-all-done.2.image_ref, f32[16,128]{1,0:T(8,128)S(1)} %add_add_fusion.refs_0_, ...), custom_call_target="tpu_custom_call" | custom-call | tf_op jit(solution)/shard_map/update/pallas_call | solution.py:326
  (60 shorter events, 10.1 us)
Async XLA Ops:
  0.6 1.0 copy-start
  1.6 15.1 %collective-permute-start = (f32[1,16,1024]{2,1,0:T(8,128)S(1)}, f32[1,16,1024]{2,1,0:T(8,128)S(1)}, u32[]{:S(2)}, u32[]{:S(2)}) collective-permute-start(f32[1,16,1024]{2,1,0:T(8,128)S(1)} %dynamic-slice_bitcast_fusion.refs_0_), channel_id=1, source_target_pairs={{0,8},{1,9},{2,10},{3,11},{4,12},{5,13},{6,14},{7,15},{8,0},{9,1},... | collective-permute-start | bytes 196616 | tf_op jit(solution)/shard_map/ppermute | solution.py:436
  8.8 12.8 %collective-permute-start.7 = (f32[64,256]{1,0:T(8,128)S(1)}, f32[64,256]{1,0:T(8,128)S(1)}, u32[]{:S(2)}, u32[]{:S(2)}) collective-permute-start(f32[64,256]{1,0:T(8,128)S(1)} %get-tuple-element.13), channel_id=1, source_target_pairs={{0,16},{16,32},{32,48},{48,64},{64,80},{80,96},{96,112},{112,128},... | collective-permute-start | bytes 196616 | tf_op jit(solution)/shard_map/ppermute | solution.py:431
  12.3 9.3 %collective-permute-start.8 = (f32[64,256]{1,0:T(8,128)S(1)}, f32[64,256]{1,0:T(8,128)S(1)}, u32[]{:S(2)}, u32[]{:S(2)}) collective-permute-start(f32[64,256]{1,0:T(8,128)S(1)} %get-tuple-element.12), channel_id=1, source_target_pairs={{16,0},{32,16},{48,32},{64,48},{80,64},{96,80},{112,96},{128,112},... | collective-permute-start | bytes 196616 | tf_op jit(solution)/shard_map/ppermute | solution.py:432
  16.8 12.7 %collective-permute-start.1 = (f32[2,16,1024]{2,1,0:T(8,128)S(1)}, f32[2,16,1024]{2,1,0:T(8,128)S(1)}, u32[]{:S(2)}, u32[]{:S(2)}) collective-permute-start(f32[2,16,1024]{2,1,0:T(8,128)S(1)} %joined.2.refs_0_), channel_id=1, source_target_pairs={{0,14},{1,15},{2,0},{3,1},{4,2},{5,3},{6,4},{7,5},{8,6},{9,7},{10,... | collective-permute-start | bytes 393224 | tf_op jit(solution)/shard_map/ppermute | solution.py:437
  17.8 11.7 %collective-permute-start.2 = (f32[2,16,1024]{2,1,0:T(8,128)S(1)}, f32[2,16,1024]{2,1,0:T(8,128)S(1)}, u32[]{:S(2)}, u32[]{:S(2)}) collective-permute-start(f32[2,16,1024]{2,1,0:T(8,128)S(1)} %joined.2.refs_0_), channel_id=1, source_target_pairs={{0,2},{1,3},{2,4},{3,5},{4,6},{5,7},{6,8},{7,9},{8,10},{9,11},{10,... | collective-permute-start | bytes 393224 | tf_op jit(solution)/shard_map/ppermute | solution.py:437
  18.9 10.7 %collective-permute-start.3 = (f32[2,16,1024]{2,1,0:T(8,128)S(1)}, f32[2,16,1024]{2,1,0:T(8,128)S(1)}, u32[]{:S(2)}, u32[]{:S(2)}) collective-permute-start(f32[2,16,1024]{2,1,0:T(8,128)S(1)} %joined.2.refs_0_), channel_id=1, source_target_pairs={{0,4},{1,5},{2,6},{3,7},{4,8},{5,9},{6,10},{7,11},{8,12},{9,13},{1... | collective-permute-start | bytes 393224 | tf_op jit(solution)/shard_map/ppermute | solution.py:437
  21.6 0.6 copy-start.13
  21.6 0.6 copy-start.14
  30.8 53.8 %all-to-all-start = ((f32[8,128,512]{2,1,0:T(8,128)}), f32[8,128,512]{2,1,0:T(8,128)S(1)}, u32[]{:S(2)}, u32[]{:S(2)}) async-start(f32[8,128,512]{2,1,0:T(8,128)} %ordered.2), calls=%async_computation | async-start | bytes 4194304 | tf_op jit(solution)/shard_map/all_to_all | solution.py:407
  36.0 14.9 %collective-permute-start.4 = (f32[8,16,1024]{2,1,0:T(8,128)S(1)}, f32[8,16,1024]{2,1,0:T(8,128)S(1)}, u32[]{:S(2)}, u32[]{:S(2)}) collective-permute-start(f32[8,16,1024]{2,1,0:T(8,128)S(1)} %joined.3.refs_0_), channel_id=1, source_target_pairs={{0,48},{16,0},{32,16},{48,32},{64,112},{80,64},{96,80},{112,96},{1... | collective-permute-start | bytes 1572872 | tf_op jit(solution)/shard_map/ppermute | solution.py:440
  37.0 16.5 %collective-permute-start.5 = (f32[8,16,1024]{2,1,0:T(8,128)S(1)}, f32[8,16,1024]{2,1,0:T(8,128)}, u32[]{:S(2)}, u32[]{:S(2)}) collective-permute-start(f32[8,16,1024]{2,1,0:T(8,128)S(1)} %joined.3.refs_0_), channel_id=1, source_target_pairs={{0,32},{16,48},{32,0},{48,16},{64,96},{80,112},{96,64},{112,80},{1... | collective-permute-start | bytes 1572872 | tf_op jit(solution)/shard_map/ppermute | solution.py:440
  37.6 23.9 %collective-permute-start.6 = (f32[8,16,1024]{2,1,0:T(8,128)S(1)}, f32[8,16,1024]{2,1,0:T(8,128)}, u32[]{:S(2)}, u32[]{:S(2)}) collective-permute-start(f32[8,16,1024]{2,1,0:T(8,128)S(1)} %joined.3.refs_0_), channel_id=1, source_target_pairs={{0,16},{16,32},{32,48},{48,0},{64,80},{80,96},{96,112},{112,64},{1... | collective-permute-start | bytes 1572872 | tf_op jit(solution)/shard_map/ppermute | solution.py:440
  39.2 22.4 %copy-start.10 = (s32[7]{0:T(128)S(1)}, s32[7]{0:T(128)}, u32[]{:S(2)}) copy-start(s32[7]{0:T(128)} %stack.31.at_ref) | copy-start | bytes 88
  63.0 1.0 copy-start.5
  64.7 1.0 copy-start.2
  84.6 2.8 %copy-start.3 = (bf16[8,64,1024]{2,1,0:T(8,128)(2,1)S(1)}, bf16[8,64,1024]{2,1,0:T(8,128)(2,1)}, u32[]{:S(2)}) copy-start(bf16[8,64,1024]{2,1,0:T(8,128)(2,1)} %copy-done.2) | copy-start | bytes 3145732
  84.6 2.8 %copy-start.6 = (bf16[8,64,1024]{2,1,0:T(8,128)(2,1)S(1)}, bf16[8,64,1024]{2,1,0:T(8,128)(2,1)}, u32[]{:S(2)}) copy-start(bf16[8,64,1024]{2,1,0:T(8,128)(2,1)} %copy-done.5) | copy-start | bytes 3145732
  84.7 2.7 %collective-permute-start.9 = (f32[8,64,512]{2,1,0:T(8,128)S(1)}, f32[8,64,512]{2,1,0:T(8,128)S(1)}, u32[]{:S(2)}, u32[]{:S(2)}) collective-permute-start(f32[8,64,512]{2,1,0:T(8,128)S(1)} %first_rows.1), channel_id=1, source_target_pairs={{0,1},{1,0},{2,3},{3,2},{4,5},{5,4},{6,7},{7,6},{8,9},{9,8},{10,11... | collective-permute-start | bytes 3145736 | tf_op jit(solution)/shard_map/ppermute | solution.py:445
  91.2 16.7 %collective-permute-start.10 = (f32[8,64,256]{2,1,0:T(8,128)}, f32[8,64,256]{2,1,0:T(8,128)}, u32[]{:S(2)}, u32[]{:S(2)}) collective-permute-start(f32[8,64,256]{2,1,0:T(8,128)} %get-tuple-element.11), channel_id=1, source_target_pairs={{0,2},{1,3},{2,4},{3,5},{4,6},{5,7},{6,8},{7,9},{8,10},{9,11},{10,... | collective-permute-start | bytes 1572872 | tf_op jit(solution)/shard_map/ppermute | solution.py:454
  93.6 17.0 %copy-start.11 = (s32[32,4]{0,1:T(4,128)S(1)}, s32[32,4]{0,1:T(4,128)}, u32[]{:S(2)}) copy-start(s32[32,4]{0,1:T(4,128)} %param.9) | copy-start | bytes 1540
  93.6 17.0 %collective-permute-start.11 = (f32[8,64,256]{2,1,0:T(8,128)}, f32[8,64,256]{2,1,0:T(8,128)}, u32[]{:S(2)}, u32[]{:S(2)}) collective-permute-start(f32[8,64,256]{2,1,0:T(8,128)} %get-tuple-element.10), channel_id=1, source_target_pairs={{2,0},{3,1},{4,2},{5,3},{6,4},{7,5},{8,6},{9,7},{10,8},{11,9},{12,... | collective-permute-start | bytes 1572872 | tf_op jit(solution)/shard_map/ppermute | solution.py:455
  98.1 36.7 %all-to-all-start.1 = ((f32[8,64,512]{2,1,0:T(8,128)}), f32[8,64,512]{2,1,0:T(8,128)}, u32[]{:S(2)}, u32[]{:S(2)}) async-start(f32[8,64,512]{2,1,0:T(8,128)} %copied.1), calls=%async_computation.1 | async-start | bytes 2097152 | tf_op jit(solution)/shard_map/all_to_all | solution.py:407
  105.9 14.1 %copy-start.4 = (bf16[8,64,1024]{2,1,0:T(8,128)(2,1)S(1)}, bf16[8,64,1024]{2,1,0:T(8,128)(2,1)}, u32[]{:S(2)}) copy-start(bf16[8,64,1024]{2,1,0:T(8,128)(2,1)} %copy-done.2) | copy-start | bytes 3145732
  105.9 14.1 %copy-start.7 = (bf16[8,64,1024]{2,1,0:T(8,128)(2,1)S(1)}, bf16[8,64,1024]{2,1,0:T(8,128)(2,1)}, u32[]{:S(2)}) copy-start(bf16[8,64,1024]{2,1,0:T(8,128)(2,1)} %copy-done.5) | copy-start | bytes 3145732
  110.6 1.2 copy-start.9
  116.9 3.0 %collective-permute-start.12 = (f32[8,64,512]{2,1,0:T(8,128)}, f32[8,64,512]{2,1,0:T(8,128)}, u32[]{:S(2)}, u32[]{:S(2)}) collective-permute-start(f32[8,64,512]{2,1,0:T(8,128)} %space_mixed.1.own_ref), channel_id=1, source_target_pairs={{0,1},{1,0},{2,3},{3,2},{4,5},{5,4},{6,7},{7,6},{8,9},{9,8},{10,11... | collective-permute-start | bytes 3145736 | tf_op jit(solution)/shard_map/ppermute | solution.py:458
  123.7 1.0 copy-start.8
  124.6 1.2 collective-permute-start.13
  125.8 7.6 %collective-permute-start.14 = (f32[16,128]{1,0:T(8,128)S(1)}, f32[16,128]{1,0:T(8,128)S(1)}, u32[]{:S(2)}, u32[]{:S(2)}) collective-permute-start(f32[16,128]{1,0:T(8,128)S(1)} %add.64), channel_id=1, source_target_pairs={{0,8},{1,9},{2,10},{3,11},{4,12},{5,13},{6,14},{7,15},{8,0},{9,1},... | collective-permute-start | bytes 24584 | tf_op jit(solution)/shard_map/ppermute | solution.py:462
  134.1 6.9 %copy-start.12 = (f32[16,128]{1,0:T(8,128)S(1)}, f32[16,128]{1,0:T(8,128)}, u32[]{:S(2)}) copy-start(f32[16,128]{1,0:T(8,128)} %add.65.refs_1_) | copy-start | bytes 24580
  134.1 37.7 %copy-start.1 = (f32[64,4096]{1,0:T(8,128)S(1)}, f32[64,4096]{1,0:T(8,128)}, u32[]{:S(2)}) copy-start(f32[64,4096]{1,0:T(8,128)} %start_ref.1) | copy-start | bytes 3145732
  134.8 36.9 %all-to-all-start.2 = ((f32[8,64,512]{2,1,0:T(8,128)}), f32[8,64,512]{2,1,0:T(8,128)S(1)}, u32[]{:S(2)}, u32[]{:S(2)}) async-start(f32[8,64,512]{2,1,0:T(8,128)} %ordered.3), calls=%async_computation.2 | async-start | bytes 2097152 | tf_op jit(solution)/shard_map/all_to_all | solution.py:407
  140.9 8.3 %collective-permute-start.17 = (f32[16,128]{1,0:T(8,128)S(1)}, f32[16,128]{1,0:T(8,128)S(1)}, u32[]{:S(2)}, u32[]{:S(2)}) collective-permute-start(f32[16,128]{1,0:T(8,128)S(1)} %copy-done.12), channel_id=1, source_target_pairs={{0,48},{16,0},{32,16},{48,32},{64,112},{80,64},{96,80},{112,96},{1... | collective-permute-start | bytes 24584 | tf_op jit(solution)/shard_map/ppermute | solution.py:465
  147.8 5.2 %collective-permute-start.16 = (f32[16,128]{1,0:T(8,128)S(1)}, f32[16,128]{1,0:T(8,128)S(1)}, u32[]{:S(2)}, u32[]{:S(2)}) collective-permute-start(f32[16,128]{1,0:T(8,128)S(1)} %copy-done.12), channel_id=1, source_target_pairs={{0,32},{16,48},{32,0},{48,16},{64,96},{80,112},{96,64},{112,80},{1... | collective-permute-start | bytes 24584 | tf_op jit(solution)/shard_map/ppermute | solution.py:465
  149.2 4.9 %collective-permute-start.15 = (f32[16,128]{1,0:T(8,128)S(1)}, f32[16,128]{1,0:T(8,128)S(1)}, u32[]{:S(2)}, u32[]{:S(2)}) collective-permute-start(f32[16,128]{1,0:T(8,128)S(1)} %copy-done.12), channel_id=1, source_target_pairs={{0,16},{16,32},{32,48},{48,0},{64,80},{80,96},{96,112},{112,64},{1... | collective-permute-start | bytes 24584 | tf_op jit(solution)/shard_map/ppermute | solution.py:465
  154.1 4.9 %collective-permute-start.20 = (f32[16,128]{1,0:T(8,128)S(1)}, f32[16,128]{1,0:T(8,128)S(1)}, u32[]{:S(2)}, u32[]{:S(2)}) collective-permute-start(f32[16,128]{1,0:T(8,128)S(1)} %add_add_fusion.1), channel_id=1, source_target_pairs={{0,192},{16,208},{32,224},{48,240},{64,0},{80,16},{96,32},{112,48}... | collective-permute-start | bytes 24584 | tf_op jit(solution)/shard_map/ppermute | solution.py:465
  155.1 5.2 %collective-permute-start.19 = (f32[16,128]{1,0:T(8,128)S(1)}, f32[16,128]{1,0:T(8,128)S(1)}, u32[]{:S(2)}, u32[]{:S(2)}) collective-permute-start(f32[16,128]{1,0:T(8,128)S(1)} %add_add_fusion.1), channel_id=1, source_target_pairs={{0,128},{16,144},{32,160},{48,176},{64,192},{80,208},{96,224},{112... | collective-permute-start | bytes 24584 | tf_op jit(solution)/shard_map/ppermute | solution.py:465
  156.5 3.7 %collective-permute-start.18 = (f32[16,128]{1,0:T(8,128)S(1)}, f32[16,128]{1,0:T(8,128)S(1)}, u32[]{:S(2)}, u32[]{:S(2)}) collective-permute-start(f32[16,128]{1,0:T(8,128)S(1)} %add_add_fusion.1), channel_id=1, source_target_pairs={{0,64},{16,80},{32,96},{48,112},{64,128},{80,144},{96,160},{112,17... | collective-permute-start | bytes 24584 | tf_op jit(solution)/shard_map/ppermute | solution.py:465
  160.3 5.4 %collective-permute-start.21 = (f32[16,128]{1,0:T(8,128)S(1)}, f32[16,128]{1,0:T(8,128)S(1)}, u32[]{:S(2)}, u32[]{:S(2)}) collective-permute-start(f32[16,128]{1,0:T(8,128)S(1)} %add_add_fusion.refs_0_), channel_id=1, source_target_pairs={{0,2},{1,3},{2,4},{3,5},{4,6},{5,7},{6,8},{7,9},{8,10},{9,11},{10,... | collective-permute-start | bytes 24584 | tf_op jit(solution)/shard_map/ppermute | solution.py:466
  161.5 6.1 %collective-permute-start.22 = (f32[16,128]{1,0:T(8,128)S(1)}, f32[16,128]{1,0:T(8,128)S(1)}, u32[]{:S(2)}, u32[]{:S(2)}) collective-permute-start(f32[16,128]{1,0:T(8,128)S(1)} %add_add_fusion.refs_0_), channel_id=1, source_target_pairs={{0,4},{1,5},{2,6},{3,7},{4,8},{5,9},{6,10},{7,11},{8,12},{9,13},{1... | collective-permute-start | bytes 24584 | tf_op jit(solution)/shard_map/ppermute | solution.py:466
  165.1 6.7 %collective-permute-start.23 = (f32[16,128]{1,0:T(8,128)S(1)}, f32[16,128]{1,0:T(8,128)S(1)}, u32[]{:S(2)}, u32[]{:S(2)}) collective-permute-start(f32[16,128]{1,0:T(8,128)S(1)} %add_add_fusion.refs_0_), channel_id=1, source_target_pairs={{0,6},{1,7},{2,8},{3,9},{4,10},{5,11},{6,12},{7,13},{8,14},{9,15},... | collective-permute-start | bytes 24584 | tf_op jit(solution)/shard_map/ppermute | solution.py:466

commit v4 on v3

--- a/solution.py
+++ b/solution.py
@@ -152,54 +152,53 @@
     )(ids, low, high, noise[None, :], x, tiles, right_side)
 
 
-def space_mixed_kernel(at_ref, ids_ref, left_ref, own_ref, right_ref, weights_ref, *refs):
-    out_ref, hi_ref, lo_ref = refs[-3:]
+def space_mixed_kernel(at_ref, ids_ref, left_ref, own_ref, right_ref, weights_ref, out_ref, hi_ref, lo_ref, *refs):
+    left_here, own_here, right_here, weights_here, sems = refs
+    chips, hours, sites = own_ref.shape
     rows, nb = weights_ref.shape[:2]
-    for i in range(rows + 2 * REACH):
-        if i < REACH:
-            piece = left_ref[:, :, i * TILE : (i + 1) * TILE]
-        elif i < rows + REACH:
-            piece = own_ref[:, :, (i - REACH) * TILE : (i - REACH + 1) * TILE]
-        else:
-            k = i - rows - REACH
-            piece = right_ref[:, :, k * TILE : (k + 1) * TILE]
+    pairs = ((own_ref, own_here), (left_ref, left_here), (right_ref, right_here), (weights_ref, weights_here))
+    copies = [pltpu.make_async_copy(source, target, sems.at[k]) for k, (source, target) in enumerate(pairs)]
+    for copy in copies:
+        copy.start()
+
+    def keep(i, piece):
         high, low = halves(piece.reshape(-1, TILE))
         hi_ref[i] = high
         lo_ref[i] = low
+
+    copies[0].wait()
+    for i in range(rows):
+        keep(i + REACH, own_here[:, :, i * TILE : (i + 1) * TILE])
+    copies[1].wait()
+    copies[2].wait()
+    for i in range(REACH):
+        keep(i, left_here[:, :, i * TILE : (i + 1) * TILE])
+        keep(i + rows + REACH, right_here[:, :, i * TILE : (i + 1) * TILE])
+    copies[3].wait()
     for row in range(rows):
-        total = None
-        for n in range(nb):
-            i = ids_ref[n, at_ref[5] * rows + row] - at_ref[2]
-            both = dot_nt(hi_ref[i], weights_ref[row, n])
-            part = both[:, :TILE] + (both[:, TILE:] + dot_nt(lo_ref[i], weights_ref[row, n, :TILE]))
-            total = part if total is None else total + part
-        out_ref[:, :, row * TILE : (row + 1) * TILE] = total.reshape(out_ref.shape[:2] + (TILE,))
-
-
-def space_mixed(at, ids, left, own, right, weights, after):
-    nb, count = ids.shape
-    rows, hours = count // CHIPS, own.shape[0] * own.shape[1]
-    whole = lambda i, at, ids: (0, 0, 0)
+        places = [ids_ref[n, at_ref[5] * rows + row] - at_ref[2] for n in range(nb)]
+        high = jnp.concatenate([hi_ref[i] for i in places], axis=1)
+        low = jnp.concatenate([lo_ref[i] for i in places], axis=1)
+        weights = jnp.concatenate([weights_here[row, n] for n in range(nb)], axis=1)
+        both = dot_nt(high, weights)
+        product = both[:, :TILE] + (both[:, TILE:] + dot_nt(low, weights[:TILE]))
+        out_ref[:, :, row * TILE : (row + 1) * TILE] = product.reshape(chips, hours, TILE)
+
+
+def space_mixed(at, ids, left, own, right, weights):
+    rows, hours = weights.shape[0], own.shape[0] * own.shape[1]
     return pl.pallas_call(
         space_mixed_kernel,
-        grid_spec=pltpu.PrefetchScalarGridSpec(
-            num_scalar_prefetch=2,
-            grid=(1,),
-            in_specs=[
-                pl.BlockSpec(left.shape, whole),
-                pl.BlockSpec(own.shape, whole),
-                pl.BlockSpec(right.shape, whole),
-                pl.BlockSpec((rows, nb, 2 * TILE, TILE), lambda i, at, ids: (0, 0, 0, 0)),
-            ]
-            + [ANY] * len(after),
-            out_specs=pl.BlockSpec(own.shape, whole),
-            scratch_shapes=[pltpu.VMEM((rows + 2 * REACH, hours, TILE), BF16)] * 2,
-        ),
+        in_specs=[SMEM, SMEM, ANY, HBM, ANY, ANY],
+        out_specs=VMEM,
         out_shape=jax.ShapeDtypeStruct(own.shape, F32),
+        scratch_shapes=[pltpu.VMEM((rows + 2 * REACH, hours, TILE), BF16)] * 2
+        + [pltpu.VMEM(a.shape, a.dtype) for a in (left, own, right, weights)]
+        + [pltpu.SemaphoreType.DMA((4,))],
         compiler_params=params(24),
         cost_estimate=cost(4000000000, 0),
         name="space_mixed",
-    )(at, ids, left, own, right, weights, *after)
+    )(at, ids, left, own, right, weights)
 
 
 def time_rows_kernel(at_ref, *refs):
@@ -453,14 +452,16 @@
             down.append((target * 2 + c, source * 2 + c))
     left = lax.ppermute(residual[:, :, width - edge :], ("space", "tm"), up)
     right = lax.ppermute(residual[:, :, :edge], ("space", "tm"), down)
-    back_r = exchange(copied(residual))
-    mixed = space_mixed(at, ids, left, residual, right, weights, [])
+    kept = copied(residual)
+    back_r = exchange(kept)
+    mixed = space_mixed(at, ids, left, kept, right, weights)
     other = lax.ppermute(mixed, "tm", SWAP)
     noise_here = lax.dynamic_slice(noise, (group * width,), (width,))[None, :]
     image, sums = image_of(at, khi, klo, mixed, other, residual, noise_here)
     sums = sums + lax.ppermute(sums, "tm", SWAP)
-    sums = sums + lax.ppermute(sums, "tm", along_z(CHIPS // 2))
-    back_p = exchange(ordered(image, sums))
+    far = lax.ppermute(sums, "tm", along_z(CHIPS // 2))
+    back_p = exchange(ordered(image, far))
+    sums = sums + far
     for axis in ("y", "x"):
         sums = sum([lax.ppermute(sums, "space", along_side(shift, axis)) for shift in range(1, SIDE)], sums)
     sums = [sums] + [lax.ppermute(sums, "tm", along_z(shift)) for shift in range(1, CHIPS // 2)]

time: 178 us -> 177 us (level); the launches traced: 175 us -> 176 us
    unnamed x30 -> x32, local copies, waits for them, and re-layouts: 5.72 us -> 6.32 us
where the time goes in v4:
time: 177 us; the launch traced here: 176 us
  waiting for transfers between devices  68.2 us (39%)
  starting transfers between devices  66.6 us (38%)
  Pallas kernels  29.4 us (17%)
  local copies, waits for them, and re-layouts  10.3 us (6%)
    all_to_all x3, starting transfers between devices, exchange(): lax.all_to_all(blocks, 'tm', 0, 0, axis_index_groups=SAME_CORE, tiled=True)  19 us
    all_to_all x3, waiting for transfers between devices, exchange(): lax.all_to_all(blocks, 'tm', 0, 0, axis_index_groups=SAME_CORE, tiled=True)  19 us
    ppermute x3, waiting for transfers between devices, local(): lax.ppermute(strip, 'space', along_side(-k, 'y'))  18.2 us
    ppermute x6, starting transfers between devices, local(): lax.ppermute(sums, 'space', along_side(shift, axis))  12.8 us
    ppermute x6, waiting for transfers between devices, local(): lax.ppermute(sums, 'space', along_side(shift, axis))  7.63 us
    pallas_call x1, Pallas kernels, space_wide(): pl.pallas_call(space_wide_kernel, in_specs=[SMEM] + [VMEM] * 3 + [HBM] *...  7.28 us
    ppermute x1, waiting for transfers between devices, local(): far = lax.ppermute(sums, 'tm', along_z(CHIPS // 2))  6.62 us
    unnamed x32, local copies, waits for them, and re-layouts  6.32 us
  transfers between devices with their start and end apart: 27, of which 16 were waited for; matrix products, arithmetic and copies ran while one was open for 2% of the time, Pallas kernels for 13%

profile of v4, /device:TPU:38, one launch (start us, length us, event | category | flops | bytes accessed | tf_op | source)
XLA Modules:
  0.0 176.0 jit_solution(11953954452502380148)
XLA Ops:
  1.6 6.3 %collective-permute-start = (f32[1,16,1024]{2,1,0:T(8,128)S(1)}, f32[1,16,1024]{2,1,0:T(8,128)S(1)}, u32[]{:S(2)}, u32[]{:S(2)}) collective-permute-start(f32[1,16,1024]{2,1,0:T(8,128)S(1)} %dynamic-slice_bitcast_fusion.refs_0_), channel_id=1, source_target_pairs={{0,8},{1,9},{2,10},{3,11},{4,12},{5,13},{6,14},{7,15},{8,0},{9,1},... | collective-permute-start | bytes 196616 | tf_op jit(solution)/shard_map/ppermute | solution.py:435
  8.8 3.5 %collective-permute-start.7 = (f32[64,256]{1,0:T(8,128)S(1)}, f32[64,256]{1,0:T(8,128)S(1)}, u32[]{:S(2)}, u32[]{:S(2)}) collective-permute-start(f32[64,256]{1,0:T(8,128)S(1)} %get-tuple-element.13), channel_id=1, source_target_pairs={{0,16},{16,32},{32,48},{48,64},{64,80},{80,96},{96,112},{112,128},... | collective-permute-start | bytes 196616 | tf_op jit(solution)/shard_map/ppermute | solution.py:430
  12.3 4.5 %collective-permute-start.8 = (f32[64,256]{1,0:T(8,128)S(1)}, f32[64,256]{1,0:T(8,128)S(1)}, u32[]{:S(2)}, u32[]{:S(2)}) collective-permute-start(f32[64,256]{1,0:T(8,128)S(1)} %get-tuple-element.12), channel_id=1, source_target_pairs={{16,0},{32,16},{48,32},{64,48},{80,64},{96,80},{112,96},{128,112},... | collective-permute-start | bytes 196616 | tf_op jit(solution)/shard_map/ppermute | solution.py:431
  16.8 1.1 collective-permute-start.1
  17.8 1.0 collective-permute-start.2
  18.9 2.7 %collective-permute-start.3 = (f32[2,16,1024]{2,1,0:T(8,128)S(1)}, f32[2,16,1024]{2,1,0:T(8,128)S(1)}, u32[]{:S(2)}, u32[]{:S(2)}) collective-permute-start(f32[2,16,1024]{2,1,0:T(8,128)S(1)} %joined.2.refs_0_), channel_id=1, source_target_pairs={{0,4},{1,5},{2,6},{3,7},{4,8},{5,9},{6,10},{7,11},{8,12},{9,13},{1... | collective-permute-start | bytes 393224 | tf_op jit(solution)/shard_map/ppermute | solution.py:436
  22.2 7.3 %space_wide.1.refs_0_ = f32[8,128,512]{2,1,0:T(8,128)} custom-call(s32[4,32]{1,0:T(4,128)} %bitcast.21, f32[64,256]{1,0:T(8,128)} %copy-done.12, f32[64,256]{1,0:T(8,128)} %copy-done.13, f32[1,4096]{1,0:T(1,128)} %bitcast.23, f32[64,4096]{1,0:T(8,128)} %start_ref.1, f32[32,4,128,128]{3,2,1,0:T(8,128)} %tiles_ref.3, f32[64,4096]{1,0:T(8,128)} %right_ref.1), custom_call_target="tpu_custom_call" | custom-call | flops 2000000000 | tf_op jit(solution)/shard_map/space_wide/pallas_call | solution.py:135
  30.8 5.1 %all-to-all-start = ((f32[8,128,512]{2,1,0:T(8,128)}), f32[8,128,512]{2,1,0:T(8,128)S(1)}, u32[]{:S(2)}, u32[]{:S(2)}) async-start(f32[8,128,512]{2,1,0:T(8,128)} %ordered.2), calls=%async_computation | async-start | bytes 4194304 | tf_op jit(solution)/shard_map/all_to_all | solution.py:406
  36.0 1.0 collective-permute-start.4
  37.6 1.0 collective-permute-start.6
  39.2 4.2 %weights_of.1.weights_ref = bf16[4,4,256,128]{3,2,1,0:T(8,128)(2,1)} custom-call(s32[7]{0:T(128)} %stack.31.at_ref, f32[32,4,128,128]{3,2,1,0:T(8,128)} %tiles_ref.3), custom_call_target="tpu_custom_call" | custom-call | tf_op jit(solution)/shard_map/weights_of/pallas_call | solution.py:64
  43.4 7.6 %collective-permute-done.4.refs_1_ = f32[8,16,1024]{2,1,0:T(8,128)S(1)} collective-permute-done((f32[8,16,1024]{2,1,0:T(8,128)S(1)}, f32[8,16,1024]{2,1,0:T(8,128)S(1)}, u32[]{:S(2)}, u32[]{:S(2)}) %collective-permute-start.4) | collective-permute-done | bytes 524320 | tf_op jit(solution)/shard_map/ppermute | solution.py:439
  50.9 2.5 %collective-permute-done.5.refs_2_ = f32[8,16,1024]{2,1,0:T(8,128)} collective-permute-done((f32[8,16,1024]{2,1,0:T(8,128)S(1)}, f32[8,16,1024]{2,1,0:T(8,128)}, u32[]{:S(2)}, u32[]{:S(2)}) %collective-permute-start.5) | collective-permute-done | bytes 524320 | tf_op jit(solution)/shard_map/ppermute | solution.py:439
  53.5 8.1 %collective-permute-done.6.refs_3_ = f32[8,16,1024]{2,1,0:T(8,128)} collective-permute-done((f32[8,16,1024]{2,1,0:T(8,128)S(1)}, f32[8,16,1024]{2,1,0:T(8,128)}, u32[]{:S(2)}, u32[]{:S(2)}) %collective-permute-start.6) | collective-permute-done | bytes 524320 | tf_op jit(solution)/shard_map/ppermute | solution.py:439
  61.6 1.5 time_rows.1
  63.0 1.0 copy-done.5
  64.7 1.0 copy-done.2
  65.7 18.9 %all-to-all-done.value_ref.got_ref = f32[8,128,512]{2,1,0:T(8,128)S(1)} async-done(((f32[8,128,512]{2,1,0:T(8,128)}), f32[8,128,512]{2,1,0:T(8,128)S(1)}, u32[]{:S(2)}, u32[]{:S(2)}) %all-to-all-start) | async-done | bytes 2097184 | tf_op jit(solution)/shard_map/all_to_all | solution.py:406
  84.8 2.6 %collective-permute-done.9.other_ref = f32[8,64,512]{2,1,0:T(8,128)S(1)} collective-permute-done((f32[8,64,512]{2,1,0:T(8,128)S(1)}, f32[8,64,512]{2,1,0:T(8,128)S(1)}, u32[]{:S(2)}, u32[]{:S(2)}) %collective-permute-start.9) | collective-permute-done | bytes 1048608 | tf_op jit(solution)/shard_map/ppermute | solution.py:444
  87.4 2.7 %residual_of.1.value_ref.r_ref = f32[8,64,512]{2,1,0:T(8,128)S(1)} custom-call(s32[7]{0:T(128)S(1)} %copy-done.10, bf16[8,64,1024]{2,1,0:T(8,128)(2,1)S(1)} %copy-done.3, bf16[8,64,1024]{2,1,0:T(8,128)(2,1)S(1)} %copy-done.6, f32[8,128,512]{2,1,0:T(8,128)S(1)} %all-to-all-done.value_ref.got_ref, f32[8,64,512]{2,1,0:T(8,128)S(1)} %collective-permute-done.9.other_ref), custom_call_target="tpu_custom_call" | custom-call | tf_op jit(solution)/shard_map/residual_of/pallas_call | solution.py:261
  90.1 1.1 fusion.1
  91.2 2.4 %collective-permute-start.10 = (f32[8,64,256]{2,1,0:T(8,128)}, f32[8,64,256]{2,1,0:T(8,128)}, u32[]{:S(2)}, u32[]{:S(2)}) collective-permute-start(f32[8,64,256]{2,1,0:T(8,128)} %get-tuple-element.11), channel_id=1, source_target_pairs={{0,2},{1,3},{2,4},{3,5},{4,6},{5,7},{6,8},{7,9},{8,10},{9,11},{10,... | collective-permute-start | bytes 1572872 | tf_op jit(solution)/shard_map/ppermute | solution.py:453
  93.6 3.5 %collective-permute-start.11 = (f32[8,64,256]{2,1,0:T(8,128)}, f32[8,64,256]{2,1,0:T(8,128)}, u32[]{:S(2)}, u32[]{:S(2)}) collective-permute-start(f32[8,64,256]{2,1,0:T(8,128)} %get-tuple-element.10), channel_id=1, source_target_pairs={{2,0},{3,1},{4,2},{5,3},{6,4},{7,5},{8,6},{9,7},{10,8},{11,9},{12,... | collective-permute-start | bytes 1572872 | tf_op jit(solution)/shard_map/ppermute | solution.py:454
  97.1 1.0 copied.1.own_ref
  98.1 7.8 %all-to-all-start.1 = ((f32[8,64,512]{2,1,0:T(8,128)}), f32[8,64,512]{2,1,0:T(8,128)}, u32[]{:S(2)}, u32[]{:S(2)}) async-start(f32[8,64,512]{2,1,0:T(8,128)} %copied.1.own_ref), calls=%async_computation.1 | async-start | bytes 2097152 | tf_op jit(solution)/shard_map/all_to_all | solution.py:406
  105.8 2.0 %collective-permute-done.10.left_ref = f32[8,64,256]{2,1,0:T(8,128)} collective-permute-done((f32[8,64,256]{2,1,0:T(8,128)}, f32[8,64,256]{2,1,0:T(8,128)}, u32[]{:S(2)}, u32[]{:S(2)}) %collective-permute-start.10) | collective-permute-done | bytes 524320 | tf_op jit(solution)/shard_map/ppermute | solution.py:453
  107.9 2.7 %collective-permute-done.11.right_ref = f32[8,64,256]{2,1,0:T(8,128)} collective-permute-done((f32[8,64,256]{2,1,0:T(8,128)}, f32[8,64,256]{2,1,0:T(8,128)}, u32[]{:S(2)}, u32[]{:S(2)}) %collective-permute-start.11) | collective-permute-done | bytes 524320 | tf_op jit(solution)/shard_map/ppermute | solution.py:454
  110.6 1.2 copy-done.9
  111.9 4.5 %space_mixed.1.own_ref = f32[8,64,512]{2,1,0:T(8,128)} custom-call(s32[7]{0:T(128)S(1)} %copy-done.10, s32[4,32]{1,0:T(4,128)S(1)} %bitcast.22, f32[8,64,256]{2,1,0:T(8,128)} %collective-permute-done.10.left_ref, f32[8,64,512]{2,1,0:T(8,128)} %copied.1.own_ref, f32[8,64,256]{2,1,0:T(8,128)} %collective-permute-done.11.right_ref, ...), custom_call_target="tpu_custom_call" | custom-call | flops 4000000000 | tf_op jit(solution)/shard_map/space_mixed/pallas_call | solution.py:190
  117.2 2.2 %collective-permute-done.12.other_ref = f32[8,64,512]{2,1,0:T(8,128)} collective-permute-done((f32[8,64,512]{2,1,0:T(8,128)}, f32[8,64,512]{2,1,0:T(8,128)}, u32[]{:S(2)}, u32[]{:S(2)}) %collective-permute-start.12) | collective-permute-done | bytes 1048608 | tf_op jit(solution)/shard_map/ppermute | solution.py:458
  119.4 3.7 %image_of.1 = (f32[8,64,512]{2,1,0:T(8,128)S(1)}, f32[16,128]{1,0:T(8,128)S(1)}) custom-call(s32[7]{0:T(128)S(1)} %copy-done.10, bf16[8,64,1024]{2,1,0:T(8,128)(2,1)S(1)} %copy-done.4, bf16[8,64,1024]{2,1,0:T(8,128)(2,1)S(1)} %copy-done.7, f32[8,64,512]{2,1,0:T(8,128)} %space_mixed.1.own_ref, f32[8,64,512]{2,1,0:T(8,128)} %collective-permute-done.12.other_ref, ...), custom_call_target="tpu_custom_call" | custom-call | tf_op jit(solution)/shard_map/image_of/pallas_call | solution.py:296
  123.2 1.0 copy-done.8
  124.3 1.0 collective-permute-done.13
  125.3 1.6 collective-permute-start.14
  126.9 6.6 %collective-permute-done.14.refs_1_ = f32[16,128]{1,0:T(8,128)S(1)} collective-permute-done((f32[16,128]{1,0:T(8,128)S(1)}, f32[16,128]{1,0:T(8,128)S(1)}, u32[]{:S(2)}, u32[]{:S(2)}) %collective-permute-start.14) | collective-permute-done | bytes 8224 | tf_op jit(solution)/shard_map/ppermute | solution.py:462
  134.9 6.1 %all-to-all-start.2 = ((f32[8,64,512]{2,1,0:T(8,128)}), f32[8,64,512]{2,1,0:T(8,128)S(1)}, u32[]{:S(2)}, u32[]{:S(2)}) async-start(f32[8,64,512]{2,1,0:T(8,128)} %ordered.3), calls=%async_computation.2 | async-start | bytes 2097152 | tf_op jit(solution)/shard_map/all_to_all | solution.py:406
  141.1 5.8 %collective-permute-start.15 = (f32[16,128]{1,0:T(8,128)S(1)}, f32[16,128]{1,0:T(8,128)S(1)}, u32[]{:S(2)}, u32[]{:S(2)}) collective-permute-start(f32[16,128]{1,0:T(8,128)S(1)} %add.65), channel_id=1, source_target_pairs={{0,16},{16,32},{32,48},{48,0},{64,80},{80,96},{96,112},{112,64},{1... | collective-permute-start | bytes 24584 | tf_op jit(solution)/shard_map/ppermute | solution.py:466
  146.8 2.1 %collective-permute-start.16 = (f32[16,128]{1,0:T(8,128)S(1)}, f32[16,128]{1,0:T(8,128)S(1)}, u32[]{:S(2)}, u32[]{:S(2)}) collective-permute-start(f32[16,128]{1,0:T(8,128)S(1)} %add.65), channel_id=1, source_target_pairs={{0,32},{16,48},{32,0},{48,16},{64,96},{80,112},{96,64},{112,80},{1... | collective-permute-start | bytes 24584 | tf_op jit(solution)/shard_map/ppermute | solution.py:466
  149.6 2.4 %collective-permute-done.16 = f32[16,128]{1,0:T(8,128)S(1)} collective-permute-done((f32[16,128]{1,0:T(8,128)S(1)}, f32[16,128]{1,0:T(8,128)S(1)}, u32[]{:S(2)}, u32[]{:S(2)}) %collective-permute-start.16) | collective-permute-done | bytes 8224 | tf_op jit(solution)/shard_map/ppermute | solution.py:466
  152.6 2.0 %collective-permute-start.18 = (f32[16,128]{1,0:T(8,128)S(1)}, f32[16,128]{1,0:T(8,128)S(1)}, u32[]{:S(2)}, u32[]{:S(2)}) collective-permute-start(f32[16,128]{1,0:T(8,128)S(1)} %add_add_fusion.1), channel_id=1, source_target_pairs={{0,64},{16,80},{32,96},{48,112},{64,128},{80,144},{96,160},{112,17... | collective-permute-start | bytes 24584 | tf_op jit(solution)/shard_map/ppermute | solution.py:466
  154.6 2.1 %collective-permute-start.19 = (f32[16,128]{1,0:T(8,128)S(1)}, f32[16,128]{1,0:T(8,128)S(1)}, u32[]{:S(2)}, u32[]{:S(2)}) collective-permute-start(f32[16,128]{1,0:T(8,128)S(1)} %add_add_fusion.1), channel_id=1, source_target_pairs={{0,128},{16,144},{32,160},{48,176},{64,192},{80,208},{96,224},{112... | collective-permute-start | bytes 24584 | tf_op jit(solution)/shard_map/ppermute | solution.py:466
  156.9 2.8 %collective-permute-done.19 = f32[16,128]{1,0:T(8,128)S(1)} collective-permute-done((f32[16,128]{1,0:T(8,128)S(1)}, f32[16,128]{1,0:T(8,128)S(1)}, u32[]{:S(2)}, u32[]{:S(2)}) %collective-permute-start.19) | collective-permute-done | bytes 8224 | tf_op jit(solution)/shard_map/ppermute | solution.py:466
  159.7 1.8 %collective-permute-done.20 = f32[16,128]{1,0:T(8,128)S(1)} collective-permute-done((f32[16,128]{1,0:T(8,128)S(1)}, f32[16,128]{1,0:T(8,128)S(1)}, u32[]{:S(2)}, u32[]{:S(2)}) %collective-permute-start.20) | collective-permute-done | bytes 8224 | tf_op jit(solution)/shard_map/ppermute | solution.py:466
  161.6 1.2 collective-permute-start.21
  162.8 3.6 %collective-permute-start.22 = (f32[16,128]{1,0:T(8,128)S(1)}, f32[16,128]{1,0:T(8,128)S(1)}, u32[]{:S(2)}, u32[]{:S(2)}) collective-permute-start(f32[16,128]{1,0:T(8,128)S(1)} %add_add_fusion.refs_0_), channel_id=1, source_target_pairs={{0,4},{1,5},{2,6},{3,7},{4,8},{5,9},{6,10},{7,11},{8,12},{9,13},{1... | collective-permute-start | bytes 24584 | tf_op jit(solution)/shard_map/ppermute | solution.py:467
  166.9 1.6 collective-permute-done.22.refs_2_
  168.6 4.5 %collective-permute-done.23.refs_3_ = f32[16,128]{1,0:T(8,128)S(1)} collective-permute-done((f32[16,128]{1,0:T(8,128)S(1)}, f32[16,128]{1,0:T(8,128)S(1)}, u32[]{:S(2)}, u32[]{:S(2)}) %collective-permute-start.23) | collective-permute-done | bytes 8224 | tf_op jit(solution)/shard_map/ppermute | solution.py:467
  173.0 2.9 %update.1 = (f32[64,4096]{1,0:T(8,128)}, f32[64,4096]{1,0:T(8,128)}) custom-call(s32[7]{0:T(128)S(1)} %copy-done.10, f32[64,4096]{1,0:T(8,128)S(1)} %copy-done.1, f32[8,64,512]{2,1,0:T(8,128)} %all-to-all-done.1.residual_ref, f32[8,64,512]{2,1,0:T(8,128)S(1)} %all-to-all-done.2.image_ref, f32[16,128]{1,0:T(8,128)S(1)} %add_add_fusion.refs_0_, ...), custom_call_target="tpu_custom_call" | custom-call | tf_op jit(solution)/shard_map/update/pallas_call | solution.py:325
  (62 shorter events, 10.4 us)
Async XLA Ops:
  0.6 1.0 copy-start
  1.6 15.1 %collective-permute-start = (f32[1,16,1024]{2,1,0:T(8,128)S(1)}, f32[1,16,1024]{2,1,0:T(8,128)S(1)}, u32[]{:S(2)}, u32[]{:S(2)}) collective-permute-start(f32[1,16,1024]{2,1,0:T(8,128)S(1)} %dynamic-slice_bitcast_fusion.refs_0_), channel_id=1, source_target_pairs={{0,8},{1,9},{2,10},{3,11},{4,12},{5,13},{6,14},{7,15},{8,0},{9,1},... | collective-permute-start | bytes 196616 | tf_op jit(solution)/shard_map/ppermute | solution.py:435
  8.8 12.8 %collective-permute-start.7 = (f32[64,256]{1,0:T(8,128)S(1)}, f32[64,256]{1,0:T(8,128)S(1)}, u32[]{:S(2)}, u32[]{:S(2)}) collective-permute-start(f32[64,256]{1,0:T(8,128)S(1)} %get-tuple-element.13), channel_id=1, source_target_pairs={{0,16},{16,32},{32,48},{48,64},{64,80},{80,96},{96,112},{112,128},... | collective-permute-start | bytes 196616 | tf_op jit(solution)/shard_map/ppermute | solution.py:430
  12.3 9.3 %collective-permute-start.8 = (f32[64,256]{1,0:T(8,128)S(1)}, f32[64,256]{1,0:T(8,128)S(1)}, u32[]{:S(2)}, u32[]{:S(2)}) collective-permute-start(f32[64,256]{1,0:T(8,128)S(1)} %get-tuple-element.12), channel_id=1, source_target_pairs={{16,0},{32,16},{48,32},{64,48},{80,64},{96,80},{112,96},{128,112},... | collective-permute-start | bytes 196616 | tf_op jit(solution)/shard_map/ppermute | solution.py:431
  16.8 12.7 %collective-permute-start.1 = (f32[2,16,1024]{2,1,0:T(8,128)S(1)}, f32[2,16,1024]{2,1,0:T(8,128)S(1)}, u32[]{:S(2)}, u32[]{:S(2)}) collective-permute-start(f32[2,16,1024]{2,1,0:T(8,128)S(1)} %joined.2.refs_0_), channel_id=1, source_target_pairs={{0,14},{1,15},{2,0},{3,1},{4,2},{5,3},{6,4},{7,5},{8,6},{9,7},{10,... | collective-permute-start | bytes 393224 | tf_op jit(solution)/shard_map/ppermute | solution.py:436
  17.8 11.7 %collective-permute-start.2 = (f32[2,16,1024]{2,1,0:T(8,128)S(1)}, f32[2,16,1024]{2,1,0:T(8,128)S(1)}, u32[]{:S(2)}, u32[]{:S(2)}) collective-permute-start(f32[2,16,1024]{2,1,0:T(8,128)S(1)} %joined.2.refs_0_), channel_id=1, source_target_pairs={{0,2},{1,3},{2,4},{3,5},{4,6},{5,7},{6,8},{7,9},{8,10},{9,11},{10,... | collective-permute-start | bytes 393224 | tf_op jit(solution)/shard_map/ppermute | solution.py:436
  18.9 10.7 %collective-permute-start.3 = (f32[2,16,1024]{2,1,0:T(8,128)S(1)}, f32[2,16,1024]{2,1,0:T(8,128)S(1)}, u32[]{:S(2)}, u32[]{:S(2)}) collective-permute-start(f32[2,16,1024]{2,1,0:T(8,128)S(1)} %joined.2.refs_0_), channel_id=1, source_target_pairs={{0,4},{1,5},{2,6},{3,7},{4,8},{5,9},{6,10},{7,11},{8,12},{9,13},{1... | collective-permute-start | bytes 393224 | tf_op jit(solution)/shard_map/ppermute | solution.py:436
  21.6 0.6 copy-start.12
  21.6 0.6 copy-start.13
  30.8 53.8 %all-to-all-start = ((f32[8,128,512]{2,1,0:T(8,128)}), f32[8,128,512]{2,1,0:T(8,128)S(1)}, u32[]{:S(2)}, u32[]{:S(2)}) async-start(f32[8,128,512]{2,1,0:T(8,128)} %ordered.2), calls=%async_computation | async-start | bytes 4194304 | tf_op jit(solution)/shard_map/all_to_all | solution.py:406
  36.0 14.9 %collective-permute-start.4 = (f32[8,16,1024]{2,1,0:T(8,128)S(1)}, f32[8,16,1024]{2,1,0:T(8,128)S(1)}, u32[]{:S(2)}, u32[]{:S(2)}) collective-permute-start(f32[8,16,1024]{2,1,0:T(8,128)S(1)} %joined.3.refs_0_), channel_id=1, source_target_pairs={{0,48},{16,0},{32,16},{48,32},{64,112},{80,64},{96,80},{112,96},{1... | collective-permute-start | bytes 1572872 | tf_op jit(solution)/shard_map/ppermute | solution.py:439
  37.0 16.5 %collective-permute-start.5 = (f32[8,16,1024]{2,1,0:T(8,128)S(1)}, f32[8,16,1024]{2,1,0:T(8,128)}, u32[]{:S(2)}, u32[]{:S(2)}) collective-permute-start(f32[8,16,1024]{2,1,0:T(8,128)S(1)} %joined.3.refs_0_), channel_id=1, source_target_pairs={{0,32},{16,48},{32,0},{48,16},{64,96},{80,112},{96,64},{112,80},{1... | collective-permute-start | bytes 1572872 | tf_op jit(solution)/shard_map/ppermute | solution.py:439
  37.6 23.9 %collective-permute-start.6 = (f32[8,16,1024]{2,1,0:T(8,128)S(1)}, f32[8,16,1024]{2,1,0:T(8,128)}, u32[]{:S(2)}, u32[]{:S(2)}) collective-permute-start(f32[8,16,1024]{2,1,0:T(8,128)S(1)} %joined.3.refs_0_), channel_id=1, source_target_pairs={{0,16},{16,32},{32,48},{48,0},{64,80},{80,96},{96,112},{112,64},{1... | collective-permute-start | bytes 1572872 | tf_op jit(solution)/shard_map/ppermute | solution.py:439
  39.2 22.4 %copy-start.10 = (s32[7]{0:T(128)S(1)}, s32[7]{0:T(128)}, u32[]{:S(2)}) copy-start(s32[7]{0:T(128)} %stack.31.at_ref) | copy-start | bytes 88
  63.0 1.0 copy-start.5
  64.7 1.0 copy-start.2
  84.6 2.8 %copy-start.3 = (bf16[8,64,1024]{2,1,0:T(8,128)(2,1)S(1)}, bf16[8,64,1024]{2,1,0:T(8,128)(2,1)}, u32[]{:S(2)}) copy-start(bf16[8,64,1024]{2,1,0:T(8,128)(2,1)} %copy-done.2) | copy-start | bytes 3145732
  84.6 2.8 %copy-start.6 = (bf16[8,64,1024]{2,1,0:T(8,128)(2,1)S(1)}, bf16[8,64,1024]{2,1,0:T(8,128)(2,1)}, u32[]{:S(2)}) copy-start(bf16[8,64,1024]{2,1,0:T(8,128)(2,1)} %copy-done.5) | copy-start | bytes 3145732
  84.7 2.7 %collective-permute-start.9 = (f32[8,64,512]{2,1,0:T(8,128)S(1)}, f32[8,64,512]{2,1,0:T(8,128)S(1)}, u32[]{:S(2)}, u32[]{:S(2)}) collective-permute-start(f32[8,64,512]{2,1,0:T(8,128)S(1)} %first_rows.1), channel_id=1, source_target_pairs={{0,1},{1,0},{2,3},{3,2},{4,5},{5,4},{6,7},{7,6},{8,9},{9,8},{10,11... | collective-permute-start | bytes 3145736 | tf_op jit(solution)/shard_map/ppermute | solution.py:444
  91.2 16.7 %collective-permute-start.10 = (f32[8,64,256]{2,1,0:T(8,128)}, f32[8,64,256]{2,1,0:T(8,128)}, u32[]{:S(2)}, u32[]{:S(2)}) collective-permute-start(f32[8,64,256]{2,1,0:T(8,128)} %get-tuple-element.11), channel_id=1, source_target_pairs={{0,2},{1,3},{2,4},{3,5},{4,6},{5,7},{6,8},{7,9},{8,10},{9,11},{10,... | collective-permute-start | bytes 1572872 | tf_op jit(solution)/shard_map/ppermute | solution.py:453
  93.6 17.0 %copy-start.11 = (s32[32,4]{0,1:T(4,128)S(1)}, s32[32,4]{0,1:T(4,128)}, u32[]{:S(2)}) copy-start(s32[32,4]{0,1:T(4,128)} %param.9) | copy-start | bytes 1540
  93.6 17.0 %collective-permute-start.11 = (f32[8,64,256]{2,1,0:T(8,128)}, f32[8,64,256]{2,1,0:T(8,128)}, u32[]{:S(2)}, u32[]{:S(2)}) collective-permute-start(f32[8,64,256]{2,1,0:T(8,128)} %get-tuple-element.10), channel_id=1, source_target_pairs={{2,0},{3,1},{4,2},{5,3},{6,4},{7,5},{8,6},{9,7},{10,8},{11,9},{12,... | collective-permute-start | bytes 1572872 | tf_op jit(solution)/shard_map/ppermute | solution.py:454
  98.1 36.8 %all-to-all-start.1 = ((f32[8,64,512]{2,1,0:T(8,128)}), f32[8,64,512]{2,1,0:T(8,128)}, u32[]{:S(2)}, u32[]{:S(2)}) async-start(f32[8,64,512]{2,1,0:T(8,128)} %copied.1.own_ref), calls=%async_computation.1 | async-start | bytes 2097152 | tf_op jit(solution)/shard_map/all_to_all | solution.py:406
  105.8 13.6 %copy-start.4 = (bf16[8,64,1024]{2,1,0:T(8,128)(2,1)S(1)}, bf16[8,64,1024]{2,1,0:T(8,128)(2,1)}, u32[]{:S(2)}) copy-start(bf16[8,64,1024]{2,1,0:T(8,128)(2,1)} %copy-done.2) | copy-start | bytes 3145732
  105.8 13.6 %copy-start.7 = (bf16[8,64,1024]{2,1,0:T(8,128)(2,1)S(1)}, bf16[8,64,1024]{2,1,0:T(8,128)(2,1)}, u32[]{:S(2)}) copy-start(bf16[8,64,1024]{2,1,0:T(8,128)(2,1)} %copy-done.5) | copy-start | bytes 3145732
  110.6 1.2 copy-start.9
  116.3 3.1 %collective-permute-start.12 = (f32[8,64,512]{2,1,0:T(8,128)}, f32[8,64,512]{2,1,0:T(8,128)}, u32[]{:S(2)}, u32[]{:S(2)}) collective-permute-start(f32[8,64,512]{2,1,0:T(8,128)} %space_mixed.1.own_ref), channel_id=1, source_target_pairs={{0,1},{1,0},{2,3},{3,2},{4,5},{5,4},{6,7},{7,6},{8,9},{9,8},{10,11... | collective-permute-start | bytes 3145736 | tf_op jit(solution)/shard_map/ppermute | solution.py:458
  123.2 1.0 copy-start.8
  124.1 1.2 collective-permute-start.13
  125.3 8.2 %collective-permute-start.14 = (f32[16,128]{1,0:T(8,128)S(1)}, f32[16,128]{1,0:T(8,128)S(1)}, u32[]{:S(2)}, u32[]{:S(2)}) collective-permute-start(f32[16,128]{1,0:T(8,128)S(1)} %add.64), channel_id=1, source_target_pairs={{0,8},{1,9},{2,10},{3,11},{4,12},{5,13},{6,14},{7,15},{8,0},{9,1},... | collective-permute-start | bytes 24584 | tf_op jit(solution)/shard_map/ppermute | solution.py:462
  133.5 0.6 copy-start.14
  134.1 38.9 %copy-start.1 = (f32[64,4096]{1,0:T(8,128)S(1)}, f32[64,4096]{1,0:T(8,128)}, u32[]{:S(2)}) copy-start(f32[64,4096]{1,0:T(8,128)} %start_ref.1) | copy-start | bytes 3145732
  134.9 6.2 %copy-start.15 = (f32[16,128]{1,0:T(8,128)S(1)}, f32[16,128]{1,0:T(8,128)}, u32[]{:S(2)}) copy-start(f32[16,128]{1,0:T(8,128)} %copy-done.14) | copy-start | bytes 24580
  134.9 38.1 %all-to-all-start.2 = ((f32[8,64,512]{2,1,0:T(8,128)}), f32[8,64,512]{2,1,0:T(8,128)S(1)}, u32[]{:S(2)}, u32[]{:S(2)}) async-start(f32[8,64,512]{2,1,0:T(8,128)} %ordered.3), calls=%async_computation.2 | async-start | bytes 2097152 | tf_op jit(solution)/shard_map/all_to_all | solution.py:406
  141.1 8.5 %collective-permute-start.15 = (f32[16,128]{1,0:T(8,128)S(1)}, f32[16,128]{1,0:T(8,128)S(1)}, u32[]{:S(2)}, u32[]{:S(2)}) collective-permute-start(f32[16,128]{1,0:T(8,128)S(1)} %add.65), channel_id=1, source_target_pairs={{0,16},{16,32},{32,48},{48,0},{64,80},{80,96},{96,112},{112,64},{1... | collective-permute-start | bytes 24584 | tf_op jit(solution)/shard_map/ppermute | solution.py:466
  146.8 5.2 %collective-permute-start.16 = (f32[16,128]{1,0:T(8,128)S(1)}, f32[16,128]{1,0:T(8,128)S(1)}, u32[]{:S(2)}, u32[]{:S(2)}) collective-permute-start(f32[16,128]{1,0:T(8,128)S(1)} %add.65), channel_id=1, source_target_pairs={{0,32},{16,48},{32,0},{48,16},{64,96},{80,112},{96,64},{112,80},{1... | collective-permute-start | bytes 24584 | tf_op jit(solution)/shard_map/ppermute | solution.py:466
  148.9 3.7 %collective-permute-start.17 = (f32[16,128]{1,0:T(8,128)S(1)}, f32[16,128]{1,0:T(8,128)S(1)}, u32[]{:S(2)}, u32[]{:S(2)}) collective-permute-start(f32[16,128]{1,0:T(8,128)S(1)} %add.65), channel_id=1, source_target_pairs={{0,48},{16,0},{32,16},{48,32},{64,112},{80,64},{96,80},{112,96},{1... | collective-permute-start | bytes 24584 | tf_op jit(solution)/shard_map/ppermute | solution.py:466
  152.6 4.3 %collective-permute-start.18 = (f32[16,128]{1,0:T(8,128)S(1)}, f32[16,128]{1,0:T(8,128)S(1)}, u32[]{:S(2)}, u32[]{:S(2)}) collective-permute-start(f32[16,128]{1,0:T(8,128)S(1)} %add_add_fusion.1), channel_id=1, source_target_pairs={{0,64},{16,80},{32,96},{48,112},{64,128},{80,144},{96,160},{112,17... | collective-permute-start | bytes 24584 | tf_op jit(solution)/shard_map/ppermute | solution.py:466
  154.6 5.2 %collective-permute-start.19 = (f32[16,128]{1,0:T(8,128)S(1)}, f32[16,128]{1,0:T(8,128)S(1)}, u32[]{:S(2)}, u32[]{:S(2)}) collective-permute-start(f32[16,128]{1,0:T(8,128)S(1)} %add_add_fusion.1), channel_id=1, source_target_pairs={{0,128},{16,144},{32,160},{48,176},{64,192},{80,208},{96,224},{112... | collective-permute-start | bytes 24584 | tf_op jit(solution)/shard_map/ppermute | solution.py:466
  156.7 4.9 %collective-permute-start.20 = (f32[16,128]{1,0:T(8,128)S(1)}, f32[16,128]{1,0:T(8,128)S(1)}, u32[]{:S(2)}, u32[]{:S(2)}) collective-permute-start(f32[16,128]{1,0:T(8,128)S(1)} %add_add_fusion.1), channel_id=1, source_target_pairs={{0,192},{16,208},{32,224},{48,240},{64,0},{80,16},{96,32},{112,48}... | collective-permute-start | bytes 24584 | tf_op jit(solution)/shard_map/ppermute | solution.py:466
  161.6 5.4 %collective-permute-start.21 = (f32[16,128]{1,0:T(8,128)S(1)}, f32[16,128]{1,0:T(8,128)S(1)}, u32[]{:S(2)}, u32[]{:S(2)}) collective-permute-start(f32[16,128]{1,0:T(8,128)S(1)} %add_add_fusion.refs_0_), channel_id=1, source_target_pairs={{0,2},{1,3},{2,4},{3,5},{4,6},{5,7},{6,8},{7,9},{8,10},{9,11},{10,... | collective-permute-start | bytes 24584 | tf_op jit(solution)/shard_map/ppermute | solution.py:467
  162.8 5.8 %collective-permute-start.22 = (f32[16,128]{1,0:T(8,128)S(1)}, f32[16,128]{1,0:T(8,128)S(1)}, u32[]{:S(2)}, u32[]{:S(2)}) collective-permute-start(f32[16,128]{1,0:T(8,128)S(1)} %add_add_fusion.refs_0_), channel_id=1, source_target_pairs={{0,4},{1,5},{2,6},{3,7},{4,8},{5,9},{6,10},{7,11},{8,12},{9,13},{1... | collective-permute-start | bytes 24584 | tf_op jit(solution)/shard_map/ppermute | solution.py:467
  166.4 6.7 %collective-permute-start.23 = (f32[16,128]{1,0:T(8,128)S(1)}, f32[16,128]{1,0:T(8,128)S(1)}, u32[]{:S(2)}, u32[]{:S(2)}) collective-permute-start(f32[16,128]{1,0:T(8,128)S(1)} %add_add_fusion.refs_0_), channel_id=1, source_target_pairs={{0,6},{1,7},{2,8},{3,9},{4,10},{5,11},{6,12},{7,13},{8,14},{9,15},... | collective-permute-start | bytes 24584 | tf_op jit(solution)/shard_map/ppermute | solution.py:467

commit v5 on v4

--- a/solution.py
+++ b/solution.py
@@ -458,10 +458,10 @@
     other = lax.ppermute(mixed, "tm", SWAP)
     noise_here = lax.dynamic_slice(noise, (group * width,), (width,))[None, :]
     image, sums = image_of(at, khi, klo, mixed, other, residual, noise_here)
-    sums = sums + lax.ppermute(sums, "tm", SWAP)
     far = lax.ppermute(sums, "tm", along_z(CHIPS // 2))
     back_p = exchange(ordered(image, far))
     sums = sums + far
+    sums = sums + lax.ppermute(sums, "tm", SWAP)
     for axis in ("y", "x"):
         sums = sum([lax.ppermute(sums, "space", along_side(shift, axis)) for shift in range(1, SIDE)], sums)
     sums = [sums] + [lax.ppermute(sums, "tm", along_z(shift)) for shift in range(1, CHIPS // 2)]

time: 177 us -> 177 us (level)
  no operation moved by 1% of the time
where the time goes in v5:
time: 177 us; the launch traced here: 176 us
  waiting for transfers between devices  69.6 us (39%)
  starting transfers between devices  65.2 us (37%)
  Pallas kernels  29.4 us (17%)
  local copies, waits for them, and re-layouts  10.3 us (6%)
    all_to_all x3, starting transfers between devices, exchange(): lax.all_to_all(blocks, 'tm', 0, 0, axis_index_groups=SAME_CORE, tiled=True)  19 us
    all_to_all x3, waiting for transfers between devices, exchange(): lax.all_to_all(blocks, 'tm', 0, 0, axis_index_groups=SAME_CORE, tiled=True)  19 us
    ppermute x3, waiting for transfers between devices, local(): lax.ppermute(strip, 'space', along_side(-k, 'y'))  18.2 us
    ppermute x6, starting transfers between devices, local(): lax.ppermute(sums, 'space', along_side(shift, axis))  11.5 us
    ppermute x1, waiting for transfers between devices, local(): far = lax.ppermute(sums, 'tm', along_z(CHIPS // 2))  7.8 us
    ppermute x6, waiting for transfers between devices, local(): lax.ppermute(sums, 'space', along_side(shift, axis))  7.72 us
    pallas_call x1, Pallas kernels, space_wide(): pl.pallas_call(space_wide_kernel, in_specs=[SMEM] + [VMEM] * 3 + [HBM] *...  7.28 us
    unnamed x32, local copies, waits for them, and re-layouts  6.32 us
  transfers between devices with their start and end apart: 27, of which 16 were waited for; matrix products, arithmetic and copies ran while one was open for 2% of the time, Pallas kernels for 13%

profile of v5, /device:TPU:38, one launch (start us, length us, event | category | flops | bytes accessed | tf_op | source)
XLA Modules:
  0.0 176.0 jit_solution(9430536685299849669)
XLA Ops:
  1.6 6.3 %collective-permute-start = (f32[1,16,1024]{2,1,0:T(8,128)S(1)}, f32[1,16,1024]{2,1,0:T(8,128)S(1)}, u32[]{:S(2)}, u32[]{:S(2)}) collective-permute-start(f32[1,16,1024]{2,1,0:T(8,128)S(1)} %dynamic-slice_bitcast_fusion.refs_0_), channel_id=1, source_target_pairs={{0,8},{1,9},{2,10},{3,11},{4,12},{5,13},{6,14},{7,15},{8,0},{9,1},... | collective-permute-start | bytes 196616 | tf_op jit(solution)/shard_map/ppermute | solution.py:435
  8.8 3.5 %collective-permute-start.7 = (f32[64,256]{1,0:T(8,128)S(1)}, f32[64,256]{1,0:T(8,128)S(1)}, u32[]{:S(2)}, u32[]{:S(2)}) collective-permute-start(f32[64,256]{1,0:T(8,128)S(1)} %get-tuple-element.13), channel_id=1, source_target_pairs={{0,16},{16,32},{32,48},{48,64},{64,80},{80,96},{96,112},{112,128},... | collective-permute-start | bytes 196616 | tf_op jit(solution)/shard_map/ppermute | solution.py:430
  12.3 4.5 %collective-permute-start.8 = (f32[64,256]{1,0:T(8,128)S(1)}, f32[64,256]{1,0:T(8,128)S(1)}, u32[]{:S(2)}, u32[]{:S(2)}) collective-permute-start(f32[64,256]{1,0:T(8,128)S(1)} %get-tuple-element.12), channel_id=1, source_target_pairs={{16,0},{32,16},{48,32},{64,48},{80,64},{96,80},{112,96},{128,112},... | collective-permute-start | bytes 196616 | tf_op jit(solution)/shard_map/ppermute | solution.py:431
  16.8 1.1 collective-permute-start.1
  17.8 1.0 collective-permute-start.2
  18.9 2.7 %collective-permute-start.3 = (f32[2,16,1024]{2,1,0:T(8,128)S(1)}, f32[2,16,1024]{2,1,0:T(8,128)S(1)}, u32[]{:S(2)}, u32[]{:S(2)}) collective-permute-start(f32[2,16,1024]{2,1,0:T(8,128)S(1)} %joined.2.refs_0_), channel_id=1, source_target_pairs={{0,4},{1,5},{2,6},{3,7},{4,8},{5,9},{6,10},{7,11},{8,12},{9,13},{1... | collective-permute-start | bytes 393224 | tf_op jit(solution)/shard_map/ppermute | solution.py:436
  22.2 7.3 %space_wide.1.refs_0_ = f32[8,128,512]{2,1,0:T(8,128)} custom-call(s32[4,32]{1,0:T(4,128)} %bitcast.21, f32[64,256]{1,0:T(8,128)} %copy-done.12, f32[64,256]{1,0:T(8,128)} %copy-done.13, f32[1,4096]{1,0:T(1,128)} %bitcast.23, f32[64,4096]{1,0:T(8,128)} %start_ref.1, f32[32,4,128,128]{3,2,1,0:T(8,128)} %tiles_ref.3, f32[64,4096]{1,0:T(8,128)} %right_ref.1), custom_call_target="tpu_custom_call" | custom-call | flops 2000000000 | tf_op jit(solution)/shard_map/space_wide/pallas_call | solution.py:135
  30.8 5.1 %all-to-all-start = ((f32[8,128,512]{2,1,0:T(8,128)}), f32[8,128,512]{2,1,0:T(8,128)S(1)}, u32[]{:S(2)}, u32[]{:S(2)}) async-start(f32[8,128,512]{2,1,0:T(8,128)} %ordered.2), calls=%async_computation | async-start | bytes 4194304 | tf_op jit(solution)/shard_map/all_to_all | solution.py:406
  36.0 1.0 collective-permute-start.4
  37.6 1.0 collective-permute-start.6
  39.2 4.2 %weights_of.1.weights_ref = bf16[4,4,256,128]{3,2,1,0:T(8,128)(2,1)} custom-call(s32[7]{0:T(128)} %stack.31.at_ref, f32[32,4,128,128]{3,2,1,0:T(8,128)} %tiles_ref.3), custom_call_target="tpu_custom_call" | custom-call | tf_op jit(solution)/shard_map/weights_of/pallas_call | solution.py:64
  43.4 7.6 %collective-permute-done.4.refs_1_ = f32[8,16,1024]{2,1,0:T(8,128)S(1)} collective-permute-done((f32[8,16,1024]{2,1,0:T(8,128)S(1)}, f32[8,16,1024]{2,1,0:T(8,128)S(1)}, u32[]{:S(2)}, u32[]{:S(2)}) %collective-permute-start.4) | collective-permute-done | bytes 524320 | tf_op jit(solution)/shard_map/ppermute | solution.py:439
  50.9 2.5 %collective-permute-done.5.refs_2_ = f32[8,16,1024]{2,1,0:T(8,128)} collective-permute-done((f32[8,16,1024]{2,1,0:T(8,128)S(1)}, f32[8,16,1024]{2,1,0:T(8,128)}, u32[]{:S(2)}, u32[]{:S(2)}) %collective-permute-start.5) | collective-permute-done | bytes 524320 | tf_op jit(solution)/shard_map/ppermute | solution.py:439
  53.5 8.1 %collective-permute-done.6.refs_3_ = f32[8,16,1024]{2,1,0:T(8,128)} collective-permute-done((f32[8,16,1024]{2,1,0:T(8,128)S(1)}, f32[8,16,1024]{2,1,0:T(8,128)}, u32[]{:S(2)}, u32[]{:S(2)}) %collective-permute-start.6) | collective-permute-done | bytes 524320 | tf_op jit(solution)/shard_map/ppermute | solution.py:439
  61.6 1.5 time_rows.1
  63.0 1.0 copy-done.5
  64.7 1.0 copy-done.2
  65.7 18.9 %all-to-all-done.value_ref.got_ref = f32[8,128,512]{2,1,0:T(8,128)S(1)} async-done(((f32[8,128,512]{2,1,0:T(8,128)}), f32[8,128,512]{2,1,0:T(8,128)S(1)}, u32[]{:S(2)}, u32[]{:S(2)}) %all-to-all-start) | async-done | bytes 2097184 | tf_op jit(solution)/shard_map/all_to_all | solution.py:406
  84.8 2.6 %collective-permute-done.9.other_ref = f32[8,64,512]{2,1,0:T(8,128)S(1)} collective-permute-done((f32[8,64,512]{2,1,0:T(8,128)S(1)}, f32[8,64,512]{2,1,0:T(8,128)S(1)}, u32[]{:S(2)}, u32[]{:S(2)}) %collective-permute-start.9) | collective-permute-done | bytes 1048608 | tf_op jit(solution)/shard_map/ppermute | solution.py:444
  87.4 2.7 %residual_of.1.value_ref.r_ref = f32[8,64,512]{2,1,0:T(8,128)S(1)} custom-call(s32[7]{0:T(128)S(1)} %copy-done.10, bf16[8,64,1024]{2,1,0:T(8,128)(2,1)S(1)} %copy-done.3, bf16[8,64,1024]{2,1,0:T(8,128)(2,1)S(1)} %copy-done.6, f32[8,128,512]{2,1,0:T(8,128)S(1)} %all-to-all-done.value_ref.got_ref, f32[8,64,512]{2,1,0:T(8,128)S(1)} %collective-permute-done.9.other_ref), custom_call_target="tpu_custom_call" | custom-call | tf_op jit(solution)/shard_map/residual_of/pallas_call | solution.py:261
  90.1 1.1 fusion.1
  91.2 2.4 %collective-permute-start.10 = (f32[8,64,256]{2,1,0:T(8,128)}, f32[8,64,256]{2,1,0:T(8,128)}, u32[]{:S(2)}, u32[]{:S(2)}) collective-permute-start(f32[8,64,256]{2,1,0:T(8,128)} %get-tuple-element.11), channel_id=1, source_target_pairs={{0,2},{1,3},{2,4},{3,5},{4,6},{5,7},{6,8},{7,9},{8,10},{9,11},{10,... | collective-permute-start | bytes 1572872 | tf_op jit(solution)/shard_map/ppermute | solution.py:453
  93.6 3.5 %collective-permute-start.11 = (f32[8,64,256]{2,1,0:T(8,128)}, f32[8,64,256]{2,1,0:T(8,128)}, u32[]{:S(2)}, u32[]{:S(2)}) collective-permute-start(f32[8,64,256]{2,1,0:T(8,128)} %get-tuple-element.10), channel_id=1, source_target_pairs={{2,0},{3,1},{4,2},{5,3},{6,4},{7,5},{8,6},{9,7},{10,8},{11,9},{12,... | collective-permute-start | bytes 1572872 | tf_op jit(solution)/shard_map/ppermute | solution.py:454
  97.1 1.0 copied.1.own_ref
  98.1 7.8 %all-to-all-start.1 = ((f32[8,64,512]{2,1,0:T(8,128)}), f32[8,64,512]{2,1,0:T(8,128)}, u32[]{:S(2)}, u32[]{:S(2)}) async-start(f32[8,64,512]{2,1,0:T(8,128)} %copied.1.own_ref), calls=%async_computation.1 | async-start | bytes 2097152 | tf_op jit(solution)/shard_map/all_to_all | solution.py:406
  105.8 2.0 %collective-permute-done.10.left_ref = f32[8,64,256]{2,1,0:T(8,128)} collective-permute-done((f32[8,64,256]{2,1,0:T(8,128)}, f32[8,64,256]{2,1,0:T(8,128)}, u32[]{:S(2)}, u32[]{:S(2)}) %collective-permute-start.10) | collective-permute-done | bytes 524320 | tf_op jit(solution)/shard_map/ppermute | solution.py:453
  107.9 2.7 %collective-permute-done.11.right_ref = f32[8,64,256]{2,1,0:T(8,128)} collective-permute-done((f32[8,64,256]{2,1,0:T(8,128)}, f32[8,64,256]{2,1,0:T(8,128)}, u32[]{:S(2)}, u32[]{:S(2)}) %collective-permute-start.11) | collective-permute-done | bytes 524320 | tf_op jit(solution)/shard_map/ppermute | solution.py:454
  110.6 1.2 copy-done.9
  111.9 4.5 %space_mixed.1.own_ref = f32[8,64,512]{2,1,0:T(8,128)} custom-call(s32[7]{0:T(128)S(1)} %copy-done.10, s32[4,32]{1,0:T(4,128)S(1)} %bitcast.22, f32[8,64,256]{2,1,0:T(8,128)} %collective-permute-done.10.left_ref, f32[8,64,512]{2,1,0:T(8,128)} %copied.1.own_ref, f32[8,64,256]{2,1,0:T(8,128)} %collective-permute-done.11.right_ref, ...), custom_call_target="tpu_custom_call" | custom-call | flops 4000000000 | tf_op jit(solution)/shard_map/space_mixed/pallas_call | solution.py:190
  117.2 2.2 %collective-permute-done.12.other_ref = f32[8,64,512]{2,1,0:T(8,128)} collective-permute-done((f32[8,64,512]{2,1,0:T(8,128)}, f32[8,64,512]{2,1,0:T(8,128)}, u32[]{:S(2)}, u32[]{:S(2)}) %collective-permute-start.12) | collective-permute-done | bytes 1048608 | tf_op jit(solution)/shard_map/ppermute | solution.py:458
  119.4 3.7 %image_of.1 = (f32[8,64,512]{2,1,0:T(8,128)S(1)}, f32[16,128]{1,0:T(8,128)S(1)}) custom-call(s32[7]{0:T(128)S(1)} %copy-done.10, bf16[8,64,1024]{2,1,0:T(8,128)(2,1)S(1)} %copy-done.4, bf16[8,64,1024]{2,1,0:T(8,128)(2,1)S(1)} %copy-done.7, f32[8,64,512]{2,1,0:T(8,128)} %space_mixed.1.own_ref, f32[8,64,512]{2,1,0:T(8,128)} %collective-permute-done.12.other_ref, ...), custom_call_target="tpu_custom_call" | custom-call | tf_op jit(solution)/shard_map/image_of/pallas_call | solution.py:296
  123.2 1.0 copy-done.8
  124.1 1.6 collective-permute-start.13
  125.7 7.8 %collective-permute-done.13.refs_1_ = f32[16,128]{1,0:T(8,128)S(1)} collective-permute-done((f32[16,128]{1,0:T(8,128)S(1)}, f32[16,128]{1,0:T(8,128)S(1)}, u32[]{:S(2)}, u32[]{:S(2)}) %collective-permute-start.13) | collective-permute-done | bytes 8224 | tf_op jit(solution)/shard_map/ppermute | solution.py:461
  134.9 6.1 %all-to-all-start.2 = ((f32[8,64,512]{2,1,0:T(8,128)}), f32[8,64,512]{2,1,0:T(8,128)S(1)}, u32[]{:S(2)}, u32[]{:S(2)}) async-start(f32[8,64,512]{2,1,0:T(8,128)} %ordered.3), calls=%async_computation.2 | async-start | bytes 2097152 | tf_op jit(solution)/shard_map/all_to_all | solution.py:406
  141.2 1.2 collective-permute-done.14
  142.3 4.5 %collective-permute-start.15 = (f32[16,128]{1,0:T(8,128)S(1)}, f32[16,128]{1,0:T(8,128)S(1)}, u32[]{:S(2)}, u32[]{:S(2)}) collective-permute-start(f32[16,128]{1,0:T(8,128)S(1)} %add.65), channel_id=1, source_target_pairs={{0,16},{16,32},{32,48},{48,0},{64,80},{80,96},{96,112},{112,64},{1... | collective-permute-start | bytes 24584 | tf_op jit(solution)/shard_map/ppermute | solution.py:466
  146.8 2.1 %collective-permute-start.16 = (f32[16,128]{1,0:T(8,128)S(1)}, f32[16,128]{1,0:T(8,128)S(1)}, u32[]{:S(2)}, u32[]{:S(2)}) collective-permute-start(f32[16,128]{1,0:T(8,128)S(1)} %add.65), channel_id=1, source_target_pairs={{0,32},{16,48},{32,0},{48,16},{64,96},{80,112},{96,64},{112,80},{1... | collective-permute-start | bytes 24584 | tf_op jit(solution)/shard_map/ppermute | solution.py:466
  149.5 2.5 %collective-permute-done.16 = f32[16,128]{1,0:T(8,128)S(1)} collective-permute-done((f32[16,128]{1,0:T(8,128)S(1)}, f32[16,128]{1,0:T(8,128)S(1)}, u32[]{:S(2)}, u32[]{:S(2)}) %collective-permute-start.16) | collective-permute-done | bytes 8224 | tf_op jit(solution)/shard_map/ppermute | solution.py:466
  152.6 2.0 %collective-permute-start.18 = (f32[16,128]{1,0:T(8,128)S(1)}, f32[16,128]{1,0:T(8,128)S(1)}, u32[]{:S(2)}, u32[]{:S(2)}) collective-permute-start(f32[16,128]{1,0:T(8,128)S(1)} %add_add_fusion.1), channel_id=1, source_target_pairs={{0,64},{16,80},{32,96},{48,112},{64,128},{80,144},{96,160},{112,17... | collective-permute-start | bytes 24584 | tf_op jit(solution)/shard_map/ppermute | solution.py:466
  154.6 2.1 %collective-permute-start.19 = (f32[16,128]{1,0:T(8,128)S(1)}, f32[16,128]{1,0:T(8,128)S(1)}, u32[]{:S(2)}, u32[]{:S(2)}) collective-permute-start(f32[16,128]{1,0:T(8,128)S(1)} %add_add_fusion.1), channel_id=1, source_target_pairs={{0,128},{16,144},{32,160},{48,176},{64,192},{80,208},{96,224},{112... | collective-permute-start | bytes 24584 | tf_op jit(solution)/shard_map/ppermute | solution.py:466
  156.9 2.8 %collective-permute-done.19 = f32[16,128]{1,0:T(8,128)S(1)} collective-permute-done((f32[16,128]{1,0:T(8,128)S(1)}, f32[16,128]{1,0:T(8,128)S(1)}, u32[]{:S(2)}, u32[]{:S(2)}) %collective-permute-start.19) | collective-permute-done | bytes 8224 | tf_op jit(solution)/shard_map/ppermute | solution.py:466
  159.7 1.8 %collective-permute-done.20 = f32[16,128]{1,0:T(8,128)S(1)} collective-permute-done((f32[16,128]{1,0:T(8,128)S(1)}, f32[16,128]{1,0:T(8,128)S(1)}, u32[]{:S(2)}, u32[]{:S(2)}) %collective-permute-start.20) | collective-permute-done | bytes 8224 | tf_op jit(solution)/shard_map/ppermute | solution.py:466
  161.6 1.2 collective-permute-start.21
  162.8 3.6 %collective-permute-start.22 = (f32[16,128]{1,0:T(8,128)S(1)}, f32[16,128]{1,0:T(8,128)S(1)}, u32[]{:S(2)}, u32[]{:S(2)}) collective-permute-start(f32[16,128]{1,0:T(8,128)S(1)} %add_add_fusion.refs_0_), channel_id=1, source_target_pairs={{0,4},{1,5},{2,6},{3,7},{4,8},{5,9},{6,10},{7,11},{8,12},{9,13},{1... | collective-permute-start | bytes 24584 | tf_op jit(solution)/shard_map/ppermute | solution.py:467
  166.9 1.7 collective-permute-done.22.refs_2_
  168.7 4.4 %collective-permute-done.23.refs_3_ = f32[16,128]{1,0:T(8,128)S(1)} collective-permute-done((f32[16,128]{1,0:T(8,128)S(1)}, f32[16,128]{1,0:T(8,128)S(1)}, u32[]{:S(2)}, u32[]{:S(2)}) %collective-permute-start.23) | collective-permute-done | bytes 8224 | tf_op jit(solution)/shard_map/ppermute | solution.py:467
  173.0 2.9 %update.1 = (f32[64,4096]{1,0:T(8,128)}, f32[64,4096]{1,0:T(8,128)}) custom-call(s32[7]{0:T(128)S(1)} %copy-done.10, f32[64,4096]{1,0:T(8,128)S(1)} %copy-done.1, f32[8,64,512]{2,1,0:T(8,128)} %all-to-all-done.1.residual_ref, f32[8,64,512]{2,1,0:T(8,128)S(1)} %all-to-all-done.2.image_ref, f32[16,128]{1,0:T(8,128)S(1)} %add_add_fusion.refs_0_, ...), custom_call_target="tpu_custom_call" | custom-call | tf_op jit(solution)/shard_map/update/pallas_call | solution.py:325
  (62 shorter events, 10.3 us)
Async XLA Ops:
  0.6 1.0 copy-start
  1.6 15.1 %collective-permute-start = (f32[1,16,1024]{2,1,0:T(8,128)S(1)}, f32[1,16,1024]{2,1,0:T(8,128)S(1)}, u32[]{:S(2)}, u32[]{:S(2)}) collective-permute-start(f32[1,16,1024]{2,1,0:T(8,128)S(1)} %dynamic-slice_bitcast_fusion.refs_0_), channel_id=1, source_target_pairs={{0,8},{1,9},{2,10},{3,11},{4,12},{5,13},{6,14},{7,15},{8,0},{9,1},... | collective-permute-start | bytes 196616 | tf_op jit(solution)/shard_map/ppermute | solution.py:435
  8.8 12.8 %collective-permute-start.7 = (f32[64,256]{1,0:T(8,128)S(1)}, f32[64,256]{1,0:T(8,128)S(1)}, u32[]{:S(2)}, u32[]{:S(2)}) collective-permute-start(f32[64,256]{1,0:T(8,128)S(1)} %get-tuple-element.13), channel_id=1, source_target_pairs={{0,16},{16,32},{32,48},{48,64},{64,80},{80,96},{96,112},{112,128},... | collective-permute-start | bytes 196616 | tf_op jit(solution)/shard_map/ppermute | solution.py:430
  12.3 9.3 %collective-permute-start.8 = (f32[64,256]{1,0:T(8,128)S(1)}, f32[64,256]{1,0:T(8,128)S(1)}, u32[]{:S(2)}, u32[]{:S(2)}) collective-permute-start(f32[64,256]{1,0:T(8,128)S(1)} %get-tuple-element.12), channel_id=1, source_target_pairs={{16,0},{32,16},{48,32},{64,48},{80,64},{96,80},{112,96},{128,112},... | collective-permute-start | bytes 196616 | tf_op jit(solution)/shard_map/ppermute | solution.py:431
  16.8 12.7 %collective-permute-start.1 = (f32[2,16,1024]{2,1,0:T(8,128)S(1)}, f32[2,16,1024]{2,1,0:T(8,128)S(1)}, u32[]{:S(2)}, u32[]{:S(2)}) collective-permute-start(f32[2,16,1024]{2,1,0:T(8,128)S(1)} %joined.2.refs_0_), channel_id=1, source_target_pairs={{0,14},{1,15},{2,0},{3,1},{4,2},{5,3},{6,4},{7,5},{8,6},{9,7},{10,... | collective-permute-start | bytes 393224 | tf_op jit(solution)/shard_map/ppermute | solution.py:436
  17.8 11.7 %collective-permute-start.2 = (f32[2,16,1024]{2,1,0:T(8,128)S(1)}, f32[2,16,1024]{2,1,0:T(8,128)S(1)}, u32[]{:S(2)}, u32[]{:S(2)}) collective-permute-start(f32[2,16,1024]{2,1,0:T(8,128)S(1)} %joined.2.refs_0_), channel_id=1, source_target_pairs={{0,2},{1,3},{2,4},{3,5},{4,6},{5,7},{6,8},{7,9},{8,10},{9,11},{10,... | collective-permute-start | bytes 393224 | tf_op jit(solution)/shard_map/ppermute | solution.py:436
  18.9 10.7 %collective-permute-start.3 = (f32[2,16,1024]{2,1,0:T(8,128)S(1)}, f32[2,16,1024]{2,1,0:T(8,128)S(1)}, u32[]{:S(2)}, u32[]{:S(2)}) collective-permute-start(f32[2,16,1024]{2,1,0:T(8,128)S(1)} %joined.2.refs_0_), channel_id=1, source_target_pairs={{0,4},{1,5},{2,6},{3,7},{4,8},{5,9},{6,10},{7,11},{8,12},{9,13},{1... | collective-permute-start | bytes 393224 | tf_op jit(solution)/shard_map/ppermute | solution.py:436
  21.6 0.6 copy-start.12
  21.6 0.6 copy-start.13
  30.8 53.8 %all-to-all-start = ((f32[8,128,512]{2,1,0:T(8,128)}), f32[8,128,512]{2,1,0:T(8,128)S(1)}, u32[]{:S(2)}, u32[]{:S(2)}) async-start(f32[8,128,512]{2,1,0:T(8,128)} %ordered.2), calls=%async_computation | async-start | bytes 4194304 | tf_op jit(solution)/shard_map/all_to_all | solution.py:406
  36.0 14.9 %collective-permute-start.4 = (f32[8,16,1024]{2,1,0:T(8,128)S(1)}, f32[8,16,1024]{2,1,0:T(8,128)S(1)}, u32[]{:S(2)}, u32[]{:S(2)}) collective-permute-start(f32[8,16,1024]{2,1,0:T(8,128)S(1)} %joined.3.refs_0_), channel_id=1, source_target_pairs={{0,48},{16,0},{32,16},{48,32},{64,112},{80,64},{96,80},{112,96},{1... | collective-permute-start | bytes 1572872 | tf_op jit(solution)/shard_map/ppermute | solution.py:439
  37.0 16.5 %collective-permute-start.5 = (f32[8,16,1024]{2,1,0:T(8,128)S(1)}, f32[8,16,1024]{2,1,0:T(8,128)}, u32[]{:S(2)}, u32[]{:S(2)}) collective-permute-start(f32[8,16,1024]{2,1,0:T(8,128)S(1)} %joined.3.refs_0_), channel_id=1, source_target_pairs={{0,32},{16,48},{32,0},{48,16},{64,96},{80,112},{96,64},{112,80},{1... | collective-permute-start | bytes 1572872 | tf_op jit(solution)/shard_map/ppermute | solution.py:439
  37.6 23.9 %collective-permute-start.6 = (f32[8,16,1024]{2,1,0:T(8,128)S(1)}, f32[8,16,1024]{2,1,0:T(8,128)}, u32[]{:S(2)}, u32[]{:S(2)}) collective-permute-start(f32[8,16,1024]{2,1,0:T(8,128)S(1)} %joined.3.refs_0_), channel_id=1, source_target_pairs={{0,16},{16,32},{32,48},{48,0},{64,80},{80,96},{96,112},{112,64},{1... | collective-permute-start | bytes 1572872 | tf_op jit(solution)/shard_map/ppermute | solution.py:439
  39.2 22.4 %copy-start.10 = (s32[7]{0:T(128)S(1)}, s32[7]{0:T(128)}, u32[]{:S(2)}) copy-start(s32[7]{0:T(128)} %stack.31.at_ref) | copy-start | bytes 88
  63.0 1.0 copy-start.5
  64.7 1.0 copy-start.2
  84.6 2.8 %copy-start.3 = (bf16[8,64,1024]{2,1,0:T(8,128)(2,1)S(1)}, bf16[8,64,1024]{2,1,0:T(8,128)(2,1)}, u32[]{:S(2)}) copy-start(bf16[8,64,1024]{2,1,0:T(8,128)(2,1)} %copy-done.2) | copy-start | bytes 3145732
  84.6 2.8 %copy-start.6 = (bf16[8,64,1024]{2,1,0:T(8,128)(2,1)S(1)}, bf16[8,64,1024]{2,1,0:T(8,128)(2,1)}, u32[]{:S(2)}) copy-start(bf16[8,64,1024]{2,1,0:T(8,128)(2,1)} %copy-done.5) | copy-start | bytes 3145732
  84.7 2.7 %collective-permute-start.9 = (f32[8,64,512]{2,1,0:T(8,128)S(1)}, f32[8,64,512]{2,1,0:T(8,128)S(1)}, u32[]{:S(2)}, u32[]{:S(2)}) collective-permute-start(f32[8,64,512]{2,1,0:T(8,128)S(1)} %first_rows.1), channel_id=1, source_target_pairs={{0,1},{1,0},{2,3},{3,2},{4,5},{5,4},{6,7},{7,6},{8,9},{9,8},{10,11... | collective-permute-start | bytes 3145736 | tf_op jit(solution)/shard_map/ppermute | solution.py:444
  91.2 16.7 %collective-permute-start.10 = (f32[8,64,256]{2,1,0:T(8,128)}, f32[8,64,256]{2,1,0:T(8,128)}, u32[]{:S(2)}, u32[]{:S(2)}) collective-permute-start(f32[8,64,256]{2,1,0:T(8,128)} %get-tuple-element.11), channel_id=1, source_target_pairs={{0,2},{1,3},{2,4},{3,5},{4,6},{5,7},{6,8},{7,9},{8,10},{9,11},{10,... | collective-permute-start | bytes 1572872 | tf_op jit(solution)/shard_map/ppermute | solution.py:453
  93.6 17.0 %copy-start.11 = (s32[32,4]{0,1:T(4,128)S(1)}, s32[32,4]{0,1:T(4,128)}, u32[]{:S(2)}) copy-start(s32[32,4]{0,1:T(4,128)} %param.9) | copy-start | bytes 1540
  93.6 17.0 %collective-permute-start.11 = (f32[8,64,256]{2,1,0:T(8,128)}, f32[8,64,256]{2,1,0:T(8,128)}, u32[]{:S(2)}, u32[]{:S(2)}) collective-permute-start(f32[8,64,256]{2,1,0:T(8,128)} %get-tuple-element.10), channel_id=1, source_target_pairs={{2,0},{3,1},{4,2},{5,3},{6,4},{7,5},{8,6},{9,7},{10,8},{11,9},{12,... | collective-permute-start | bytes 1572872 | tf_op jit(solution)/shard_map/ppermute | solution.py:454
  98.1 36.8 %all-to-all-start.1 = ((f32[8,64,512]{2,1,0:T(8,128)}), f32[8,64,512]{2,1,0:T(8,128)}, u32[]{:S(2)}, u32[]{:S(2)}) async-start(f32[8,64,512]{2,1,0:T(8,128)} %copied.1.own_ref), calls=%async_computation.1 | async-start | bytes 2097152 | tf_op jit(solution)/shard_map/all_to_all | solution.py:406
  105.8 13.6 %copy-start.4 = (bf16[8,64,1024]{2,1,0:T(8,128)(2,1)S(1)}, bf16[8,64,1024]{2,1,0:T(8,128)(2,1)}, u32[]{:S(2)}) copy-start(bf16[8,64,1024]{2,1,0:T(8,128)(2,1)} %copy-done.2) | copy-start | bytes 3145732
  105.8 13.6 %copy-start.7 = (bf16[8,64,1024]{2,1,0:T(8,128)(2,1)S(1)}, bf16[8,64,1024]{2,1,0:T(8,128)(2,1)}, u32[]{:S(2)}) copy-start(bf16[8,64,1024]{2,1,0:T(8,128)(2,1)} %copy-done.5) | copy-start | bytes 3145732
  110.6 1.2 copy-start.9
  116.3 3.1 %collective-permute-start.12 = (f32[8,64,512]{2,1,0:T(8,128)}, f32[8,64,512]{2,1,0:T(8,128)}, u32[]{:S(2)}, u32[]{:S(2)}) collective-permute-start(f32[8,64,512]{2,1,0:T(8,128)} %space_mixed.1.own_ref), channel_id=1, source_target_pairs={{0,1},{1,0},{2,3},{3,2},{4,5},{5,4},{6,7},{7,6},{8,9},{9,8},{10,11... | collective-permute-start | bytes 3145736 | tf_op jit(solution)/shard_map/ppermute | solution.py:458
  123.2 1.0 copy-start.8
  124.1 9.4 %collective-permute-start.13 = (f32[16,128]{1,0:T(8,128)S(1)}, f32[16,128]{1,0:T(8,128)S(1)}, u32[]{:S(2)}, u32[]{:S(2)}) collective-permute-start(f32[16,128]{1,0:T(8,128)S(1)} %get-tuple-element.9), channel_id=1, source_target_pairs={{0,8},{1,9},{2,10},{3,11},{4,12},{5,13},{6,14},{7,15},{8,0},{9,1},... | collective-permute-start | bytes 24584 | tf_op jit(solution)/shard_map/ppermute | solution.py:461
  133.5 0.6 copy-start.14
  134.1 38.9 %copy-start.1 = (f32[64,4096]{1,0:T(8,128)S(1)}, f32[64,4096]{1,0:T(8,128)}, u32[]{:S(2)}) copy-start(f32[64,4096]{1,0:T(8,128)} %start_ref.1) | copy-start | bytes 3145732
  134.9 6.2 %copy-start.15 = (f32[16,128]{1,0:T(8,128)S(1)}, f32[16,128]{1,0:T(8,128)}, u32[]{:S(2)}) copy-start(f32[16,128]{1,0:T(8,128)} %copy-done.14) | copy-start | bytes 24580
  134.9 38.1 %all-to-all-start.2 = ((f32[8,64,512]{2,1,0:T(8,128)}), f32[8,64,512]{2,1,0:T(8,128)S(1)}, u32[]{:S(2)}, u32[]{:S(2)}) async-start(f32[8,64,512]{2,1,0:T(8,128)} %ordered.3), calls=%async_computation.2 | async-start | bytes 2097152 | tf_op jit(solution)/shard_map/all_to_all | solution.py:406
  141.1 1.3 collective-permute-start.14
  142.3 7.2 %collective-permute-start.15 = (f32[16,128]{1,0:T(8,128)S(1)}, f32[16,128]{1,0:T(8,128)S(1)}, u32[]{:S(2)}, u32[]{:S(2)}) collective-permute-start(f32[16,128]{1,0:T(8,128)S(1)} %add.65), channel_id=1, source_target_pairs={{0,16},{16,32},{32,48},{48,0},{64,80},{80,96},{96,112},{112,64},{1... | collective-permute-start | bytes 24584 | tf_op jit(solution)/shard_map/ppermute | solution.py:466
  146.8 5.2 %collective-permute-start.16 = (f32[16,128]{1,0:T(8,128)S(1)}, f32[16,128]{1,0:T(8,128)S(1)}, u32[]{:S(2)}, u32[]{:S(2)}) collective-permute-start(f32[16,128]{1,0:T(8,128)S(1)} %add.65), channel_id=1, source_target_pairs={{0,32},{16,48},{32,0},{48,16},{64,96},{80,112},{96,64},{112,80},{1... | collective-permute-start | bytes 24584 | tf_op jit(solution)/shard_map/ppermute | solution.py:466
  149.0 3.7 %collective-permute-start.17 = (f32[16,128]{1,0:T(8,128)S(1)}, f32[16,128]{1,0:T(8,128)S(1)}, u32[]{:S(2)}, u32[]{:S(2)}) collective-permute-start(f32[16,128]{1,0:T(8,128)S(1)} %add.65), channel_id=1, source_target_pairs={{0,48},{16,0},{32,16},{48,32},{64,112},{80,64},{96,80},{112,96},{1... | collective-permute-start | bytes 24584 | tf_op jit(solution)/shard_map/ppermute | solution.py:466
  152.6 4.3 %collective-permute-start.18 = (f32[16,128]{1,0:T(8,128)S(1)}, f32[16,128]{1,0:T(8,128)S(1)}, u32[]{:S(2)}, u32[]{:S(2)}) collective-permute-start(f32[16,128]{1,0:T(8,128)S(1)} %add_add_fusion.1), channel_id=1, source_target_pairs={{0,64},{16,80},{32,96},{48,112},{64,128},{80,144},{96,160},{112,17... | collective-permute-start | bytes 24584 | tf_op jit(solution)/shard_map/ppermute | solution.py:466
  154.6 5.2 %collective-permute-start.19 = (f32[16,128]{1,0:T(8,128)S(1)}, f32[16,128]{1,0:T(8,128)S(1)}, u32[]{:S(2)}, u32[]{:S(2)}) collective-permute-start(f32[16,128]{1,0:T(8,128)S(1)} %add_add_fusion.1), channel_id=1, source_target_pairs={{0,128},{16,144},{32,160},{48,176},{64,192},{80,208},{96,224},{112... | collective-permute-start | bytes 24584 | tf_op jit(solution)/shard_map/ppermute | solution.py:466
  156.7 4.9 %collective-permute-start.20 = (f32[16,128]{1,0:T(8,128)S(1)}, f32[16,128]{1,0:T(8,128)S(1)}, u32[]{:S(2)}, u32[]{:S(2)}) collective-permute-start(f32[16,128]{1,0:T(8,128)S(1)} %add_add_fusion.1), channel_id=1, source_target_pairs={{0,192},{16,208},{32,224},{48,240},{64,0},{80,16},{96,32},{112,48}... | collective-permute-start | bytes 24584 | tf_op jit(solution)/shard_map/ppermute | solution.py:466
  161.6 5.4 %collective-permute-start.21 = (f32[16,128]{1,0:T(8,128)S(1)}, f32[16,128]{1,0:T(8,128)S(1)}, u32[]{:S(2)}, u32[]{:S(2)}) collective-permute-start(f32[16,128]{1,0:T(8,128)S(1)} %add_add_fusion.refs_0_), channel_id=1, source_target_pairs={{0,2},{1,3},{2,4},{3,5},{4,6},{5,7},{6,8},{7,9},{8,10},{9,11},{10,... | collective-permute-start | bytes 24584 | tf_op jit(solution)/shard_map/ppermute | solution.py:467
  162.8 5.9 %collective-permute-start.22 = (f32[16,128]{1,0:T(8,128)S(1)}, f32[16,128]{1,0:T(8,128)S(1)}, u32[]{:S(2)}, u32[]{:S(2)}) collective-permute-start(f32[16,128]{1,0:T(8,128)S(1)} %add_add_fusion.refs_0_), channel_id=1, source_target_pairs={{0,4},{1,5},{2,6},{3,7},{4,8},{5,9},{6,10},{7,11},{8,12},{9,13},{1... | collective-permute-start | bytes 24584 | tf_op jit(solution)/shard_map/ppermute | solution.py:467
  166.4 6.7 %collective-permute-start.23 = (f32[16,128]{1,0:T(8,128)S(1)}, f32[16,128]{1,0:T(8,128)S(1)}, u32[]{:S(2)}, u32[]{:S(2)}) collective-permute-start(f32[16,128]{1,0:T(8,128)S(1)} %add_add_fusion.refs_0_), channel_id=1, source_target_pairs={{0,6},{1,7},{2,8},{3,9},{4,10},{5,11},{6,12},{7,13},{8,14},{9,15},... | collective-permute-start | bytes 24584 | tf_op jit(solution)/shard_map/ppermute | solution.py:467
